TPU v7x, 256 devices: a whole 4x4x8 slice. The times are simulated.
256 devices in a mesh: lead: 16 (over y_lo, z), mesh: 16 (over x, y_hi, core).
Axes of the slice: x: 4, y: 4 (y_hi: 2, y_lo: 2; y = y_hi * 2 + y_lo), z: 8, core: 2. Of those that a mesh axis runs over, the one named last changes fastest.
Arguments:
- states: bfloat16 [16, 2, 2048, 1024], P('lead', None, 'mesh'), may hold values from -6 to 6
- entering: bfloat16 [2, 2, 2048, 1024], P(None, None, 'mesh'), may hold values from -6 to 6
- norm_gain: float32 [1024], replicated, may hold values from 0.1 to 1.9
- query_weight: bfloat16 [1024, 1024], replicated
- key_weight: bfloat16 [1024, 1024], replicated, as said below
- value_weight: bfloat16 [1024, 1024], replicated, may hold values from -0.1875 to 0.1875
- out_weight: bfloat16 [1024, 1024], replicated, may hold values from -0.1875 to 0.1875
- senders: int32 [2048, 8], P('mesh'), may hold values from 0 to 191, as said below
- halo_rows: int32 [16, 2, 32], P('mesh'), may hold values from 0 to 127
Outputs:
- advanced: bfloat16 [16, 2, 2048, 1024], P('lead', None, 'mesh')
Inputs may be any that keep to these rules, and one draw needn't show every extreme that they name: senders[n, 0] is n's own position in its partition; the others index the 128 own nodes, the 32 nodes from the partition before and the 32 from the one after, in that order; the first partition names none from before and the last none from after. `key_weight`: weights of fan-in 1024.
All inputs are finite; a program needn't handle non-finite values.
Results may differ from a plain program's by a relative error of at most 0.014.
Values may be sent and summed in bfloat16 or wider, within the bound.
No kernel may reach another device: no remote copies, remote signals or barrier semaphores. Data moves between devices by JAX's collectives and lax.ppermute only.
A program may use at most 64 MiB of HBM per device.

v0:
```python
import math

import jax
import jax.numpy as jnp
from jax import lax
from jax.sharding import PartitionSpec as P

HEADS = 16
HEAD_DIM = 64


def extended_2(block, sides, width):
    for axis, dim in sides:
        count = lax.axis_size(axis)
        forward = [(i, i + 1) for i in range(count - 1)]
        backward = [(target, source) for source, target in forward]
        low = lax.ppermute(
            lax.slice_in_dim(block, block.shape[dim] - width, None, axis=dim), axis, forward
        )
        high = lax.ppermute(lax.slice_in_dim(block, 0, width, axis=dim), axis, backward)
        block = jnp.concatenate([low, block, high], axis=dim)
    return block


def passed_along(block, axis, distance):
    devices = range(lax.axis_size(axis))
    route = [(i - distance, i) for i in devices if i - distance in devices]
    return lax.ppermute(block, axis, route)


def layer_norm(state, norm_gain):
    values = state.astype(jnp.float32)
    average = jnp.mean(values, axis=-1, keepdims=True)
    centred = values - average
    spread = jnp.mean(centred * centred, axis=-1, keepdims=True)
    return (centred * lax.rsqrt(spread + 1e-05) * norm_gain).astype(jnp.bfloat16)


def one_hot_table(indices, count):
    return (indices[..., None] == jnp.arange(count, dtype=jnp.int32)).astype(jnp.bfloat16)


def advance(state, norm_gain, query_weight, pair_weight, out_weight, sender_table, send_table):
    members, node_count, width = state.shape
    normed = layer_norm(state, norm_gain)
    queries = jnp.einsum(
        "mnd,de->mne", normed, query_weight, preferred_element_type=jnp.float32
    ).astype(jnp.bfloat16)
    key_value = jnp.einsum(
        "mnd,de->mne", normed, pair_weight, preferred_element_type=jnp.float32
    ).astype(jnp.bfloat16)
    outgoing = jnp.einsum(
        "shk,mkd->mshd", send_table, normed, preferred_element_type=jnp.float32
    ).astype(jnp.bfloat16)
    arrived = extended_2(outgoing, (("mesh", 1),), 1)
    remote = jnp.concatenate([arrived[:, 0], arrived[:, 3]], axis=1)
    extra = jnp.einsum(
        "mnd,de->mne", remote, pair_weight, preferred_element_type=jnp.float32
    ).astype(jnp.bfloat16)
    extended = jnp.concatenate([key_value, extra], axis=1)
    gathered = jnp.einsum(
        "njk,mkd->mnjd", sender_table, extended, preferred_element_type=jnp.float32
    ).astype(jnp.bfloat16)
    degree = sender_table.shape[1]
    sender_keys = gathered[..., :width].reshape(members, node_count, degree, HEADS, HEAD_DIM)
    sender_values = gathered[..., width:].reshape(members, node_count, degree, HEADS, HEAD_DIM)
    head_queries = queries.reshape(members, node_count, HEADS, HEAD_DIM)
    scores = jnp.einsum(
        "mnhd,mnjhd->mnjh", head_queries, sender_keys, preferred_element_type=jnp.float32
    ) / math.sqrt(HEAD_DIM)
    scores = scores - jnp.max(scores, axis=2, keepdims=True)
    expo = jnp.exp(scores)
    weights = (expo / jnp.sum(expo, axis=2, keepdims=True)).astype(jnp.bfloat16)
    attended = jnp.einsum(
        "mnjh,mnjhd->mnhd", weights, sender_values, preferred_element_type=jnp.float32
    )
    attended = attended.reshape(members, node_count, width).astype(jnp.bfloat16)
    update = jnp.einsum("mnd,de->mne", attended, out_weight, preferred_element_type=jnp.float32)
    return (state.astype(jnp.float32) + update).astype(jnp.bfloat16)


def per_device(
    states,
    entering,
    norm_gain,
    query_weight,
    key_weight,
    value_weight,
    out_weight,
    senders,
    halo_rows,
):
    pair_weight = jnp.concatenate([key_weight, value_weight], axis=1)
    node_count = states.shape[2]
    extended_count = node_count + 2 * halo_rows.shape[2]
    sender_table = one_hot_table(senders, extended_count)
    send_table = one_hot_table(halo_rows[0], node_count)
    is_first = lax.axis_index("lead") == 0
    current = states[0]
    for tick_index in range(entering.shape[0]):
        moved = passed_along(current, "lead", 1)
        current = jnp.where(is_first, entering[tick_index], moved)
        current = advance(
            current, norm_gain, query_weight, pair_weight, out_weight, sender_table, send_table
        )
    return current[None]


def solution(mesh):
    in_specs = (
        P("lead", None, "mesh", None),
        P(None, None, "mesh", None),
        P(),
        P(),
        P(),
        P(),
        P(),
        P("mesh", None),
        P("mesh", None, None),
    )
    out_specs = P("lead", None, "mesh", None)
    return jax.shard_map(
        per_device, mesh=mesh, in_specs=in_specs, out_specs=out_specs, check_vma=False
    )
```

profile of v0, /device:TPU:14, one launch (start us, length us, event | category | flops | bytes accessed | tf_op | source)
XLA Modules:
  0.0 98.7 jit_solution(17958206226939646049)
XLA Ops:
  0.0 3.9 %collective-permute-start = (bf16[2,128,1024]{2,1,0:T(8,128)(2,1)}, bf16[2,128,1024]{2,1,0:T(8,128)(2,1)S(1)}, u32[]{:S(2)}, u32[]{:S(2)}) collective-permute-start(bf16[2,128,1024]{2,1,0:T(8,128)(2,1)} %bitcast.130), channel_id=1, source_target_pairs={{0,16},{16,32},{32,48},{48,64},{64,80},{80,96},{96,112},{112,128},... | collective-permute-start | bytes 1572872 | tf_op jit(solution)/shard_map/ppermute | solution.py:28
  4.0 15.9 %collective-permute-done = bf16[2,128,1024]{2,1,0:T(8,128)(2,1)S(1)} collective-permute-done((bf16[2,128,1024]{2,1,0:T(8,128)(2,1)}, bf16[2,128,1024]{2,1,0:T(8,128)(2,1)S(1)}, u32[]{:S(2)}, u32[]{:S(2)}) %collective-permute-start) | collective-permute-done | bytes 524320 | tf_op jit(solution)/shard_map/ppermute | solution.py:28
  19.9 1.3 %convert_reduce_fusion.1 = (f32[2,128]{1,0:T(2,128)S(1)}, bf16[2,128,1024]{2,1,0:T(8,128)(2,1)S(1)}) fusion(bf16[2,128,1024]{2,1,0:T(8,128)(2,1)S(1)} %collective-permute-done, bf16[2,2,128,1024]{3,2,1,0:T(8,128)(2,1)} %param.10, pred[]{:T(512)S(6)} %eq.31), kind=kLoop, calls=%fused_computation.34 | loop fusion | flops 786176 | bytes 1573889 | tf_op jit(solution)/shard_map/reduce_sum | solution.py:33
  21.2 0.3 fusion.56
  21.5 1.1 %fusion.39 = bf16[2,2,32,1024]{3,2,1,0:T(8,128)(2,1)S(1)} fusion(bf16[2,128,1024]{2,1,0:T(8,128)(2,1)S(1)} %get-tuple-element.8, f32[1024]{0:T(1024)} %param.11, f32[2,128]{1,0:T(2,128)S(1)} %add_rsqrt_fusion.1, f32[2,128]{1,0:T(2,128)S(1)} %broadcast_multiply_fusion.1, s32[2,32]{1,0:T(2,128)} %bitcast.133), kind=kOutput, calls=%fused_computation.46 | convolution fusion | flops 35004416 | bytes 792832 | tf_op jit(solution)/shard_map/shk,mkd->mshd/dot_general | solution.py:52
  22.6 3.6 %collective-permute-start.2 = (bf16[2,1,32,1024]{3,2,1,0:T(8,128)(2,1)S(1)}, bf16[2,1,32,1024]{3,2,1,0:T(8,128)(2,1)S(1)}, u32[]{:S(2)}, u32[]{:S(2)}) collective-permute-start(bf16[2,1,32,1024]{3,2,1,0:T(8,128)(2,1)S(1)} %get-tuple-element.16), channel_id=1, source_target_pairs={{1,0},{2,1},{3,2},{4,3},{5,4},{6,5},{7,6},{8,7},{9,8},{10,9},{11,1... | collective-permute-start | bytes 393224 | tf_op jit(solution)/shard_map/ppermute | solution.py:20
  26.2 1.9 %collective-permute-start.1 = (bf16[2,1,32,1024]{3,2,0,1:T(8,128)(2,1)S(1)}, bf16[2,1,32,1024]{3,2,0,1:T(8,128)(2,1)}, u32[]{:S(2)}, u32[]{:S(2)}) collective-permute-start(bf16[2,1,32,1024]{3,2,0,1:T(8,128)(2,1)S(1)} %get-tuple-element.15), channel_id=1, source_target_pairs={{0,1},{1,2},{2,3},{3,4},{4,5},{5,6},{6,7},{7,8},{8,9},{9,10},{10,1... | collective-permute-start | bytes 393224 | tf_op jit(solution)/shard_map/ppermute | solution.py:17
  28.2 2.2 %fusion.26 = bf16[2,128,1024]{2,1,0:T(8,128)(2,1)} fusion(bf16[1024,1024]{1,0:T(8,128)(2,1)S(1)} %copy-done, bf16[2,128,1024]{2,1,0:T(8,128)(2,1)S(1)} %get-tuple-element.8, f32[1024]{0:T(1024)} %param.11, f32[2,128]{1,0:T(2,128)S(1)} %add_rsqrt_fusion.1, f32[2,128]{1,0:T(2,128)S(1)} %broadcast_multiply_fusion.1), kind=kOutput, calls=%fused_computation.37 | convolution fusion | flops 538443776 | bytes 3151872 | tf_op jit(solution)/shard_map/mnd,de->mne/dot_general | solution.py:46
  30.4 1.3 %copy.19 = bf16[2,128,1024]{1,2,0:T(8,128)(2,1)S(1)} copy(bf16[2,128,1024]{2,1,0:T(8,128)(2,1)} %fusion.26) | data formatting | bytes 1048576 | tf_op jit(solution)/shard_map/convert_element_type | solution.py:48
  31.8 3.7 %convolution_convert_fusion.1 = bf16[2,128,2048]{2,1,0:T(8,128)(2,1)S(1)} fusion(bf16[2,128,1024]{2,1,0:T(8,128)(2,1)S(1)} %get-tuple-element.8, f32[1024]{0:T(1024)S(1)} %copy-done.8, f32[2,128]{1,0:T(2,128)S(1)} %add_rsqrt_fusion.1, f32[2,128]{1,0:T(2,128)S(1)} %broadcast_multiply_fusion.1, bf16[1024,1024]{1,0:T(8,128)(2,1)} %param.14, ...), kind=kOutput, calls=%fused_computation.12 | convolution fusion | flops 1083965440 | bytes 5773312 | tf_op jit(solution)/shard_map/mnd,de->mne/dot_general | solution.py:49
  35.7 1.6 %convolution_convert_fusion.3 = bf16[2,64,2048]{2,1,0:T(8,128)(2,1)S(1)} fusion(bf16[2,32,1024]{2,1,0:T(8,128)(2,1)S(1)} %bitcast.131, bf16[2,32,1024]{2,1,0:T(8,128)(2,1)} %bitcast.15, bf16[1024,1024]{1,0:T(8,128)(2,1)S(1)} %copy-done.4, bf16[1024,1024]{1,0:T(8,128)(2,1)S(1)} %copy-done.6), kind=kOutput, calls=%fused_computation.14 | convolution fusion | flops 546045952 | bytes 4980736 | tf_op jit(solution)/shard_map/mnd,de->mne/dot_general | solution.py:57
  37.3 2.4 %convert_bitcast_fusion.1 = bf16[2,128,8,2048]{1,3,2,0:T(8,128)(2,1)S(1)} fusion(bf16[2,64,2048]{2,1,0:T(8,128)(2,1)S(1)} %convolution_convert_fusion.3, bf16[2,128,2048]{2,1,0:T(8,128)(2,1)S(1)} %convolution_convert_fusion.1, s32[128,8]{0,1:T(8,128)S(1)} %copy-done.9), kind=kOutput, calls=%fused_computation.9 | convolution fusion | flops 1618149376 | bytes 9965568 | tf_op jit(solution)/shard_map/njk,mkd->mnjd/dot_general | solution.py:61
  39.8 2.2 %fusion.102 = (bf16[2,128,8,1024]{1,3,2,0:T(8,128)(2,1)S(1)}, bf16[2,128,8,1024]{1,3,2,0:T(8,128)(2,1)}) fusion(bf16[2,128,8,2048]{1,3,2,0:T(8,128)(2,1)S(1)} %convert_bitcast_fusion.1), kind=kLoop, calls=%fused_computation.109 | loop fusion | bytes 16777216 | tf_op jit(solution)/shard_map/slice | solution.py:65
  42.0 1.8 %multiply_reduce_fusion.3 = f32[2,128,16,8]{1,2,3,0:T(8,128)S(1)} fusion(f32[2,128,16,64]{1,3,2,0:T(8,128)S(1)} %bitcast_convert_fusion.1, bf16[2,128,8,1024]{1,3,2,0:T(8,128)(2,1)S(1)} %get-tuple-element.11), kind=kLoop, calls=%fused_computation.7 | loop fusion | flops 6258688 | bytes 5373952
  43.9 3.6 %multiply_reduce_fusion.2 = bf16[2,128,16,64]{1,3,2,0:T(8,128)(2,1)S(1)} fusion(bf16[2,128,16,8,64]{1,4,2,3,0:T(8,128)(2,1)} %bitcast.126, f32[2,128,16,8]{1,2,3,0:T(8,128)S(1)} %copy.69), kind=kLoop, calls=%fused_computation.6 | loop fusion | flops 6029312 | bytes 4849664 | tf_op jit(solution)/shard_map/mnjh,mnjhd->mnhd/dot_general | solution.py:74
  47.6 0.7 fusion.20
  48.3 2.2 %collective-permute-start.3 = (bf16[2,128,1024]{2,1,0:T(8,128)(2,1)S(1)}, bf16[2,128,1024]{2,1,0:T(8,128)(2,1)S(1)}, u32[]{:S(2)}, u32[]{:S(2)}) collective-permute-start(bf16[2,128,1024]{2,1,0:T(8,128)(2,1)S(1)} %fusion.20), channel_id=1, source_target_pairs={{0,16},{16,32},{32,48},{48,64},{64,80},{80,96},{96,112},{112,128},... | collective-permute-start | bytes 1572872 | tf_op jit(solution)/shard_map/ppermute | solution.py:28
  50.6 16.7 %collective-permute-done.3 = bf16[2,128,1024]{2,1,0:T(8,128)(2,1)S(1)} collective-permute-done((bf16[2,128,1024]{2,1,0:T(8,128)(2,1)S(1)}, bf16[2,128,1024]{2,1,0:T(8,128)(2,1)S(1)}, u32[]{:S(2)}, u32[]{:S(2)}) %collective-permute-start.3) | collective-permute-done | bytes 524320 | tf_op jit(solution)/shard_map/ppermute | solution.py:28
  67.5 0.3 fusion.53
  67.8 0.4 fusion.40
  68.2 2.4 %convolution_convert_fusion = bf16[2,128,2048]{2,1,0:T(8,128)(2,1)} fusion(bf16[2,128,1024]{2,1,0:T(8,128)(2,1)S(1)} %get-tuple-element.6, f32[2,128]{1,0:T(2,128)S(1)} %add_rsqrt_fusion, f32[2,128]{1,0:T(2,128)S(1)} %broadcast_multiply_fusion, f32[1024]{0:T(1024)S(1)} %copy-done.8, bf16[1024,1024]{1,0:T(8,128)(2,1)S(1)} %copy-done.5, ...), kind=kOutput, calls=%fused_computation.11 | convolution fusion | flops 1083965440 | bytes 5773312 | tf_op jit(solution)/shard_map/mnd,de->mne/dot_general | solution.py:49
  70.6 1.6 %fusion.29 = bf16[2,128,1024]{2,1,0:T(8,128)(2,1)} fusion(bf16[1024,1024]{1,0:T(8,128)(2,1)S(1)} %copy-done, bf16[2,128,1024]{2,1,0:T(8,128)(2,1)S(1)} %get-tuple-element.6, f32[2,128]{1,0:T(2,128)S(1)} %add_rsqrt_fusion, f32[2,128]{1,0:T(2,128)S(1)} %broadcast_multiply_fusion, f32[1024]{0:T(1024)S(1)} %copy-done.8), kind=kOutput, calls=%fused_computation.38 | convolution fusion | flops 538443776 | bytes 3151872 | tf_op jit(solution)/shard_map/mnd,de->mne/dot_general | solution.py:46
  72.2 2.9 %collective-permute-start.5 = (bf16[2,1,32,1024]{3,2,1,0:T(8,128)(2,1)S(1)}, bf16[2,1,32,1024]{3,2,1,0:T(8,128)(2,1)S(1)}, u32[]{:S(2)}, u32[]{:S(2)}) collective-permute-start(bf16[2,1,32,1024]{3,2,1,0:T(8,128)(2,1)S(1)} %get-tuple-element.14), channel_id=1, source_target_pairs={{1,0},{2,1},{3,2},{4,3},{5,4},{6,5},{7,6},{8,7},{9,8},{10,9},{11,1... | collective-permute-start | bytes 393224 | tf_op jit(solution)/shard_map/ppermute | solution.py:20
  75.1 1.9 %collective-permute-start.4 = (bf16[2,1,32,1024]{3,2,0,1:T(8,128)(2,1)S(1)}, bf16[2,1,32,1024]{3,2,0,1:T(8,128)(2,1)}, u32[]{:S(2)}, u32[]{:S(2)}) collective-permute-start(bf16[2,1,32,1024]{3,2,0,1:T(8,128)(2,1)S(1)} %get-tuple-element.13), channel_id=1, source_target_pairs={{0,1},{1,2},{2,3},{3,4},{4,5},{5,6},{6,7},{7,8},{8,9},{9,10},{10,1... | collective-permute-start | bytes 393224 | tf_op jit(solution)/shard_map/ppermute | solution.py:17
  77.1 1.3 %copy.24 = bf16[2,128,1024]{1,2,0:T(8,128)(2,1)S(1)} copy(bf16[2,128,1024]{2,1,0:T(8,128)(2,1)} %fusion.29) | data formatting | bytes 1048576 | tf_op jit(solution)/shard_map/convert_element_type | solution.py:48
  78.5 5.4 %collective-permute-done.4 = bf16[2,1,32,1024]{3,2,0,1:T(8,128)(2,1)} collective-permute-done((bf16[2,1,32,1024]{3,2,0,1:T(8,128)(2,1)S(1)}, bf16[2,1,32,1024]{3,2,0,1:T(8,128)(2,1)}, u32[]{:S(2)}, u32[]{:S(2)}) %collective-permute-start.4) | collective-permute-done | bytes 131104 | tf_op jit(solution)/shard_map/ppermute | solution.py:17
  83.9 3.0 %convolution_convert_fusion.2 = bf16[2,64,2048]{2,1,0:T(8,128)(2,1)S(1)} fusion(bf16[2,32,1024]{2,1,0:T(8,128)(2,1)S(1)} %bitcast.132, bf16[2,32,1024]{2,1,0:T(8,128)(2,1)} %bitcast.33, bf16[1024,1024]{1,0:T(8,128)(2,1)} %param.14, bf16[1024,1024]{1,0:T(8,128)(2,1)} %param.13), kind=kOutput, calls=%fused_computation.13 | convolution fusion | flops 546045952 | bytes 4980736 | tf_op jit(solution)/shard_map/mnd,de->mne/dot_general | solution.py:57
  87.0 2.4 %convert_bitcast_fusion = bf16[2,128,8,2048]{1,3,2,0:T(8,128)(2,1)S(1)} fusion(bf16[2,64,2048]{2,1,0:T(8,128)(2,1)S(1)} %convolution_convert_fusion.2, bf16[2,128,2048]{2,1,0:T(8,128)(2,1)S(1)} %copy-done.11, s32[128,8]{0,1:T(8,128)S(1)} %copy-done.9), kind=kOutput, calls=%fused_computation.8 | convolution fusion | flops 1618149376 | bytes 9965568 | tf_op jit(solution)/shard_map/njk,mkd->mnjd/dot_general | solution.py:61
  89.4 2.2 %fusion.101 = (bf16[2,128,8,1024]{1,3,2,0:T(8,128)(2,1)S(1)}, bf16[2,128,8,1024]{1,3,2,0:T(8,128)(2,1)}) fusion(bf16[2,128,8,2048]{1,3,2,0:T(8,128)(2,1)S(1)} %convert_bitcast_fusion), kind=kLoop, calls=%fused_computation.108 | loop fusion | bytes 16777216 | tf_op jit(solution)/shard_map/slice | solution.py:65
  91.6 1.8 %multiply_reduce_fusion.1 = f32[2,128,16,8]{1,2,3,0:T(8,128)S(1)} fusion(f32[2,128,16,64]{1,3,2,0:T(8,128)S(1)} %bitcast_convert_fusion, bf16[2,128,8,1024]{1,3,2,0:T(8,128)(2,1)S(1)} %get-tuple-element.9), kind=kLoop, calls=%fused_computation.5 | loop fusion | flops 6258688 | bytes 5373952
  93.5 3.6 %multiply_reduce_fusion = bf16[2,128,16,64]{1,3,2,0:T(8,128)(2,1)S(1)} fusion(bf16[2,128,16,8,64]{1,4,2,3,0:T(8,128)(2,1)} %bitcast.127, f32[2,128,16,8]{1,2,3,0:T(8,128)S(1)} %copy.71), kind=kLoop, calls=%fused_computation.4 | loop fusion | flops 6029312 | bytes 4849664 | tf_op jit(solution)/shard_map/mnjh,mnjhd->mnhd/dot_general | solution.py:74
  97.1 1.5 %fusion.36 = bf16[1,2,128,1024]{3,2,1,0:T(8,128)(2,1)} fusion(bf16[2,128,1024]{1,2,0:T(8,128)(2,1)S(1)} %bitcast.129, bf16[1024,1024]{1,0:T(8,128)(2,1)S(1)} %copy-done.2, bf16[2,128,1024]{2,1,0:T(8,128)(2,1)S(1)} %get-tuple-element.6), kind=kOutput, calls=%fused_computation.43 | convolution fusion | flops 537657344 | bytes 3670016 | tf_op jit(solution)/shard_map/mnd,de->mne/dot_general | solution.py:78
  (40 shorter events, 0.9 us)
Async XLA Ops:
  0.0 28.2 %copy-start = (bf16[1024,1024]{1,0:T(8,128)(2,1)S(1)}, bf16[1024,1024]{1,0:T(8,128)(2,1)}, u32[]{:S(2)}) copy-start(bf16[1024,1024]{1,0:T(8,128)(2,1)} %param.12) | copy-start | bytes 6291460
  0.0 19.9 %collective-permute-start = (bf16[2,128,1024]{2,1,0:T(8,128)(2,1)}, bf16[2,128,1024]{2,1,0:T(8,128)(2,1)S(1)}, u32[]{:S(2)}, u32[]{:S(2)}) collective-permute-start(bf16[2,128,1024]{2,1,0:T(8,128)(2,1)} %bitcast.130), channel_id=1, source_target_pairs={{0,16},{16,32},{32,48},{48,64},{64,80},{80,96},{96,112},{112,128},... | collective-permute-start | bytes 1572872 | tf_op jit(solution)/shard_map/ppermute | solution.py:28
  4.0 27.8 %copy-start.8 = (f32[1024]{0:T(1024)S(1)}, f32[1024]{0:T(1024)}, u32[]{:S(2)}) copy-start(f32[1024]{0:T(1024)} %param.11) | copy-start | bytes 12292
  22.6 13.1 %collective-permute-start.2 = (bf16[2,1,32,1024]{3,2,1,0:T(8,128)(2,1)S(1)}, bf16[2,1,32,1024]{3,2,1,0:T(8,128)(2,1)S(1)}, u32[]{:S(2)}, u32[]{:S(2)}) collective-permute-start(bf16[2,1,32,1024]{3,2,1,0:T(8,128)(2,1)S(1)} %get-tuple-element.16), channel_id=1, source_target_pairs={{1,0},{2,1},{3,2},{4,3},{5,4},{6,5},{7,6},{8,7},{9,8},{10,9},{11,1... | collective-permute-start | bytes 393224 | tf_op jit(solution)/shard_map/ppermute | solution.py:20
  26.2 9.4 %collective-permute-start.1 = (bf16[2,1,32,1024]{3,2,0,1:T(8,128)(2,1)S(1)}, bf16[2,1,32,1024]{3,2,0,1:T(8,128)(2,1)}, u32[]{:S(2)}, u32[]{:S(2)}) collective-permute-start(bf16[2,1,32,1024]{3,2,0,1:T(8,128)(2,1)S(1)} %get-tuple-element.15), channel_id=1, source_target_pairs={{0,1},{1,2},{2,3},{3,4},{4,5},{5,6},{6,7},{7,8},{8,9},{9,10},{10,1... | collective-permute-start | bytes 393224 | tf_op jit(solution)/shard_map/ppermute | solution.py:17
  31.8 3.9 %copy-start.4 = (bf16[1024,1024]{1,0:T(8,128)(2,1)S(1)}, bf16[1024,1024]{1,0:T(8,128)(2,1)}, u32[]{:S(2)}) copy-start(bf16[1024,1024]{1,0:T(8,128)(2,1)} %param.14) | copy-start | bytes 6291460
  31.8 3.9 %copy-start.6 = (bf16[1024,1024]{1,0:T(8,128)(2,1)S(1)}, bf16[1024,1024]{1,0:T(8,128)(2,1)}, u32[]{:S(2)}) copy-start(bf16[1024,1024]{1,0:T(8,128)(2,1)} %param.13) | copy-start | bytes 6291460
  35.6 1.7 %copy-start.9 = (s32[128,8]{0,1:T(8,128)S(1)}, s32[128,8]{0,1:T(8,128)}, u32[]{:S(2)}) copy-start(s32[128,8]{0,1:T(8,128)} %param.16) | copy-start | bytes 12292
  43.9 3.7 %copy-start.1 = (bf16[1024,1024]{1,0:T(8,128)(2,1)S(1)}, bf16[1024,1024]{1,0:T(8,128)(2,1)}, u32[]{:S(2)}) copy-start(bf16[1024,1024]{1,0:T(8,128)(2,1)} %param.15) | copy-start | bytes 6291460
  43.9 23.3 %copy-start.3 = (bf16[2,2,128,1024]{3,2,1,0:T(8,128)(2,1)S(1)}, bf16[2,2,128,1024]{3,2,1,0:T(8,128)(2,1)}, u32[]{:S(2)}) copy-start(bf16[2,2,128,1024]{3,2,1,0:T(8,128)(2,1)} %param.10) | copy-start | bytes 3145732
  43.9 23.9 %copy-start.10 = (s32[1,2,32]{2,1,0:T(2,128)S(1)}, s32[1,2,32]{2,1,0:T(2,128)}, u32[]{:S(2)}) copy-start(s32[1,2,32]{2,1,0:T(2,128)} %param.17) | copy-start | bytes 772
  47.5 20.6 %copy-start.5 = (bf16[1024,1024]{1,0:T(8,128)(2,1)S(1)}, bf16[1024,1024]{1,0:T(8,128)(2,1)}, u32[]{:S(2)}) copy-start(bf16[1024,1024]{1,0:T(8,128)(2,1)} %param.14) | copy-start | bytes 6291460
  47.6 20.6 %copy-start.7 = (bf16[1024,1024]{1,0:T(8,128)(2,1)S(1)}, bf16[1024,1024]{1,0:T(8,128)(2,1)}, u32[]{:S(2)}) copy-start(bf16[1024,1024]{1,0:T(8,128)(2,1)} %param.13) | copy-start | bytes 6291460
  48.3 18.9 %collective-permute-start.3 = (bf16[2,128,1024]{2,1,0:T(8,128)(2,1)S(1)}, bf16[2,128,1024]{2,1,0:T(8,128)(2,1)S(1)}, u32[]{:S(2)}, u32[]{:S(2)}) collective-permute-start(bf16[2,128,1024]{2,1,0:T(8,128)(2,1)S(1)} %fusion.20), channel_id=1, source_target_pairs={{0,16},{16,32},{32,48},{48,64},{64,80},{80,96},{96,112},{112,128},... | collective-permute-start | bytes 1572872 | tf_op jit(solution)/shard_map/ppermute | solution.py:28
  72.2 6.3 %collective-permute-start.5 = (bf16[2,1,32,1024]{3,2,1,0:T(8,128)(2,1)S(1)}, bf16[2,1,32,1024]{3,2,1,0:T(8,128)(2,1)S(1)}, u32[]{:S(2)}, u32[]{:S(2)}) collective-permute-start(bf16[2,1,32,1024]{3,2,1,0:T(8,128)(2,1)S(1)} %get-tuple-element.14), channel_id=1, source_target_pairs={{1,0},{2,1},{3,2},{4,3},{5,4},{6,5},{7,6},{8,7},{9,8},{10,9},{11,1... | collective-permute-start | bytes 393224 | tf_op jit(solution)/shard_map/ppermute | solution.py:20
  75.1 8.8 %collective-permute-start.4 = (bf16[2,1,32,1024]{3,2,0,1:T(8,128)(2,1)S(1)}, bf16[2,1,32,1024]{3,2,0,1:T(8,128)(2,1)}, u32[]{:S(2)}, u32[]{:S(2)}) collective-permute-start(bf16[2,1,32,1024]{3,2,0,1:T(8,128)(2,1)S(1)} %get-tuple-element.13), channel_id=1, source_target_pairs={{0,1},{1,2},{2,3},{3,4},{4,5},{5,6},{6,7},{7,8},{8,9},{9,10},{10,1... | collective-permute-start | bytes 393224 | tf_op jit(solution)/shard_map/ppermute | solution.py:17
  78.5 8.5 %copy-start.11 = (bf16[2,128,2048]{2,1,0:T(8,128)(2,1)S(1)}, bf16[2,128,2048]{2,1,0:T(8,128)(2,1)}, u32[]{:S(2)}) copy-start(bf16[2,128,2048]{2,1,0:T(8,128)(2,1)} %convolution_convert_fusion) | copy-start | bytes 3145732
  93.5 3.7 %copy-start.2 = (bf16[1024,1024]{1,0:T(8,128)(2,1)S(1)}, bf16[1024,1024]{1,0:T(8,128)(2,1)}, u32[]{:S(2)}) copy-start(bf16[1024,1024]{1,0:T(8,128)(2,1)} %param.15) | copy-start | bytes 6291460
where the time goes:
time: 99.1 us; the launch traced here: 98.7 us
  waiting for transfers between devices  38 us (38%)
  matrix products  23.1 us (23%)
  starting transfers between devices  16.6 us (17%)
  other arithmetic  13.3 us (13%)
  local copies, waits for them, and re-layouts  7.23 us (7%)
    ppermute x2, waiting for transfers between devices, passed_along(): return lax.ppermute(block, axis, route)  32.6 us
    dot_general x2, other arithmetic, advance(): jnp.einsum('mnjh,mnjhd->mnhd', weights, sender_values, preferred_element_...  7.21 us
    ppermute x2, starting transfers between devices, extended_2(): lax.ppermute(lax.slice_in_dim(block, 0, width, axis=dim), axis, backward)  6.59 us
    ppermute x2, starting transfers between devices, passed_along(): return lax.ppermute(block, axis, route)  6.18 us
    dot_general x2, matrix products, advance(): jnp.einsum('mnd,de->mne', normed, pair_weight, preferred_element_type=jnp...  6.1 us
    ppermute x2, waiting for transfers between devices, extended_2(): lax.ppermute(lax.slice_in_dim(block, block.shape[dim] - width, None, axis...  5.41 us
    dot_general x2, matrix products, advance(): jnp.einsum('njk,mkd->mnjd', sender_table, extended, preferred_element_typ...  4.81 us
    dot_general x2, matrix products, advance(): jnp.einsum('mnd,de->mne', remote, pair_weight, preferred_element_type=jnp...  4.66 us
  transfers between devices with their start and end apart: 6, of which 3 were waited for; matrix products, arithmetic and copies ran while one was open for 9% of the time, Pallas kernels for 0%

commit v1 on v0

v1 whole, which is shorter than its diff:
```python
import functools
import jax
import jax.numpy as jnp
from jax import lax
from jax.experimental import pallas as pl
from jax.experimental.pallas import tpu as pltpu

HEAD_DIM = 64
LANES = 128
NEVER = -1e30
BF = jnp.bfloat16
F32 = jnp.float32
VMEM_BYTES = 24 * 1024 * 1024


def normalised(x, gain):
    values = x.astype(F32)
    centred = values - jnp.mean(values, axis=-1, keepdims=True)
    spread = jnp.mean(centred * centred, axis=-1, keepdims=True)
    return (centred * lax.rsqrt(spread + 1e-05) * gain).astype(BF)


def rows_of(table, indices):
    spots = lax.broadcasted_iota(jnp.int32, (table.shape[0], indices.shape[1]), 0)
    picks = jnp.where(spots == indices, 1.0, 0.0)
    return jnp.dot(picks.T.astype(BF), table, preferred_element_type=F32).astype(BF)


def prep_body(flag, x, other, gain, halo, senders, state, normed, low, high, table):
    chosen = jnp.where(flag[0] == 1, other[...], x[...])
    state[...] = chosen
    rows = normalised(chosen, gain[...])
    normed[...] = rows
    low[...] = rows_of(rows, halo[0:1])
    high[...] = rows_of(rows, halo[1:2])
    if table is not None:
        count = jnp.zeros(table.shape, F32)
        spots = lax.broadcasted_iota(jnp.int32, table.shape, 1)
        for j in range(senders.shape[1]):
            count += jnp.where(spots == senders[:, j:j + 1], 1.0, 0.0)
        table[...] = jnp.where(count > 0, jnp.log(count), NEVER)


def project_body(normed, wq, wk, wv, q, k, v):
    rows = normed[...]
    q[...] = (jnp.dot(rows, wq[...], preferred_element_type=F32)).astype(BF) * BF(HEAD_DIM ** -0.5)
    k[...] = jnp.dot(rows, wk[...], preferred_element_type=F32).astype(BF)
    v[...] = jnp.dot(rows, wv[...], preferred_element_type=F32).astype(BF)


def attend(state, q, k, v, before, after, table, wk, wv, wo, attended):
    halo = jnp.concatenate([before[...], after[...]], axis=0)
    more_k = jnp.dot(halo, wk[...], preferred_element_type=F32).astype(BF)
    more_v = jnp.dot(halo, wv[...], preferred_element_type=F32).astype(BF)
    bias = table[...]
    nodes, width = q.shape
    bias = jnp.concatenate([bias, bias], axis=0)
    first = lax.broadcasted_iota(jnp.int32, (nodes, LANES), 1) < HEAD_DIM
    ones = jnp.ones((table.shape[1], LANES), BF)
    for i in range(width // LANES):
        at = slice(i * LANES, (i + 1) * LANES)
        pair = q[:, at]
        zero = jnp.zeros_like(pair)
        both = jnp.concatenate([jnp.where(first, pair, zero), jnp.where(first, zero, pair)], axis=0)
        keys = jnp.concatenate([k[:, at], more_k[:, at]], axis=0)
        values = jnp.concatenate([v[:, at], more_v[:, at]], axis=0)
        scores = lax.dot_general(both, keys, (((1,), (1,)), ((), ())), preferred_element_type=F32) + bias
        expo = jnp.exp(scores - jnp.max(scores, axis=1, keepdims=True)).astype(BF)
        sums = jnp.dot(expo, jnp.concatenate([values, ones], axis=1), preferred_element_type=F32)
        top = sums[:nodes, :LANES] / sums[:nodes, LANES:]
        low = sums[nodes:, :LANES] / sums[nodes:, LANES:]
        attended[:, at] = jnp.where(first, top, low).astype(BF)
    update = jnp.dot(attended[...], wo[...], preferred_element_type=F32)
    return (state[...].astype(F32) + update).astype(BF)


def middle_body(flag, state, q, k, v, before, after, table, wk, wv, wo, other, gain, halo,
                new_state, normed, low, high, attended):
    moved = attend(state, q, k, v, before, after, table, wk, wv, wo, attended)
    chosen = jnp.where(flag[0] == 1, other[...], moved)
    new_state[...] = chosen
    rows = normalised(chosen, gain[...])
    normed[...] = rows
    low[...] = rows_of(rows, halo[0:1])
    high[...] = rows_of(rows, halo[1:2])


def last_body(state, q, k, v, before, after, table, wk, wv, wo, out, attended):
    out[...] = attend(state, q, k, v, before, after, table, wk, wv, wo, attended)

SMEM = pl.BlockSpec(memory_space=pltpu.SMEM)
VM = pl.BlockSpec(memory_space=pltpu.VMEM)

def shape(*dims, dtype=BF):
    return jax.ShapeDtypeStruct(dims, dtype)

def params():
    return pltpu.CompilerParams(vmem_limit_bytes=VMEM_BYTES)

def cost(flops, nbytes):
    return pl.CostEstimate(flops=flops, bytes_accessed=nbytes, transcendentals=0)

def prep(flag, x, other, gain, halo, senders=None):
    n, d = x.shape
    h = halo.shape[1]
    outs = [shape(n, d), shape(n, d), shape(h, d), shape(h, d)]
    ins = [flag, x, other, gain, halo]
    specs = [SMEM] + [VM] * 4
    if senders is not None:
        outs.append(shape(n, n + 2 * h, dtype=F32)); ins.append(senders); specs.append(VM)
        body = prep_body
    else:
        def body(flag, x, other, gain, halo, *outs):
            prep_body(flag, x, other, gain, halo, None, *outs, None)
    return pl.pallas_call(body, out_shape=outs, in_specs=specs, out_specs=[VM] * len(outs),
        compiler_params=params(), cost_estimate=cost(64 * n * d * 2, 8 * n * d), name="prep")(*ins)

def project(normed, wq, wk, wv):
    n, d = normed.shape
    return pl.pallas_call(project_body, out_shape=[shape(n, d)] * 3, in_specs=[VM] * 4, out_specs=[VM] * 3,
        compiler_params=params(), cost_estimate=cost(6 * n * d * d, 8 * n * d), name="project")(normed, wq, wk, wv)

def middle(flag, state, q, k, v, before, after, table, wk, wv, wo, other, gain, halo):
    n, d = state.shape
    h = halo.shape[1]
    return pl.pallas_call(middle_body, out_shape=[shape(n, d), shape(n, d), shape(h, d), shape(h, d)],
        in_specs=[SMEM] + [VM] * 13, out_specs=[VM] * 4, scratch_shapes=[pltpu.VMEM((n, d), BF)],
        compiler_params=params(), cost_estimate=cost(8 * n * d * d, 8 * n * d), name="middle")(
            flag, state, q, k, v, before, after, table, wk, wv, wo, other, gain, halo)

def last(state, q, k, v, before, after, table, wk, wv, wo):
    n, d = state.shape
    return pl.pallas_call(last_body, out_shape=shape(n, d),
        in_specs=[VM] * 10, out_specs=VM, scratch_shapes=[pltpu.VMEM((n, d), BF)],
        compiler_params=params(), cost_estimate=cost(8 * n * d * d, 8 * n * d), name="last")(
            state, q, k, v, before, after, table, wk, wv, wo)


def per_device(states, entering, norm_gain, wq, wk, wv, wo, senders, halo_rows):
    lead = lax.axis_index("lead")
    gain = norm_gain[None]
    halo = halo_rows[0]
    forward = [(i, (i + 1) % 16) for i in range(lax.axis_size("mesh"))]
    backward = [(b, a) for a, b in forward]
    leads = lax.axis_size("lead")
    route = [(i, (i + 2) % leads) for i in range(leads)]

    def is_lead(index):
        return (lead == index).astype(jnp.int32)[None]

    def swapped(low, high):
        return lax.ppermute(high, "mesh", forward), lax.ppermute(low, "mesh", backward)

    def first_half(state, member, at, senders=None):
        return prep(is_lead(at), state, entering[0, member], gain, halo, senders)

    far = lax.ppermute(states[0, 0], "lead", route)
    state, normed, low, high, table = first_half(states[0, 1], 1, leads - 1, senders)

    def advance_twice(state, normed, low, high, member, at):
        before, after = swapped(low, high)
        q, k, v = project(normed, wq, wk, wv)
        state, normed, low, high = middle(
            is_lead(at), state, q, k, v, before, after, table, wk, wv, wo, entering[1, member], gain, halo)
        before, after = swapped(low, high)
        q, k, v = project(normed, wq, wk, wv)
        return last(state, q, k, v, before, after, table, wk, wv, wo)

    near = advance_twice(state, normed, low, high, 1, leads - 2)
    done_far = lax.ppermute(near, "lead", route)
    state, normed, low, high = first_half(far, 0, 1)
    here = advance_twice(state, normed, low, high, 0, 0)
    return jnp.stack([here, done_far])[None]


def solution(mesh):
    P = jax.sharding.PartitionSpec
    in_specs = (
        P("lead", None, "mesh", None),
        P(None, None, "mesh", None),
        P(),
        P(),
        P(),
        P(),
        P(),
        P("mesh", None),
        P("mesh", None, None),
    )
    return jax.shard_map(
        per_device, mesh=mesh, in_specs=in_specs, out_specs=P("lead", None, "mesh", None), check_vma=False
    )
```

time: 99.1 us -> 62.2 us (0.63)
  the two profiles are of different devices: /device:TPU:14 before, /device:TPU:31 now
where the time goes in v1:
time: 62.2 us; the launch traced here: 61.9 us
  waiting for transfers between devices  18.3 us (29%)
  Pallas kernels  16.1 us (26%)
  starting transfers between devices  15.6 us (25%)
  local copies, waits for them, and re-layouts  10.9 us (18%)
  other arithmetic  0.84 us (1%)
    ppermute x4, waiting for transfers between devices, swapped(): lax.ppermute(low, 'mesh', backward)  17.8 us
    unnamed x29, local copies, waits for them, and re-layouts  7.67 us
    ppermute x4, starting transfers between devices, swapped(): lax.ppermute(high, 'mesh', forward)  7.6 us
    pallas_call x2, Pallas kernels, middle(): pl.pallas_call(middle_body, out_shape=[shape(n, d), shape(n, d), shape(h,...  6.23 us
    pallas_call x2, Pallas kernels, last(): pl.pallas_call(last_body, out_shape=shape(n, d), in_specs=[VM] * 10, out_...  4.41 us
    ppermute x1, starting transfers between devices, per_device(): done_far = lax.ppermute(near, 'lead', route)  4.28 us
    pallas_call x4, Pallas kernels, project(): pl.pallas_call(project_body, out_shape=[shape(n, d)] * 3, in_specs=[VM] *...  3.98 us
    ppermute x1, starting transfers between devices, per_device(): far = lax.ppermute(states[0, 0], 'lead', route)  2.99 us
  transfers between devices with their start and end apart: 10, of which 5 were waited for; matrix products, arithmetic and copies ran while one was open for 0% of the time, Pallas kernels for 24%

profile of v1, /device:TPU:31, one launch (start us, length us, event | category | flops | bytes accessed | tf_op | source)
XLA Modules:
  0.0 61.9 jit_solution(7769152668087148947)
XLA Ops:
  0.0 1.9 %slice_bitcast_fusion.5 = (bf16[128,1024]{1,0:T(8,128)(2,1)}, bf16[128,1024]{1,0:T(8,128)(2,1)S(1)}) fusion(bf16[1,2,128,1024]{3,2,1,0:T(8,128)(2,1)} %param.9), kind=kLoop, calls=%fused_computation.6 | loop fusion | bytes 1048576 | tf_op jit(solution)/shard_map/squeeze | solution.py:157
  1.9 1.3 %slice_bitcast_fusion.1 = (bf16[128,1024]{1,0:T(8,128)(2,1)S(1)}, bf16[128,1024]{1,0:T(8,128)(2,1)S(1)}, bf16[128,1024]{1,0:T(8,128)(2,1)S(1)}, bf16[128,1024]{1,0:T(8,128)(2,1)S(1)}) fusion(bf16[2,2,128,1024]{3,2,1,0:T(8,128)(2,1)} %param.10), kind=kLoop, calls=%fused_computation.2 | loop fusion | bytes 2097152 | tf_op jit(solution)/shard_map/squeeze | solution.py:164
  3.2 0.7 %copy.10.senders = s32[128,8]{1,0:T(8,128)} copy(s32[128,8]{0,1:T(8,128)S(1)} %copy-done.13) | data formatting | bytes 8192 | tf_op args[7]
  4.0 0.8 %copy-done.10 = s32[128,8]{1,0:T(8,128)S(1)} copy-done((s32[128,8]{1,0:T(8,128)S(1)}, s32[128,8]{1,0:T(8,128)}, u32[]{:S(2)}) %copy-start.10) | copy-done | bytes 4120
  4.8 1.1 %prep.3 = (bf16[128,1024]{1,0:T(8,128)(2,1)S(1)}, bf16[128,1024]{1,0:T(8,128)(2,1)S(1)}, bf16[32,1024]{1,0:T(8,128)(2,1)}, bf16[32,1024]{1,0:T(8,128)(2,1)}, f32[128,192]{1,0:T(8,128)S(1)}) custom-call(s32[1]{0:T(128)} %bitcast.6.flag, bf16[128,1024]{1,0:T(8,128)(2,1)S(1)} %get-tuple-element.68.x, bf16[128,1024]{1,0:T(8,128)(2,1)S(1)} %get-tuple-element.64.other, ...), custom_call_target="tpu_custom_call" | custom-call | flops 16777216 | bytes 1048576 | tf_op jit(solution)/shard_map/prep/pallas_call | solution.py:115
  5.9 0.7 %copy-done.6 = bf16[128,1024]{1,0:T(8,128)(2,1)} copy-done((bf16[128,1024]{1,0:T(8,128)(2,1)}, bf16[128,1024]{1,0:T(8,128)(2,1)S(1)}, u32[]{:S(2)}) %copy-start.6) | copy-done | bytes 262168
  6.6 0.7 %copy-done.8 = bf16[128,1024]{1,0:T(8,128)(2,1)} copy-done((bf16[128,1024]{1,0:T(8,128)(2,1)}, bf16[128,1024]{1,0:T(8,128)(2,1)S(1)}, u32[]{:S(2)}) %copy-start.8) | copy-done | bytes 262168
  7.3 1.4 %collective-permute-start.5 = (bf16[32,1024]{1,0:T(8,128)(2,1)}, bf16[32,1024]{1,0:T(8,128)(2,1)}, u32[]{:S(2)}, u32[]{:S(2)}) collective-permute-start(bf16[32,1024]{1,0:T(8,128)(2,1)} %get-tuple-element.54), channel_id=1, source_target_pairs={{0,1},{1,2},{2,3},{3,4},{4,5},{5,6},{6,7},{7,8},{8,9},{9,10},{10,1... | collective-permute-start | bytes 196616 | tf_op jit(solution)/shard_map/ppermute | solution.py:152
  8.7 3.0 %collective-permute-start = (bf16[128,1024]{1,0:T(8,128)(2,1)}, bf16[128,1024]{1,0:T(8,128)(2,1)S(1)}, u32[]{:S(2)}, u32[]{:S(2)}) collective-permute-start(bf16[128,1024]{1,0:T(8,128)(2,1)} %get-tuple-element.67), channel_id=1, source_target_pairs={{0,32},{16,48},{32,64},{48,80},{64,96},{80,112},{96,128},{112,144}... | collective-permute-start | bytes 786440 | tf_op jit(solution)/shard_map/ppermute | solution.py:157
  11.7 1.6 %copy-done.1 = bf16[1024,1024]{1,0:T(8,128)(2,1)S(1)} copy-done((bf16[1024,1024]{1,0:T(8,128)(2,1)S(1)}, bf16[1024,1024]{1,0:T(8,128)(2,1)}, u32[]{:S(2)}) %copy-start.1) | copy-done | bytes 2097176
  13.3 1.6 %copy-done.3 = bf16[1024,1024]{1,0:T(8,128)(2,1)S(1)} copy-done((bf16[1024,1024]{1,0:T(8,128)(2,1)S(1)}, bf16[1024,1024]{1,0:T(8,128)(2,1)}, u32[]{:S(2)}) %copy-start.3) | copy-done | bytes 2097176
  14.9 0.9 %copy-done.9 = bf16[128,1024]{1,0:T(8,128)(2,1)S(1)} copy-done((bf16[128,1024]{1,0:T(8,128)(2,1)S(1)}, bf16[128,1024]{1,0:T(8,128)(2,1)}, u32[]{:S(2)}) %copy-start.9) | copy-done | bytes 262168
  15.9 1.0 %project.6 = (bf16[128,1024]{1,0:T(8,128)(2,1)S(1)}, bf16[128,1024]{1,0:T(8,128)(2,1)S(1)}, bf16[128,1024]{1,0:T(8,128)(2,1)S(1)}) custom-call(bf16[128,1024]{1,0:T(8,128)(2,1)S(1)} %copy-done.9, bf16[1024,1024]{1,0:T(8,128)(2,1)S(1)} %copy-done.3, bf16[1024,1024]{1,0:T(8,128)(2,1)S(1)} %copy-done, bf16[1024,1024]{1,0:T(8,128)(2,1)S(1)} %copy-done.1), custom_call_target="tpu_custom_call" | custom-call | flops 805306368 | bytes 1048576 | tf_op jit(solution)/shard_map/project/pallas_call | solution.py:120
  16.9 0.6 copy-done.5
  17.4 3.6 %middle.3 = (bf16[128,1024]{1,0:T(8,128)(2,1)S(1)}, bf16[128,1024]{1,0:T(8,128)(2,1)S(1)}, bf16[32,1024]{1,0:T(8,128)(2,1)S(1)}, bf16[32,1024]{1,0:T(8,128)(2,1)S(1)}) custom-call(s32[1]{0:T(128)} %bitcast.11.flag, bf16[128,1024]{1,0:T(8,128)(2,1)S(1)} %copy-done.7, bf16[128,1024]{1,0:T(8,128)(2,1)S(1)} %get-tuple-element.51.q, ...), custom_call_target="tpu_custom_call" | custom-call | flops 1073741824 | bytes 1048576 | tf_op jit(solution)/shard_map/middle/pallas_call | solution.py:126
  21.1 5.7 %collective-permute-start.7 = (bf16[32,1024]{1,0:T(8,128)(2,1)S(1)}, bf16[32,1024]{1,0:T(8,128)(2,1)S(1)}, u32[]{:S(2)}, u32[]{:S(2)}) collective-permute-start(bf16[32,1024]{1,0:T(8,128)(2,1)S(1)} %get-tuple-element.61), channel_id=1, source_target_pairs={{0,1},{1,2},{2,3},{3,4},{4,5},{5,6},{6,7},{7,8},{8,9},{9,10},{10,1... | collective-permute-start | bytes 196616 | tf_op jit(solution)/shard_map/ppermute | solution.py:152
  26.8 1.0 %project.7 = (bf16[128,1024]{1,0:T(8,128)(2,1)S(1)}, bf16[128,1024]{1,0:T(8,128)(2,1)S(1)}, bf16[128,1024]{1,0:T(8,128)(2,1)S(1)}) custom-call(bf16[128,1024]{1,0:T(8,128)(2,1)S(1)} %get-tuple-element.57.normed, bf16[1024,1024]{1,0:T(8,128)(2,1)S(1)} %copy-done.4, bf16[1024,1024]{1,0:T(8,128)(2,1)S(1)} %copy-done, bf16[1024,1024]{1,0:T(8,128)(2,1)S(1)} %copy-done.1), custom_call_target="tpu_custom_call" | custom-call | flops 805306368 | bytes 1048576 | tf_op jit(solution)/shard_map/project/pallas_call | solution.py:120
  27.8 0.3 collective-permute-done.7.before
  28.1 6.0 %collective-permute-done.8.after = bf16[32,1024]{1,0:T(8,128)(2,1)S(1)} collective-permute-done((bf16[32,1024]{1,0:T(8,128)(2,1)S(1)}, bf16[32,1024]{1,0:T(8,128)(2,1)S(1)}, u32[]{:S(2)}, u32[]{:S(2)}) %collective-permute-start.8) | collective-permute-done | bytes 65568 | tf_op jit(solution)/shard_map/ppermute | solution.py:152
  34.1 2.2 %last.3 = bf16[128,1024]{1,0:T(8,128)(2,1)S(1)} custom-call(bf16[128,1024]{1,0:T(8,128)(2,1)S(1)} %get-tuple-element.56.state, bf16[128,1024]{1,0:T(8,128)(2,1)S(1)} %get-tuple-element.58.q, bf16[128,1024]{1,0:T(8,128)(2,1)S(1)} %get-tuple-element.59.k, bf16[128,1024]{1,0:T(8,128)(2,1)S(1)} %get-tuple-element.60.v, ...), custom_call_target="tpu_custom_call" | custom-call | flops 1073741824 | bytes 1048576 | tf_op jit(solution)/shard_map/last/pallas_call | solution.py:133
  36.3 4.3 %collective-permute-start.9 = (bf16[128,1024]{1,0:T(8,128)(2,1)S(1)}, bf16[128,1024]{1,0:T(8,128)(2,1)S(1)}, u32[]{:S(2)}, u32[]{:S(2)}) collective-permute-start(bf16[128,1024]{1,0:T(8,128)(2,1)S(1)} %last.3), channel_id=1, source_target_pairs={{0,32},{16,48},{32,64},{48,80},{64,96},{80,112},{96,128},{112,144}... | collective-permute-start | bytes 786440 | tf_op jit(solution)/shard_map/ppermute | solution.py:170
  40.6 0.4 prep.2
  41.0 0.4 collective-permute-start.1
  41.4 0.2 collective-permute-start.2
  41.6 1.0 %project.4 = (bf16[128,1024]{1,0:T(8,128)(2,1)S(1)}, bf16[128,1024]{1,0:T(8,128)(2,1)S(1)}, bf16[128,1024]{1,0:T(8,128)(2,1)S(1)}) custom-call(bf16[128,1024]{1,0:T(8,128)(2,1)S(1)} %get-tuple-element.35.normed, bf16[1024,1024]{1,0:T(8,128)(2,1)S(1)} %copy-done.4, bf16[1024,1024]{1,0:T(8,128)(2,1)S(1)} %copy-done, bf16[1024,1024]{1,0:T(8,128)(2,1)S(1)} %copy-done.2), custom_call_target="tpu_custom_call" | custom-call | flops 805306368 | bytes 1048576 | tf_op jit(solution)/shard_map/project/pallas_call | solution.py:120
  42.7 6.0 %collective-permute-done.2.after = bf16[32,1024]{1,0:T(8,128)(2,1)S(1)} collective-permute-done((bf16[32,1024]{1,0:T(8,128)(2,1)S(1)}, bf16[32,1024]{1,0:T(8,128)(2,1)S(1)}, u32[]{:S(2)}, u32[]{:S(2)}) %collective-permute-start.2) | collective-permute-done | bytes 65568 | tf_op jit(solution)/shard_map/ppermute | solution.py:152
  48.7 2.6 %middle.2 = (bf16[128,1024]{1,0:T(8,128)(2,1)S(1)}, bf16[128,1024]{1,0:T(8,128)(2,1)S(1)}, bf16[32,1024]{1,0:T(8,128)(2,1)S(1)}, bf16[32,1024]{1,0:T(8,128)(2,1)S(1)}) custom-call(s32[1]{0:T(128)} %bitcast.flag, bf16[128,1024]{1,0:T(8,128)(2,1)S(1)} %get-tuple-element.34.state, bf16[128,1024]{1,0:T(8,128)(2,1)S(1)} %get-tuple-element.36.q, ...), custom_call_target="tpu_custom_call" | custom-call | flops 1073741824 | bytes 1048576 | tf_op jit(solution)/shard_map/middle/pallas_call | solution.py:126
  51.4 0.5 collective-permute-start.4
  51.9 1.0 %project.5 = (bf16[128,1024]{1,0:T(8,128)(2,1)S(1)}, bf16[128,1024]{1,0:T(8,128)(2,1)S(1)}, bf16[128,1024]{1,0:T(8,128)(2,1)S(1)}) custom-call(bf16[128,1024]{1,0:T(8,128)(2,1)S(1)} %get-tuple-element.43.normed, bf16[1024,1024]{1,0:T(8,128)(2,1)S(1)} %copy-done.4, bf16[1024,1024]{1,0:T(8,128)(2,1)S(1)} %copy-done, bf16[1024,1024]{1,0:T(8,128)(2,1)S(1)} %copy-done.2), custom_call_target="tpu_custom_call" | custom-call | flops 805306368 | bytes 1048576 | tf_op jit(solution)/shard_map/project/pallas_call | solution.py:120
  52.9 5.9 %collective-permute-done.4.after = bf16[32,1024]{1,0:T(8,128)(2,1)S(1)} collective-permute-done((bf16[32,1024]{1,0:T(8,128)(2,1)S(1)}, bf16[32,1024]{1,0:T(8,128)(2,1)S(1)}, u32[]{:S(2)}, u32[]{:S(2)}) %collective-permute-start.4) | collective-permute-done | bytes 65568 | tf_op jit(solution)/shard_map/ppermute | solution.py:152
  58.8 2.2 %last.2 = bf16[128,1024]{1,0:T(8,128)(2,1)S(1)} custom-call(bf16[128,1024]{1,0:T(8,128)(2,1)S(1)} %get-tuple-element.42.state, bf16[128,1024]{1,0:T(8,128)(2,1)S(1)} %get-tuple-element.44.q, bf16[128,1024]{1,0:T(8,128)(2,1)S(1)} %get-tuple-element.45.k, bf16[128,1024]{1,0:T(8,128)(2,1)S(1)} %get-tuple-element.46.v, ...), custom_call_target="tpu_custom_call" | custom-call | flops 1073741824 | bytes 1048576 | tf_op jit(solution)/shard_map/last/pallas_call | solution.py:133
  61.0 0.8 %maximum_bitcast_fusion = bf16[1,2,128,1024]{3,2,1,0:T(8,128)(2,1)} fusion(bf16[1,128,1024]{2,1,0:T(8,128)(2,1)S(1)} %bitcast.31, bf16[1,128,1024]{2,1,0:T(8,128)(2,1)S(1)} %bitcast.22), kind=kLoop, calls=%fused_computation | loop fusion | flops 262144 | bytes 1048576 | tf_op jit(solution)/shard_map/broadcast_in_dim | solution.py:173
  (30 shorter events, 0.2 us)
Async XLA Ops:
  0.0 3.2 %copy-start.13 = (s32[128,8]{0,1:T(8,128)S(1)}, s32[128,8]{0,1:T(8,128)}, u32[]{:S(2)}) copy-start(s32[128,8]{0,1:T(8,128)} %param.16) | copy-start | bytes 12292
  0.0 3.9 %copy-start.11 = (f32[1024]{0:T(1024)S(1)}, f32[1024]{0:T(1024)}, u32[]{:S(2)}) copy-start(f32[1024]{0:T(1024)} %param.11) | copy-start | bytes 12292
  0.0 3.9 %copy-start.12 = (s32[1,2,32]{2,1,0:T(2,128)S(1)}, s32[1,2,32]{2,1,0:T(2,128)}, u32[]{:S(2)}) copy-start(s32[1,2,32]{2,1,0:T(2,128)} %param.17) | copy-start | bytes 772
  0.0 11.7 %copy-start = (bf16[1024,1024]{1,0:T(8,128)(2,1)S(1)}, bf16[1024,1024]{1,0:T(8,128)(2,1)}, u32[]{:S(2)}) copy-start(bf16[1024,1024]{1,0:T(8,128)(2,1)} %wk.15) | copy-start | bytes 6291460
  4.0 0.8 %copy-start.10 = (s32[128,8]{1,0:T(8,128)S(1)}, s32[128,8]{1,0:T(8,128)}, u32[]{:S(2)}) copy-start(s32[128,8]{1,0:T(8,128)} %copy.10.senders) | copy-start | bytes 12292
  5.9 0.7 %copy-start.6 = (bf16[128,1024]{1,0:T(8,128)(2,1)}, bf16[128,1024]{1,0:T(8,128)(2,1)S(1)}, u32[]{:S(2)}) copy-start(bf16[128,1024]{1,0:T(8,128)(2,1)S(1)} %get-tuple-element.49.state) | copy-start | bytes 786436
  6.6 0.7 %copy-start.8 = (bf16[128,1024]{1,0:T(8,128)(2,1)}, bf16[128,1024]{1,0:T(8,128)(2,1)S(1)}, u32[]{:S(2)}) copy-start(bf16[128,1024]{1,0:T(8,128)(2,1)S(1)} %get-tuple-element.50.normed) | copy-start | bytes 786436
  7.3 9.6 %collective-permute-start.5 = (bf16[32,1024]{1,0:T(8,128)(2,1)}, bf16[32,1024]{1,0:T(8,128)(2,1)}, u32[]{:S(2)}, u32[]{:S(2)}) collective-permute-start(bf16[32,1024]{1,0:T(8,128)(2,1)} %get-tuple-element.54), channel_id=1, source_target_pairs={{0,1},{1,2},{2,3},{3,4},{4,5},{5,6},{6,7},{7,8},{8,9},{9,10},{10,1... | collective-permute-start | bytes 196616 | tf_op jit(solution)/shard_map/ppermute | solution.py:152
  8.7 8.2 %collective-permute-start.6 = (bf16[32,1024]{1,0:T(8,128)(2,1)}, bf16[32,1024]{1,0:T(8,128)(2,1)}, u32[]{:S(2)}, u32[]{:S(2)}) collective-permute-start(bf16[32,1024]{1,0:T(8,128)(2,1)} %get-tuple-element.55), channel_id=1, source_target_pairs={{1,0},{2,1},{3,2},{4,3},{5,4},{6,5},{7,6},{8,7},{9,8},{10,9},{11,1... | collective-permute-start | bytes 196616 | tf_op jit(solution)/shard_map/ppermute | solution.py:152
  8.7 31.9 %collective-permute-start = (bf16[128,1024]{1,0:T(8,128)(2,1)}, bf16[128,1024]{1,0:T(8,128)(2,1)S(1)}, u32[]{:S(2)}, u32[]{:S(2)}) collective-permute-start(bf16[128,1024]{1,0:T(8,128)(2,1)} %get-tuple-element.67), channel_id=1, source_target_pairs={{0,32},{16,48},{32,64},{48,80},{64,96},{80,112},{96,128},{112,144}... | collective-permute-start | bytes 786440 | tf_op jit(solution)/shard_map/ppermute | solution.py:157
  11.7 1.6 %copy-start.1 = (bf16[1024,1024]{1,0:T(8,128)(2,1)S(1)}, bf16[1024,1024]{1,0:T(8,128)(2,1)}, u32[]{:S(2)}) copy-start(bf16[1024,1024]{1,0:T(8,128)(2,1)} %wv.15) | copy-start | bytes 6291460
  13.3 1.6 %copy-start.3 = (bf16[1024,1024]{1,0:T(8,128)(2,1)S(1)}, bf16[1024,1024]{1,0:T(8,128)(2,1)}, u32[]{:S(2)}) copy-start(bf16[1024,1024]{1,0:T(8,128)(2,1)} %wq.7) | copy-start | bytes 6291460
  14.9 0.9 %copy-start.9 = (bf16[128,1024]{1,0:T(8,128)(2,1)S(1)}, bf16[128,1024]{1,0:T(8,128)(2,1)}, u32[]{:S(2)}) copy-start(bf16[128,1024]{1,0:T(8,128)(2,1)} %copy-done.8) | copy-start | bytes 786436
  15.9 1.6 %copy-start.5 = (bf16[1024,1024]{1,0:T(8,128)(2,1)S(1)}, bf16[1024,1024]{1,0:T(8,128)(2,1)}, u32[]{:S(2)}) copy-start(bf16[1024,1024]{1,0:T(8,128)(2,1)} %wo.7) | copy-start | bytes 6291460
  15.9 1.6 %copy-start.7 = (bf16[128,1024]{1,0:T(8,128)(2,1)S(1)}, bf16[128,1024]{1,0:T(8,128)(2,1)}, u32[]{:S(2)}) copy-start(bf16[128,1024]{1,0:T(8,128)(2,1)} %copy-done.6) | copy-start | bytes 786436
  17.4 9.4 %copy-start.4 = (bf16[1024,1024]{1,0:T(8,128)(2,1)S(1)}, bf16[1024,1024]{1,0:T(8,128)(2,1)}, u32[]{:S(2)}) copy-start(bf16[1024,1024]{1,0:T(8,128)(2,1)} %wq.7) | copy-start | bytes 6291460
  21.1 7.0 %collective-permute-start.7 = (bf16[32,1024]{1,0:T(8,128)(2,1)S(1)}, bf16[32,1024]{1,0:T(8,128)(2,1)S(1)}, u32[]{:S(2)}, u32[]{:S(2)}) collective-permute-start(bf16[32,1024]{1,0:T(8,128)(2,1)S(1)} %get-tuple-element.61), channel_id=1, source_target_pairs={{0,1},{1,2},{2,3},{3,4},{4,5},{5,6},{6,7},{7,8},{8,9},{9,10},{10,1... | collective-permute-start | bytes 196616 | tf_op jit(solution)/shard_map/ppermute | solution.py:152
  26.8 7.3 %collective-permute-start.8 = (bf16[32,1024]{1,0:T(8,128)(2,1)S(1)}, bf16[32,1024]{1,0:T(8,128)(2,1)S(1)}, u32[]{:S(2)}, u32[]{:S(2)}) collective-permute-start(bf16[32,1024]{1,0:T(8,128)(2,1)S(1)} %get-tuple-element.62), channel_id=1, source_target_pairs={{1,0},{2,1},{3,2},{4,3},{5,4},{6,5},{7,6},{8,7},{9,8},{10,9},{11,1... | collective-permute-start | bytes 196616 | tf_op jit(solution)/shard_map/ppermute | solution.py:152
  26.8 7.3 %copy-start.2 = (bf16[1024,1024]{1,0:T(8,128)(2,1)S(1)}, bf16[1024,1024]{1,0:T(8,128)(2,1)}, u32[]{:S(2)}) copy-start(bf16[1024,1024]{1,0:T(8,128)(2,1)} %wv.15) | copy-start | bytes 6291460
  36.3 24.7 %collective-permute-start.9 = (bf16[128,1024]{1,0:T(8,128)(2,1)S(1)}, bf16[128,1024]{1,0:T(8,128)(2,1)S(1)}, u32[]{:S(2)}, u32[]{:S(2)}) collective-permute-start(bf16[128,1024]{1,0:T(8,128)(2,1)S(1)} %last.3), channel_id=1, source_target_pairs={{0,32},{16,48},{32,64},{48,80},{64,96},{80,112},{96,128},{112,144}... | collective-permute-start | bytes 786440 | tf_op jit(solution)/shard_map/ppermute | solution.py:170
  41.0 1.7 %collective-permute-start.1 = (bf16[32,1024]{1,0:T(8,128)(2,1)S(1)}, bf16[32,1024]{1,0:T(8,128)(2,1)S(1)}, u32[]{:S(2)}, u32[]{:S(2)}) collective-permute-start(bf16[32,1024]{1,0:T(8,128)(2,1)S(1)} %get-tuple-element.39), channel_id=1, source_target_pairs={{0,1},{1,2},{2,3},{3,4},{4,5},{5,6},{6,7},{7,8},{8,9},{9,10},{10,1... | collective-permute-start | bytes 196616 | tf_op jit(solution)/shard_map/ppermute | solution.py:152
  41.4 7.3 %collective-permute-start.2 = (bf16[32,1024]{1,0:T(8,128)(2,1)S(1)}, bf16[32,1024]{1,0:T(8,128)(2,1)S(1)}, u32[]{:S(2)}, u32[]{:S(2)}) collective-permute-start(bf16[32,1024]{1,0:T(8,128)(2,1)S(1)} %get-tuple-element.40), channel_id=1, source_target_pairs={{1,0},{2,1},{3,2},{4,3},{5,4},{6,5},{7,6},{8,7},{9,8},{10,9},{11,1... | collective-permute-start | bytes 196616 | tf_op jit(solution)/shard_map/ppermute | solution.py:152
  51.3 1.6 %collective-permute-start.3 = (bf16[32,1024]{1,0:T(8,128)(2,1)S(1)}, bf16[32,1024]{1,0:T(8,128)(2,1)S(1)}, u32[]{:S(2)}, u32[]{:S(2)}) collective-permute-start(bf16[32,1024]{1,0:T(8,128)(2,1)S(1)} %get-tuple-element.47), channel_id=1, source_target_pairs={{0,1},{1,2},{2,3},{3,4},{4,5},{5,6},{6,7},{7,8},{8,9},{9,10},{10,1... | collective-permute-start | bytes 196616 | tf_op jit(solution)/shard_map/ppermute | solution.py:152
  51.4 7.4 %collective-permute-start.4 = (bf16[32,1024]{1,0:T(8,128)(2,1)S(1)}, bf16[32,1024]{1,0:T(8,128)(2,1)S(1)}, u32[]{:S(2)}, u32[]{:S(2)}) collective-permute-start(bf16[32,1024]{1,0:T(8,128)(2,1)S(1)} %get-tuple-element.48), channel_id=1, source_target_pairs={{1,0},{2,1},{3,2},{4,3},{5,4},{6,5},{7,6},{8,7},{9,8},{10,9},{11,1... | collective-permute-start | bytes 196616 | tf_op jit(solution)/shard_map/ppermute | solution.py:152

commit v2 on v1

v2 whole, which is shorter than its diff:
```python
import functools

import jax
import jax.numpy as jnp
from jax import lax
from jax.experimental import pallas as pl
from jax.experimental.pallas import tpu as pltpu

HEAD_DIM = 64
LANES = 128
NEVER = -1e30
BF = jnp.bfloat16
F32 = jnp.float32
VMEM_BYTES = 16 * 1024 * 1024
VMEM = pl.BlockSpec(memory_space=pltpu.VMEM)
HBM = pl.BlockSpec(memory_space=pltpu.HBM)
ANY = pl.BlockSpec(memory_space=pl.ANY)


def shape(*dims, dtype=BF):
    return jax.ShapeDtypeStruct(dims, dtype)


def call(body, name, ins, specs, outs, out_specs, scratch=(), micros=1.0, **more):
    return pl.pallas_call(
        body,
        out_shape=outs,
        in_specs=specs,
        out_specs=out_specs,
        scratch_shapes=list(scratch),
        compiler_params=pltpu.CompilerParams(vmem_limit_bytes=VMEM_BYTES),
        cost_estimate=pl.CostEstimate(flops=int(micros * 1e9), bytes_accessed=1000, transcendentals=0),
        name=name,
        **more,
    )(*ins)


def normalised(x, gain):
    values = x.astype(F32)
    centred = values - jnp.mean(values, axis=-1, keepdims=True)
    spread = jnp.mean(centred * centred, axis=-1, keepdims=True)
    return (centred * lax.rsqrt(spread + 1e-05) * gain).astype(BF)


def rows_of(table, indices):
    spots = lax.broadcasted_iota(jnp.int32, (table.shape[0], indices.shape[1]), 0)
    picks = jnp.where(spots == indices, 1.0, 0.0)
    return jnp.dot(picks.T.astype(BF), table, preferred_element_type=F32).astype(BF)


def begin(chosen, gain, halo, odd, state, normed, cross, inner):
    state[...] = chosen
    rows = normalised(chosen, gain[...])
    normed[...] = rows
    low, high = halo[0:1], halo[1:2]
    cross[...] = rows_of(rows, jnp.where(odd == 1, high, low))
    inner[...] = rows_of(rows, jnp.where(odd == 1, low, high))


def bias_table(senders, odd, table):
    nodes = table.shape[0]
    count = jnp.zeros((table.shape[1], nodes), F32)
    spots = lax.broadcasted_iota(jnp.int32, count.shape, 0)
    half = (table.shape[1] - nodes) // 2
    spots = jnp.where((spots >= nodes) & (odd == 1), jnp.where(spots >= nodes + half, spots - half, spots + half), spots)
    for j in range(senders.shape[0]):
        count += jnp.where(spots == senders[j:j + 1], 1.0, 0.0)
    table[...] = jnp.where(count > 0, jnp.log(count), NEVER).T


def place_of(index):
    return lax.axis_index("lead") == index, lax.rem(lax.axis_index("mesh"), 2)


def near_first_body(index, states, entering, all_gain, all_halo, all_senders,
                    state, normed, cross, inner, table, far, own, gain, halo, senders, sems):
    special, odd = place_of(index)
    small = [
        pltpu.make_async_copy(source, target, sems.at[2 + i])
        for i, (source, target) in enumerate(((all_senders, senders), (all_halo, halo), (all_gain, gain)))
    ]
    for copy in small:
        copy.start()

    @pl.when(special)
    def _():
        pltpu.make_async_copy(entering.at[0, 1], own, sems.at[1]).start()

    @pl.when(jnp.logical_not(special))
    def _():
        pltpu.make_async_copy(states.at[0, 1], own, sems.at[1]).start()

    to_far = pltpu.make_async_copy(states.at[0, 0], far, sems.at[0])
    to_far.start()
    for copy in small:
        copy.wait()
    bias_table(senders, odd, table)
    pltpu.make_async_copy(states.at[0, 1], own, sems.at[1]).wait()
    begin(own[...], gain, halo, odd, state, normed, cross, inner)
    to_far.wait()


def far_first_body(index, moved, entering, gain, halo, token, state, normed, cross, inner, own, sem):
    special, odd = place_of(index)
    copy = pltpu.make_async_copy(entering.at[0, 0], own, sem)

    @pl.when(special)
    def _():
        copy.start()
        copy.wait()

    begin(jnp.where(special, own[...], moved[...]), gain, halo, odd, state, normed, cross, inner)


def stream_body(normed, wq, wk, wv, wo, q, k, v, vq, vk, vv, vo, sems):
    copies = [
        pltpu.make_async_copy(source, target, sems.at[i])
        for i, (source, target) in enumerate(((wk, vk), (wv, vv), (wq, vq), (wo, vo)))
    ]
    for copy in copies:
        copy.start()
    rows = normed[...]
    copies[0].wait()
    k[...] = jnp.dot(rows, vk[...], preferred_element_type=F32).astype(BF)
    copies[1].wait()
    v[...] = jnp.dot(rows, vv[...], preferred_element_type=F32).astype(BF)
    copies[2].wait()
    q[...] = jnp.dot(rows, vq[...], preferred_element_type=F32).astype(BF) * BF(HEAD_DIM ** -0.5)
    copies[3].wait()


def project_body(normed, wq, wk, wv, q, k, v):
    rows = normed[...]
    q[...] = jnp.dot(rows, wq[...], preferred_element_type=F32).astype(BF) * BF(HEAD_DIM ** -0.5)
    k[...] = jnp.dot(rows, wk[...], preferred_element_type=F32).astype(BF)
    v[...] = jnp.dot(rows, wv[...], preferred_element_type=F32).astype(BF)


def attend(state, q, k, v, cross, inner, table, wk, wv, wo, attended):
    halo = jnp.concatenate([cross[...], inner[...]], axis=0)
    more_k = jnp.dot(halo, wk[...], preferred_element_type=F32).astype(BF)
    more_v = jnp.dot(halo, wv[...], preferred_element_type=F32).astype(BF)
    bias = table[...]
    nodes, width = q.shape
    bias = jnp.concatenate([bias, bias], axis=0)
    first = lax.broadcasted_iota(jnp.int32, (nodes, LANES), 1) < HEAD_DIM
    ones = jnp.ones((table.shape[1], LANES), BF)
    for i in range(width // LANES):
        at = slice(i * LANES, (i + 1) * LANES)
        pair = q[:, at]
        zero = jnp.zeros_like(pair)
        both = jnp.concatenate([jnp.where(first, pair, zero), jnp.where(first, zero, pair)], axis=0)
        keys = jnp.concatenate([k[:, at], more_k[:, at]], axis=0)
        values = jnp.concatenate([v[:, at], more_v[:, at]], axis=0)
        scores = lax.dot_general(both, keys, (((1,), (1,)), ((), ())), preferred_element_type=F32) + bias
        expo = jnp.exp(scores - jnp.max(scores, axis=1, keepdims=True)).astype(BF)
        sums = jnp.dot(expo, jnp.concatenate([values, ones], axis=1), preferred_element_type=F32)
        top = sums[:nodes, :LANES] / sums[:nodes, LANES:]
        low = sums[nodes:, :LANES] / sums[nodes:, LANES:]
        attended[:, at] = jnp.where(first, top, low).astype(BF)
    update = jnp.dot(attended[...], wo[...], preferred_element_type=F32)
    return (state[...].astype(F32) + update).astype(BF)


def middle_of(member, index):
    def body(state, q, k, v, cross, inner, table, wk, wv, wo, entering, gain, halo, token,
             new_state, normed, new_cross, new_inner, attended, own, sem):
        special, odd = place_of(index)
        copy = pltpu.make_async_copy(entering.at[1, member], own, sem)

        @pl.when(special)
        def _():
            copy.start()

        moved = attend(state, q, k, v, cross, inner, table, wk, wv, wo, attended)

        @pl.when(special)
        def _():
            copy.wait()

        begin(jnp.where(special, own[...], moved), gain, halo, odd, new_state, normed, new_cross, new_inner)

    return body


def last_body(state, q, k, v, cross, inner, table, wk, wv, wo, token, out, attended):
    out[...] = attend(state, q, k, v, cross, inner, table, wk, wv, wo, attended)


def last_out_body(state, q, k, v, cross, inner, table, wk, wv, wo, out, attended, result, sem):
    result[...] = attend(state, q, k, v, cross, inner, table, wk, wv, wo, attended)
    copy = pltpu.make_async_copy(result, out.at[0, 0], sem)
    copy.start()
    copy.wait()


def join_body(whole, arrived, out, sem):
    copy = pltpu.make_async_copy(arrived, out.at[0, 1], sem)
    copy.start()
    copy.wait()


def per_device(states, entering, norm_gain, wq, wk, wv, wo, senders, halo_rows):
    leads, places = lax.axis_size("lead"), lax.axis_size("mesh")
    members, nodes, width = states.shape[1:]
    edge = halo_rows.shape[2]
    gain, halo, senders = norm_gain[None], halo_rows[0], senders.T
    states, entering, wq, wk, wv, wo = (
        pltpu.with_memory_space_constraint(x, pltpu.HBM) for x in (states, entering, wq, wk, wv, wo)
    )
    inner_route = [(i, i ^ 1) for i in range(places)]
    partner = [min(max(((i - 1) ^ 1) + 1, 0), places - 1) if 0 < i < places - 1 else i for i in range(places)]
    cross_route = list(enumerate(partner))
    route = [(i, (i + 2) % leads) for i in range(leads)]
    block, rim = shape(nodes, width), shape(edge, width)
    weight = shape(width, width)
    begun, begun_specs = [block, block, rim, rim], [VMEM] * 4
    dma = pltpu.SemaphoreType.DMA

    def exchanged(cross, inner):
        return lax.ppermute(cross, "mesh", cross_route), lax.ppermute(inner, "mesh", inner_route)

    def project(normed):
        return call(project_body, "project", [normed, vq, vk, vv], [VMEM] * 4, [block] * 3, [VMEM] * 3)

    def middle(member, index, state, q, k, v, cross, inner, token):
        return call(
            middle_of(member, index), f"middle_{member}",
            [state, q, k, v, cross, inner, table, vk, vv, vo, entering, gain, halo, token],
            [VMEM] * 10 + [HBM, VMEM, VMEM, ANY], begun, begun_specs,
            [pltpu.VMEM((nodes, width), BF), pltpu.VMEM((nodes, width), BF), dma],
        )

    state1, normed1, cross1, inner1, table, far = call(
        functools.partial(near_first_body, leads - 1), "near_first",
        [states, entering] + [pltpu.with_memory_space_constraint(x, pltpu.HBM) for x in (gain, halo, senders)],
        [HBM] * 5,
        begun + [shape(nodes, nodes + 2 * edge, dtype=F32), block], begun_specs + [VMEM] * 2,
        [pltpu.VMEM((nodes, width), BF)] + [pltpu.VMEM(x.shape, x.dtype) for x in (gain, halo, senders)] + [dma((5,))],
    )
    far = lax.ppermute(far, "lead", route)
    cross1, inner1 = exchanged(cross1, inner1)
    q1, k1, v1, vq, vk, vv, vo = call(
        stream_body, "stream", [normed1, wq, wk, wv, wo], [VMEM] + [HBM] * 4,
        [block] * 3 + [weight] * 4, [VMEM] * 7, [dma((4,))],
    )
    state1, normed1, cross1, inner1 = middle(1, leads - 2, state1, q1, k1, v1, cross1, inner1, k1)
    cross1, inner1 = exchanged(cross1, inner1)
    q1, k1, v1 = project(normed1)
    state0, normed0, cross0, inner0 = call(
        functools.partial(far_first_body, 1), "far_first",
        [far, entering, gain, halo, k1],
        [VMEM, HBM, VMEM, VMEM, ANY], begun, begun_specs,
        [pltpu.VMEM((nodes, width), BF), dma],
    )
    token = cross0
    cross0, inner0 = exchanged(cross0, inner0)
    near = call(
        last_body, "last_1",
        [state1, q1, k1, v1, cross1, inner1, table, vk, vv, vo, token],
        [VMEM] * 10 + [ANY], block, VMEM, [pltpu.VMEM((nodes, width), BF)],
    )
    arrived = lax.ppermute(near, "lead", route)
    q0, k0, v0 = project(normed0)
    state0, normed0, cross0, inner0 = middle(0, 0, state0, q0, k0, v0, cross0, inner0, near)
    cross0, inner0 = exchanged(cross0, inner0)
    q0, k0, v0 = project(normed0)
    whole = call(
        last_out_body, "last_0",
        [state0, q0, k0, v0, cross0, inner0, table, vk, vv, vo],
        [VMEM] * 10, shape(1, members, nodes, width), HBM,
        [pltpu.VMEM((nodes, width), BF), pltpu.VMEM((nodes, width), BF), dma],
    )
    return call(
        join_body, "join", [whole, arrived], [HBM, VMEM],
        shape(1, members, nodes, width), HBM, [dma], input_output_aliases={0: 0},
    )


def solution(mesh):
    P = jax.sharding.PartitionSpec
    in_specs = (
        P("lead", None, "mesh", None),
        P(None, None, "mesh", None),
        P(),
        P(),
        P(),
        P(),
        P(),
        P("mesh", None),
        P("mesh", None, None),
    )
    return jax.shard_map(
        per_device, mesh=mesh, in_specs=in_specs, out_specs=P("lead", None, "mesh", None), check_vma=False
    )
```

time: 62.2 us -> 52.3 us (0.84)
  the two profiles are of different devices: /device:TPU:31 before, /device:TPU:1 now
where the time goes in v2:
time: 52.3 us; the launch traced here: 52.1 us
  starting transfers between devices  26.8 us (51%)
  Pallas kernels  20.4 us (39%)
  waiting for transfers between devices  4.42 us (8%)
    pallas_call x11, Pallas kernels, call(): pl.pallas_call(body, out_shape=outs, in_specs=specs, out_specs=out_specs,...  20.4 us
    ppermute x4, starting transfers between devices, exchanged(): lax.ppermute(cross, 'mesh', cross_route)  19.7 us
    ppermute x4, waiting for transfers between devices, exchanged(): lax.ppermute(cross, 'mesh', cross_route)  4.22 us
    ppermute x1, starting transfers between devices, per_device(): arrived = lax.ppermute(near, 'lead', route)  3.75 us
    ppermute x1, starting transfers between devices, per_device(): far = lax.ppermute(far, 'lead', route)  3.07 us
  transfers between devices with their start and end apart: 10, of which 2 were waited for; matrix products, arithmetic and copies ran while one was open for 0% of the time, Pallas kernels for 35%

profile of v2, /device:TPU:1, one launch (start us, length us, event | category | flops | bytes accessed | tf_op | source)
XLA Modules:
  0.0 52.1 jit_solution(12913613109610193859)
XLA Ops:
  0.0 1.5 %near_first.1 = (bf16[128,1024]{1,0:T(8,128)(2,1)S(1)}, bf16[128,1024]{1,0:T(8,128)(2,1)S(1)}, bf16[32,1024]{1,0:T(8,128)(2,1)S(1)}, bf16[32,1024]{1,0:T(8,128)(...) custom-call(bf16[1,2,128,1024]{3,2,1,0:T(8,128)(2,1)} %states.1, bf16[2,2,128,1024]{3,2,1,0:T(8,128)(2,1)} %entering.7, ...), custom_call_target="tpu_custom_call" | custom-call | flops 1000000000 | bytes 1000 | tf_op jit(solution)/shard_map/near_first/pallas_call | solution.py:25
  1.5 6.2 %collective-permute-start.1 = (bf16[32,1024]{1,0:T(8,128)(2,1)S(1)}, bf16[32,1024]{1,0:T(8,128)(2,1)S(1)}, u32[]{:S(2)}, u32[]{:S(2)}) collective-permute-start(bf16[32,1024]{1,0:T(8,128)(2,1)S(1)} %get-tuple-element.45), channel_id=1, source_target_pairs={{0,0},{1,2},{2,1},{3,4},{4,3},{5,6},{6,5},{7,8},{8,7},{9,10},{10,9... | collective-permute-start | bytes 196616 | tf_op jit(solution)/shard_map/ppermute | solution.py:221
  7.7 0.1 collective-permute-start.2
  7.8 3.1 %collective-permute-start = (bf16[128,1024]{1,0:T(8,128)(2,1)S(1)}, bf16[128,1024]{1,0:T(8,128)(2,1)S(1)}, u32[]{:S(2)}, u32[]{:S(2)}) collective-permute-start(bf16[128,1024]{1,0:T(8,128)(2,1)S(1)} %get-tuple-element.39), channel_id=1, source_target_pairs={{0,32},{16,48},{32,64},{48,80},{64,96},{80,112},{96,128},{112,144}... | collective-permute-start | bytes 786440 | tf_op jit(solution)/shard_map/ppermute | solution.py:241
  10.9 3.5 %stream.1 = (bf16[128,1024]{1,0:T(8,128)(2,1)S(1)}, bf16[128,1024]{1,0:T(8,128)(2,1)S(1)}, bf16[128,1024]{1,0:T(8,128)(2,1)S(1)}, bf16[1024,1024]{1,0:T(8,128)(2...) custom-call(bf16[128,1024]{1,0:T(8,128)(2,1)S(1)} %get-tuple-element.41.norm, ...), custom_call_target="tpu_custom_call" | custom-call | flops 1000000000 | bytes 1000 | tf_op jit(solution)/shard_map/stream/pallas_call | solution.py:25
  14.4 0.0 collective-permute-done.1.cross
  14.4 0.0 collective-permute-done.2.inner
  14.4 0.0 copy-done
  14.5 2.7 %middle_1.1 = (bf16[128,1024]{1,0:T(8,128)(2,1)S(1)}, bf16[128,1024]{1,0:T(8,128)(2,1)S(1)}, bf16[32,1024]{1,0:T(8,128)(2,1)S(1)}, bf16[32,1024]{1,0:T(8,128)(2,1)S(1)}) custom-call(bf16[128,1024]{1,0:T(8,128)(2,1)S(1)} %get-tuple-element.40.state, bf16[128,1024]{1,0:T(8,128)(2,1)S(1)} %get-tuple-element.42.q, ...), custom_call_target="tpu_custom_call" | custom-call | flops 1000000000 | bytes 1000 | tf_op jit(solution)/shard_map/middle_1/pallas_call | solution.py:25
  17.1 3.5 %collective-permute-start.5 = (bf16[32,1024]{1,0:T(8,128)(2,1)S(1)}, bf16[32,1024]{1,0:T(8,128)(2,1)S(1)}, u32[]{:S(2)}, u32[]{:S(2)}) collective-permute-start(bf16[32,1024]{1,0:T(8,128)(2,1)S(1)} %get-tuple-element.64), channel_id=1, source_target_pairs={{0,0},{1,2},{2,1},{3,4},{4,3},{5,6},{6,5},{7,8},{8,7},{9,10},{10,9... | collective-permute-start | bytes 196616 | tf_op jit(solution)/shard_map/ppermute | solution.py:221
  20.6 0.1 collective-permute-start.6
  20.7 1.0 %project.3 = (bf16[128,1024]{1,0:T(8,128)(2,1)S(1)}, bf16[128,1024]{1,0:T(8,128)(2,1)S(1)}, bf16[128,1024]{1,0:T(8,128)(2,1)S(1)}) custom-call(bf16[128,1024]{1,0:T(8,128)(2,1)S(1)} %get-tuple-element.51.normed, bf16[1024,1024]{1,0:T(8,128)(2,1)S(1)} %get-tuple-element.52.wq, bf16[1024,1024]{1,0:T(8,128)(2,1)S(1)} %get-tuple-element.48.wk, ...), custom_call_target="tpu_custom_call" | custom-call | flops 1000000000 | bytes 1000 | tf_op jit(solution)/shard_map/project/pallas_call | solution.py:25
  21.7 0.2 collective-permute-done.moved
  21.9 0.5 far_first.1
  22.4 5.7 %collective-permute-start.3 = (bf16[32,1024]{1,0:T(8,128)(2,1)S(1)}, bf16[32,1024]{1,0:T(8,128)(2,1)S(1)}, u32[]{:S(2)}, u32[]{:S(2)}) collective-permute-start(bf16[32,1024]{1,0:T(8,128)(2,1)S(1)} %get-tuple-element.59.token), channel_id=1, source_target_pairs={{0,0},{1,2},{2,1},{3,4},{4,3},{5,6},{6,5},{7,8},{8,7},{9,10},{10,9... | collective-permute-start | bytes 196616 | tf_op jit(solution)/shard_map/ppermute | solution.py:221
  28.1 0.1 collective-permute-start.4
  28.2 0.0 collective-permute-done.5.cross
  28.2 0.0 collective-permute-done.6.inner
  28.3 2.2 %last_1.1.token = bf16[128,1024]{1,0:T(8,128)(2,1)S(1)} custom-call(bf16[128,1024]{1,0:T(8,128)(2,1)S(1)} %get-tuple-element.61.state, bf16[128,1024]{1,0:T(8,128)(2,1)S(1)} %get-tuple-element.62.q, bf16[128,1024]{1,0:T(8,128)(2,1)S(1)} %get-tuple-element.53.token.k, bf16[128,1024]{1,0:T(8,128)(2,1)S(1)} %get-tuple-element.63.v, ...), custom_call_target="tpu_custom_call" | custom-call | flops 1000000000 | bytes 1000 | tf_op jit(solution)/shard_map/last_1/pallas_call | solution.py:25
  30.5 3.7 %collective-permute-start.9 = (bf16[128,1024]{1,0:T(8,128)(2,1)S(1)}, bf16[128,1024]{1,0:T(8,128)(2,1)S(1)}, u32[]{:S(2)}, u32[]{:S(2)}) collective-permute-start(bf16[128,1024]{1,0:T(8,128)(2,1)S(1)} %last_1.1.token), channel_id=1, source_target_pairs={{0,32},{16,48},{32,64},{48,80},{64,96},{80,112},{96,128},{112,144}... | collective-permute-start | bytes 786440 | tf_op jit(solution)/shard_map/ppermute | solution.py:263
  34.2 1.0 %project.4 = (bf16[128,1024]{1,0:T(8,128)(2,1)S(1)}, bf16[128,1024]{1,0:T(8,128)(2,1)S(1)}, bf16[128,1024]{1,0:T(8,128)(2,1)S(1)}) custom-call(bf16[128,1024]{1,0:T(8,128)(2,1)S(1)} %get-tuple-element.55.normed, bf16[1024,1024]{1,0:T(8,128)(2,1)S(1)} %get-tuple-element.52.wq, bf16[1024,1024]{1,0:T(8,128)(2,1)S(1)} %get-tuple-element.48.wk, ...), custom_call_target="tpu_custom_call" | custom-call | flops 1000000000 | bytes 1000 | tf_op jit(solution)/shard_map/project/pallas_call | solution.py:25
  35.2 0.0 collective-permute-done.3.cross
  35.2 0.0 collective-permute-done.4.inner
  35.2 3.5 %middle_0.1 = (bf16[128,1024]{1,0:T(8,128)(2,1)S(1)}, bf16[128,1024]{1,0:T(8,128)(2,1)S(1)}, bf16[32,1024]{1,0:T(8,128)(2,1)S(1)}, bf16[32,1024]{1,0:T(8,128)(2,1)S(1)}) custom-call(bf16[128,1024]{1,0:T(8,128)(2,1)S(1)} %get-tuple-element.54.state, bf16[128,1024]{1,0:T(8,128)(2,1)S(1)} %get-tuple-element.56.q, bf16[128,1024]{1,0:T(8,128)(2,1)S(1)} %get-tuple-element.57.k, ...), custom_call_target="tpu_custom_call" | custom-call | flops 1000000000 | bytes 1000 | tf_op jit(solution)/shard_map/middle_0/pallas_call | solution.py:25
  38.7 4.2 %collective-permute-start.7 = (bf16[32,1024]{1,0:T(8,128)(2,1)S(1)}, bf16[32,1024]{1,0:T(8,128)(2,1)S(1)}, u32[]{:S(2)}, u32[]{:S(2)}) collective-permute-start(bf16[32,1024]{1,0:T(8,128)(2,1)S(1)} %get-tuple-element.71), channel_id=1, source_target_pairs={{0,0},{1,2},{2,1},{3,4},{4,3},{5,6},{6,5},{7,8},{8,7},{9,10},{10,9... | collective-permute-start | bytes 196616 | tf_op jit(solution)/shard_map/ppermute | solution.py:221
  42.9 0.1 collective-permute-start.8
  43.0 1.0 %project.5 = (bf16[128,1024]{1,0:T(8,128)(2,1)S(1)}, bf16[128,1024]{1,0:T(8,128)(2,1)S(1)}, bf16[128,1024]{1,0:T(8,128)(2,1)S(1)}) custom-call(bf16[128,1024]{1,0:T(8,128)(2,1)S(1)} %get-tuple-element.67.normed, bf16[1024,1024]{1,0:T(8,128)(2,1)S(1)} %get-tuple-element.52.wq, bf16[1024,1024]{1,0:T(8,128)(2,1)S(1)} %get-tuple-element.48.wk, ...), custom_call_target="tpu_custom_call" | custom-call | flops 1000000000 | bytes 1000 | tf_op jit(solution)/shard_map/project/pallas_call | solution.py:25
  44.0 4.2 %collective-permute-done.7.cross = bf16[32,1024]{1,0:T(8,128)(2,1)S(1)} collective-permute-done((bf16[32,1024]{1,0:T(8,128)(2,1)S(1)}, bf16[32,1024]{1,0:T(8,128)(2,1)S(1)}, u32[]{:S(2)}, u32[]{:S(2)}) %collective-permute-start.7) | collective-permute-done | bytes 65568 | tf_op jit(solution)/shard_map/ppermute | solution.py:221
  48.2 0.0 collective-permute-done.8.inner
  48.2 2.9 %last_0.1.whole = bf16[1,2,128,1024]{3,2,1,0:T(8,128)(2,1)} custom-call(bf16[128,1024]{1,0:T(8,128)(2,1)S(1)} %get-tuple-element.66.state, bf16[128,1024]{1,0:T(8,128)(2,1)S(1)} %get-tuple-element.68.q, bf16[128,1024]{1,0:T(8,128)(2,1)S(1)} %get-tuple-element.69.k, bf16[128,1024]{1,0:T(8,128)(2,1)S(1)} %get-tuple-element.70.v, ...), custom_call_target="tpu_custom_call" | custom-call | flops 1000000000 | bytes 1000 | tf_op jit(solution)/shard_map/last_0/pallas_call | solution.py:25
  51.2 0.0 collective-permute-done.9.arrived
  51.2 0.7 %join.1 = bf16[1,2,128,1024]{3,2,1,0:T(8,128)(2,1)} custom-call(bf16[1,2,128,1024]{3,2,1,0:T(8,128)(2,1)} %last_0.1.whole, bf16[128,1024]{1,0:T(8,128)(2,1)S(1)} %collective-permute-done.9.arrived), custom_call_target="tpu_custom_call", output_to_operand_aliasing={{}: (0, {})} | custom-call | flops 1000000000 | bytes 1000 | tf_op jit(solution)/shard_map/join/pallas_call | solution.py:25
  (3 shorter events, 0.0 us)
Async XLA Ops:
  1.5 12.9 %collective-permute-start.1 = (bf16[32,1024]{1,0:T(8,128)(2,1)S(1)}, bf16[32,1024]{1,0:T(8,128)(2,1)S(1)}, u32[]{:S(2)}, u32[]{:S(2)}) collective-permute-start(bf16[32,1024]{1,0:T(8,128)(2,1)S(1)} %get-tuple-element.45), channel_id=1, source_target_pairs={{0,0},{1,2},{2,1},{3,4},{4,3},{5,6},{6,5},{7,8},{8,7},{9,10},{10,9... | collective-permute-start | bytes 196616 | tf_op jit(solution)/shard_map/ppermute | solution.py:221
  7.7 6.7 %collective-permute-start.2 = (bf16[32,1024]{1,0:T(8,128)(2,1)S(1)}, bf16[32,1024]{1,0:T(8,128)(2,1)S(1)}, u32[]{:S(2)}, u32[]{:S(2)}) collective-permute-start(bf16[32,1024]{1,0:T(8,128)(2,1)S(1)} %get-tuple-element.46), channel_id=1, source_target_pairs={{0,1},{1,0},{2,3},{3,2},{4,5},{5,4},{6,7},{7,6},{8,9},{9,8},{10,11... | collective-permute-start | bytes 196616 | tf_op jit(solution)/shard_map/ppermute | solution.py:221
  7.8 14.1 %collective-permute-start = (bf16[128,1024]{1,0:T(8,128)(2,1)S(1)}, bf16[128,1024]{1,0:T(8,128)(2,1)S(1)}, u32[]{:S(2)}, u32[]{:S(2)}) collective-permute-start(bf16[128,1024]{1,0:T(8,128)(2,1)S(1)} %get-tuple-element.39), channel_id=1, source_target_pairs={{0,32},{16,48},{32,64},{48,80},{64,96},{80,112},{96,128},{112,144}... | collective-permute-start | bytes 786440 | tf_op jit(solution)/shard_map/ppermute | solution.py:241
  10.9 3.6 %copy-start = (f32[1024]{0:T(1024)S(1)}, f32[1024]{0:T(1024)}, u32[]{:S(2)}) copy-start(f32[1024]{0:T(1024)} %param.11) | copy-start | bytes 12292
  10.9 3.6 %copy-start.1 = (s32[1,2,32]{2,1,0:T(2,128)S(1)}, s32[1,2,32]{2,1,0:T(2,128)}, u32[]{:S(2)}) copy-start(s32[1,2,32]{2,1,0:T(2,128)} %param.17) | copy-start | bytes 772
  17.1 11.1 %collective-permute-start.5 = (bf16[32,1024]{1,0:T(8,128)(2,1)S(1)}, bf16[32,1024]{1,0:T(8,128)(2,1)S(1)}, u32[]{:S(2)}, u32[]{:S(2)}) collective-permute-start(bf16[32,1024]{1,0:T(8,128)(2,1)S(1)} %get-tuple-element.64), channel_id=1, source_target_pairs={{0,0},{1,2},{2,1},{3,4},{4,3},{5,6},{6,5},{7,8},{8,7},{9,10},{10,9... | collective-permute-start | bytes 196616 | tf_op jit(solution)/shard_map/ppermute | solution.py:221
  20.6 7.6 %collective-permute-start.6 = (bf16[32,1024]{1,0:T(8,128)(2,1)S(1)}, bf16[32,1024]{1,0:T(8,128)(2,1)S(1)}, u32[]{:S(2)}, u32[]{:S(2)}) collective-permute-start(bf16[32,1024]{1,0:T(8,128)(2,1)S(1)} %get-tuple-element.65), channel_id=1, source_target_pairs={{0,1},{1,0},{2,3},{3,2},{4,5},{5,4},{6,7},{7,6},{8,9},{9,8},{10,11... | collective-permute-start | bytes 196616 | tf_op jit(solution)/shard_map/ppermute | solution.py:221
  22.4 12.8 %collective-permute-start.3 = (bf16[32,1024]{1,0:T(8,128)(2,1)S(1)}, bf16[32,1024]{1,0:T(8,128)(2,1)S(1)}, u32[]{:S(2)}, u32[]{:S(2)}) collective-permute-start(bf16[32,1024]{1,0:T(8,128)(2,1)S(1)} %get-tuple-element.59.token), channel_id=1, source_target_pairs={{0,0},{1,2},{2,1},{3,4},{4,3},{5,6},{6,5},{7,8},{8,7},{9,10},{10,9... | collective-permute-start | bytes 196616 | tf_op jit(solution)/shard_map/ppermute | solution.py:221
  28.1 7.1 %collective-permute-start.4 = (bf16[32,1024]{1,0:T(8,128)(2,1)S(1)}, bf16[32,1024]{1,0:T(8,128)(2,1)S(1)}, u32[]{:S(2)}, u32[]{:S(2)}) collective-permute-start(bf16[32,1024]{1,0:T(8,128)(2,1)S(1)} %get-tuple-element.60), channel_id=1, source_target_pairs={{0,1},{1,0},{2,3},{3,2},{4,5},{5,4},{6,7},{7,6},{8,9},{9,8},{10,11... | collective-permute-start | bytes 196616 | tf_op jit(solution)/shard_map/ppermute | solution.py:221
  30.5 20.7 %collective-permute-start.9 = (bf16[128,1024]{1,0:T(8,128)(2,1)S(1)}, bf16[128,1024]{1,0:T(8,128)(2,1)S(1)}, u32[]{:S(2)}, u32[]{:S(2)}) collective-permute-start(bf16[128,1024]{1,0:T(8,128)(2,1)S(1)} %last_1.1.token), channel_id=1, source_target_pairs={{0,32},{16,48},{32,64},{48,80},{64,96},{80,112},{96,128},{112,144}... | collective-permute-start | bytes 786440 | tf_op jit(solution)/shard_map/ppermute | solution.py:263
  38.7 9.5 %collective-permute-start.7 = (bf16[32,1024]{1,0:T(8,128)(2,1)S(1)}, bf16[32,1024]{1,0:T(8,128)(2,1)S(1)}, u32[]{:S(2)}, u32[]{:S(2)}) collective-permute-start(bf16[32,1024]{1,0:T(8,128)(2,1)S(1)} %get-tuple-element.71), channel_id=1, source_target_pairs={{0,0},{1,2},{2,1},{3,4},{4,3},{5,6},{6,5},{7,8},{8,7},{9,10},{10,9... | collective-permute-start | bytes 196616 | tf_op jit(solution)/shard_map/ppermute | solution.py:221
  42.9 5.3 %collective-permute-start.8 = (bf16[32,1024]{1,0:T(8,128)(2,1)S(1)}, bf16[32,1024]{1,0:T(8,128)(2,1)S(1)}, u32[]{:S(2)}, u32[]{:S(2)}) collective-permute-start(bf16[32,1024]{1,0:T(8,128)(2,1)S(1)} %get-tuple-element.72), channel_id=1, source_target_pairs={{0,1},{1,0},{2,3},{3,2},{4,5},{5,4},{6,7},{7,6},{8,9},{9,8},{10,11... | collective-permute-start | bytes 196616 | tf_op jit(solution)/shard_map/ppermute | solution.py:221

commit v3 on v2

--- a/solution.py
+++ b/solution.py
@@ -72,8 +72,14 @@
     return lax.axis_index("lead") == index, lax.rem(lax.axis_index("mesh"), 2)
 
 
-def near_first_body(index, states, entering, all_gain, all_halo, all_senders,
-                    state, normed, cross, inner, table, far, own, gain, halo, senders, sems):
+def fetch_body(states, far, sem):
+    copy = pltpu.make_async_copy(states.at[0, 0], far, sem)
+    copy.start()
+    copy.wait()
+
+
+def near_first_body(index, states, entering, all_gain, all_halo, all_senders, token,
+                    state, normed, cross, inner, table, own, gain, halo, senders, sems):
     special, odd = place_of(index)
     small = [
         pltpu.make_async_copy(source, target, sems.at[2 + i])
@@ -90,14 +96,11 @@
     def _():
         pltpu.make_async_copy(states.at[0, 1], own, sems.at[1]).start()
 
-    to_far = pltpu.make_async_copy(states.at[0, 0], far, sems.at[0])
-    to_far.start()
     for copy in small:
         copy.wait()
     bias_table(senders, odd, table)
     pltpu.make_async_copy(states.at[0, 1], own, sems.at[1]).wait()
     begin(own[...], gain, halo, odd, state, normed, cross, inner)
-    to_far.wait()
 
 
 def far_first_body(index, moved, entering, gain, halo, token, state, normed, cross, inner, own, sem):
@@ -136,7 +139,7 @@
     v[...] = jnp.dot(rows, wv[...], preferred_element_type=F32).astype(BF)
 
 
-def attend(state, q, k, v, cross, inner, table, wk, wv, wo, attended):
+def attention(q, k, v, cross, inner, table, wk, wv, attended):
     halo = jnp.concatenate([cross[...], inner[...]], axis=0)
     more_k = jnp.dot(halo, wk[...], preferred_element_type=F32).astype(BF)
     more_v = jnp.dot(halo, wv[...], preferred_element_type=F32).astype(BF)
@@ -158,8 +161,16 @@
         top = sums[:nodes, :LANES] / sums[:nodes, LANES:]
         low = sums[nodes:, :LANES] / sums[nodes:, LANES:]
         attended[:, at] = jnp.where(first, top, low).astype(BF)
+
+
+def updated(state, attended, wo):
     update = jnp.dot(attended[...], wo[...], preferred_element_type=F32)
     return (state[...].astype(F32) + update).astype(BF)
+
+
+def attend(state, q, k, v, cross, inner, table, wk, wv, wo, attended):
+    attention(q, k, v, cross, inner, table, wk, wv, attended)
+    return updated(state, attended, wo)
 
 
 def middle_of(member, index):
@@ -187,17 +198,18 @@
     out[...] = attend(state, q, k, v, cross, inner, table, wk, wv, wo, attended)
 
 
-def last_out_body(state, q, k, v, cross, inner, table, wk, wv, wo, out, attended, result, sem):
-    result[...] = attend(state, q, k, v, cross, inner, table, wk, wv, wo, attended)
-    copy = pltpu.make_async_copy(result, out.at[0, 0], sem)
-    copy.start()
-    copy.wait()
-
-
-def join_body(whole, arrived, out, sem):
-    copy = pltpu.make_async_copy(arrived, out.at[0, 1], sem)
-    copy.start()
-    copy.wait()
+def last_0_body(q, k, v, cross, inner, table, wk, wv, attended):
+    attention(q, k, v, cross, inner, table, wk, wv, attended)
+
+
+def finish_body(state, attended, wo, arrived, out, result, sems):
+    there = pltpu.make_async_copy(arrived, out.at[0, 1], sems.at[0])
+    there.start()
+    result[...] = updated(state, attended, wo)
+    here = pltpu.make_async_copy(result, out.at[0, 0], sems.at[1])
+    here.start()
+    there.wait()
+    here.wait()
 
 
 def per_device(states, entering, norm_gain, wq, wk, wv, wo, senders, halo_rows):
@@ -209,8 +221,7 @@
         pltpu.with_memory_space_constraint(x, pltpu.HBM) for x in (states, entering, wq, wk, wv, wo)
     )
     inner_route = [(i, i ^ 1) for i in range(places)]
-    partner = [min(max(((i - 1) ^ 1) + 1, 0), places - 1) if 0 < i < places - 1 else i for i in range(places)]
-    cross_route = list(enumerate(partner))
+    cross_route = [(i, (((i - 1) ^ 1) + 1) % places) for i in range(places)]
     route = [(i, (i + 2) % leads) for i in range(leads)]
     block, rim = shape(nodes, width), shape(edge, width)
     weight = shape(width, width)
@@ -231,14 +242,16 @@
             [pltpu.VMEM((nodes, width), BF), pltpu.VMEM((nodes, width), BF), dma],
         )
 
-    state1, normed1, cross1, inner1, table, far = call(
+    far = call(fetch_body, "fetch", [states], [HBM], block, VMEM, [dma])
+    token = far
+    far = lax.ppermute(far, "lead", route)
+    state1, normed1, cross1, inner1, table = call(
         functools.partial(near_first_body, leads - 1), "near_first",
-        [states, entering] + [pltpu.with_memory_space_constraint(x, pltpu.HBM) for x in (gain, halo, senders)],
-        [HBM] * 5,
-        begun + [shape(nodes, nodes + 2 * edge, dtype=F32), block], begun_specs + [VMEM] * 2,
+        [states, entering] + [pltpu.with_memory_space_constraint(x, pltpu.HBM) for x in (gain, halo, senders)] + [token],
+        [HBM] * 5 + [ANY],
+        begun + [shape(nodes, nodes + 2 * edge, dtype=F32)], begun_specs + [VMEM],
         [pltpu.VMEM((nodes, width), BF)] + [pltpu.VMEM(x.shape, x.dtype) for x in (gain, halo, senders)] + [dma((5,))],
     )
-    far = lax.ppermute(far, "lead", route)
     cross1, inner1 = exchanged(cross1, inner1)
     q1, k1, v1, vq, vk, vv, vo = call(
         stream_body, "stream", [normed1, wq, wk, wv, wo], [VMEM] + [HBM] * 4,
@@ -265,15 +278,12 @@
     state0, normed0, cross0, inner0 = middle(0, 0, state0, q0, k0, v0, cross0, inner0, near)
     cross0, inner0 = exchanged(cross0, inner0)
     q0, k0, v0 = project(normed0)
-    whole = call(
-        last_out_body, "last_0",
-        [state0, q0, k0, v0, cross0, inner0, table, vk, vv, vo],
-        [VMEM] * 10, shape(1, members, nodes, width), HBM,
-        [pltpu.VMEM((nodes, width), BF), pltpu.VMEM((nodes, width), BF), dma],
+    attended = call(
+        last_0_body, "last_0", [q0, k0, v0, cross0, inner0, table, vk, vv], [VMEM] * 8, block, VMEM,
     )
     return call(
-        join_body, "join", [whole, arrived], [HBM, VMEM],
-        shape(1, members, nodes, width), HBM, [dma], input_output_aliases={0: 0},
+        finish_body, "finish", [state0, attended, vo, arrived], [VMEM] * 4,
+        shape(1, members, nodes, width), HBM, [pltpu.VMEM((nodes, width), BF), dma((2,))],
     )
 
 

time: 52.3 us -> 46.7 us (0.89)
  the two profiles are of different devices: /device:TPU:1 before, /device:TPU:33 now
where the time goes in v3:
time: 46.7 us; the launch traced here: 46.5 us
  starting transfers between devices  21 us (45%)
  Pallas kernels  20.9 us (45%)
  waiting for transfers between devices  4.28 us (9%)
    pallas_call x12, Pallas kernels, call(): pl.pallas_call(body, out_shape=outs, in_specs=specs, out_specs=out_specs,...  20.9 us
    ppermute x4, starting transfers between devices, exchanged(): lax.ppermute(inner, 'mesh', inner_route)  9.78 us
    ppermute x4, starting transfers between devices, exchanged(): lax.ppermute(cross, 'mesh', cross_route)  6.04 us
    ppermute x1, waiting for transfers between devices, per_device(): arrived = lax.ppermute(near, 'lead', route)  3.87 us
    ppermute x1, starting transfers between devices, per_device(): far = lax.ppermute(far, 'lead', route)  3.07 us
    ppermute x1, starting transfers between devices, per_device(): arrived = lax.ppermute(near, 'lead', route)  2.1 us
  transfers between devices with their start and end apart: 10, of which 2 were waited for; matrix products, arithmetic and copies ran while one was open for 0% of the time, Pallas kernels for 40%

profile of v3, /device:TPU:33, one launch (start us, length us, event | category | flops | bytes accessed | tf_op | source)
XLA Modules:
  0.0 46.5 jit_solution(6868859637479139580)
XLA Ops:
  0.0 1.0 %fetch.1.token = bf16[128,1024]{1,0:T(8,128)(2,1)S(1)} custom-call(bf16[1,2,128,1024]{3,2,1,0:T(8,128)(2,1)} %states.3), custom_call_target="tpu_custom_call" | custom-call | flops 1000000000 | bytes 1000 | tf_op jit(solution)/shard_map/fetch/pallas_call | solution.py:25
  1.0 3.1 %collective-permute-start = (bf16[128,1024]{1,0:T(8,128)(2,1)S(1)}, bf16[128,1024]{1,0:T(8,128)(2,1)S(1)}, u32[]{:S(2)}, u32[]{:S(2)}) collective-permute-start(bf16[128,1024]{1,0:T(8,128)(2,1)S(1)} %fetch.1.token), channel_id=1, source_target_pairs={{0,32},{16,48},{32,64},{48,80},{64,96},{80,112},{96,128},{112,144}... | collective-permute-start | bytes 786440 | tf_op jit(solution)/shard_map/ppermute | solution.py:247
  4.0 1.5 %near_first.1 = (bf16[128,1024]{1,0:T(8,128)(2,1)S(1)}, bf16[128,1024]{1,0:T(8,128)(2,1)S(1)}, bf16[32,1024]{1,0:T(8,128)(2,1)S(1)}, bf16[32,1024]{1,0:T(8,128)(2,1)S(1)}, f32[128,192]{1,0:T(8,128)S(1)}) custom-call(bf16[1,2,128,1024]{3,2,1,0:T(8,128)(2,1)} %states.3, bf16[2,2,128,1024]{3,2,1,0:T(8,128)(2,1)} %entering.7, f32[1,1024]{1,0:T(1,128)} %bitcast.3, ...), custom_call_target="tpu_custom_call" | custom-call | flops 1000000000 | bytes 1000 | tf_op jit(solution)/shard_map/near_first/pallas_call | solution.py:25
  5.5 3.8 %collective-permute-start.1 = (bf16[32,1024]{1,0:T(8,128)(2,1)S(1)}, bf16[32,1024]{1,0:T(8,128)(2,1)S(1)}, u32[]{:S(2)}, u32[]{:S(2)}) collective-permute-start(bf16[32,1024]{1,0:T(8,128)(2,1)S(1)} %get-tuple-element.43), channel_id=1, source_target_pairs={{0,15},{1,2},{2,1},{3,4},{4,3},{5,6},{6,5},{7,8},{8,7},{9,10},{10,... | collective-permute-start | bytes 196616 | tf_op jit(solution)/shard_map/ppermute | solution.py:232
  9.4 1.7 %collective-permute-start.2 = (bf16[32,1024]{1,0:T(8,128)(2,1)S(1)}, bf16[32,1024]{1,0:T(8,128)(2,1)S(1)}, u32[]{:S(2)}, u32[]{:S(2)}) collective-permute-start(bf16[32,1024]{1,0:T(8,128)(2,1)S(1)} %get-tuple-element.44), channel_id=1, source_target_pairs={{0,1},{1,0},{2,3},{3,2},{4,5},{5,4},{6,7},{7,6},{8,9},{9,8},{10,11... | collective-permute-start | bytes 196616 | tf_op jit(solution)/shard_map/ppermute | solution.py:232
  11.1 3.5 %stream.1 = (bf16[128,1024]{1,0:T(8,128)(2,1)S(1)}, bf16[128,1024]{1,0:T(8,128)(2,1)S(1)}, bf16[128,1024]{1,0:T(8,128)(2,1)S(1)}, bf16[1024,1024]{1,0:T(8,128)(2...) custom-call(bf16[128,1024]{1,0:T(8,128)(2,1)S(1)} %get-tuple-element.39.norm, ...), custom_call_target="tpu_custom_call" | custom-call | flops 1000000000 | bytes 1000 | tf_op jit(solution)/shard_map/stream/pallas_call | solution.py:25
  14.6 0.0 collective-permute-done.1.cross
  14.7 0.0 collective-permute-done.2.inner
  14.7 2.7 %middle_1.1 = (bf16[128,1024]{1,0:T(8,128)(2,1)S(1)}, bf16[128,1024]{1,0:T(8,128)(2,1)S(1)}, bf16[32,1024]{1,0:T(8,128)(2,1)S(1)}, bf16[32,1024]{1,0:T(8,128)(2,1)S(1)}) custom-call(bf16[128,1024]{1,0:T(8,128)(2,1)S(1)} %get-tuple-element.38.state, bf16[128,1024]{1,0:T(8,128)(2,1)S(1)} %get-tuple-element.40.q, ...), custom_call_target="tpu_custom_call" | custom-call | flops 1000000000 | bytes 1000 | tf_op jit(solution)/shard_map/middle_1/pallas_call | solution.py:25
  17.4 0.1 collective-permute-start.5
  17.5 4.1 %collective-permute-start.6 = (bf16[32,1024]{1,0:T(8,128)(2,1)S(1)}, bf16[32,1024]{1,0:T(8,128)(2,1)S(1)}, u32[]{:S(2)}, u32[]{:S(2)}) collective-permute-start(bf16[32,1024]{1,0:T(8,128)(2,1)S(1)} %get-tuple-element.63), channel_id=1, source_target_pairs={{0,1},{1,0},{2,3},{3,2},{4,5},{5,4},{6,7},{7,6},{8,9},{9,8},{10,11... | collective-permute-start | bytes 196616 | tf_op jit(solution)/shard_map/ppermute | solution.py:232
  21.5 1.0 %project.3 = (bf16[128,1024]{1,0:T(8,128)(2,1)S(1)}, bf16[128,1024]{1,0:T(8,128)(2,1)S(1)}, bf16[128,1024]{1,0:T(8,128)(2,1)S(1)}) custom-call(bf16[128,1024]{1,0:T(8,128)(2,1)S(1)} %get-tuple-element.49.normed, bf16[1024,1024]{1,0:T(8,128)(2,1)S(1)} %get-tuple-element.50.wq, bf16[1024,1024]{1,0:T(8,128)(2,1)S(1)} %get-tuple-element.46.wk, ...), custom_call_target="tpu_custom_call" | custom-call | flops 1000000000 | bytes 1000 | tf_op jit(solution)/shard_map/project/pallas_call | solution.py:25
  22.5 0.0 collective-permute-done.moved
  22.5 1.4 %far_first.1 = (bf16[128,1024]{1,0:T(8,128)(2,1)S(1)}, bf16[128,1024]{1,0:T(8,128)(2,1)S(1)}, bf16[32,1024]{1,0:T(8,128)(2,1)S(1)}, bf16[32,1024]{1,0:T(8,128)(2,1)S(1)}) custom-call(bf16[128,1024]{1,0:T(8,128)(2,1)S(1)} %collective-permute-done.moved, bf16[2,2,128,1024]{3,2,1,0:T(8,128)(2,1)} %entering.7, f32[1,1024]{1,0:T(1,128)S(1)} %bitcast.5, ...), custom_call_target="tpu_custom_call" | custom-call | flops 1000000000 | bytes 1000 | tf_op jit(solution)/shard_map/far_first/pallas_call | solution.py:25
  24.0 0.1 collective-permute-start.3
  24.1 1.8 %collective-permute-start.4 = (bf16[32,1024]{1,0:T(8,128)(2,1)S(1)}, bf16[32,1024]{1,0:T(8,128)(2,1)S(1)}, u32[]{:S(2)}, u32[]{:S(2)}) collective-permute-start(bf16[32,1024]{1,0:T(8,128)(2,1)S(1)} %get-tuple-element.58), channel_id=1, source_target_pairs={{0,1},{1,0},{2,3},{3,2},{4,5},{5,4},{6,7},{7,6},{8,9},{9,8},{10,11... | collective-permute-start | bytes 196616 | tf_op jit(solution)/shard_map/ppermute | solution.py:232
  25.8 0.0 collective-permute-done.5.cross
  25.8 0.0 collective-permute-done.6.inner
  25.8 2.2 %last_1.1.token = bf16[128,1024]{1,0:T(8,128)(2,1)S(1)} custom-call(bf16[128,1024]{1,0:T(8,128)(2,1)S(1)} %get-tuple-element.59.state, bf16[128,1024]{1,0:T(8,128)(2,1)S(1)} %get-tuple-element.60.q, bf16[128,1024]{1,0:T(8,128)(2,1)S(1)} %get-tuple-element.51.token.k, bf16[128,1024]{1,0:T(8,128)(2,1)S(1)} %get-tuple-element.61.v, ...), custom_call_target="tpu_custom_call" | custom-call | flops 1000000000 | bytes 1000 | tf_op jit(solution)/shard_map/last_1/pallas_call | solution.py:25
  28.0 2.1 %collective-permute-start.9 = (bf16[128,1024]{1,0:T(8,128)(2,1)S(1)}, bf16[128,1024]{1,0:T(8,128)(2,1)S(1)}, u32[]{:S(2)}, u32[]{:S(2)}) collective-permute-start(bf16[128,1024]{1,0:T(8,128)(2,1)S(1)} %last_1.1.token), channel_id=1, source_target_pairs={{0,32},{16,48},{32,64},{48,80},{64,96},{80,112},{96,128},{112,144}... | collective-permute-start | bytes 786440 | tf_op jit(solution)/shard_map/ppermute | solution.py:276
  30.1 1.0 %project.4 = (bf16[128,1024]{1,0:T(8,128)(2,1)S(1)}, bf16[128,1024]{1,0:T(8,128)(2,1)S(1)}, bf16[128,1024]{1,0:T(8,128)(2,1)S(1)}) custom-call(bf16[128,1024]{1,0:T(8,128)(2,1)S(1)} %get-tuple-element.53.normed, bf16[1024,1024]{1,0:T(8,128)(2,1)S(1)} %get-tuple-element.50.wq, bf16[1024,1024]{1,0:T(8,128)(2,1)S(1)} %get-tuple-element.46.wk, ...), custom_call_target="tpu_custom_call" | custom-call | flops 1000000000 | bytes 1000 | tf_op jit(solution)/shard_map/project/pallas_call | solution.py:25
  31.1 0.0 collective-permute-done.3.cross
  31.2 0.0 collective-permute-done.4.inner
  31.2 2.7 %middle_0.1 = (bf16[128,1024]{1,0:T(8,128)(2,1)S(1)}, bf16[128,1024]{1,0:T(8,128)(2,1)S(1)}, bf16[32,1024]{1,0:T(8,128)(2,1)S(1)}, bf16[32,1024]{1,0:T(8,128)(2,1)S(1)}) custom-call(bf16[128,1024]{1,0:T(8,128)(2,1)S(1)} %get-tuple-element.52.state, bf16[128,1024]{1,0:T(8,128)(2,1)S(1)} %get-tuple-element.54.q, bf16[128,1024]{1,0:T(8,128)(2,1)S(1)} %get-tuple-element.55.k, ...), custom_call_target="tpu_custom_call" | custom-call | flops 1000000000 | bytes 1000 | tf_op jit(solution)/shard_map/middle_0/pallas_call | solution.py:25
  33.8 2.0 %collective-permute-start.7 = (bf16[32,1024]{1,0:T(8,128)(2,1)S(1)}, bf16[32,1024]{1,0:T(8,128)(2,1)S(1)}, u32[]{:S(2)}, u32[]{:S(2)}) collective-permute-start(bf16[32,1024]{1,0:T(8,128)(2,1)S(1)} %get-tuple-element.69), channel_id=1, source_target_pairs={{0,15},{1,2},{2,1},{3,4},{4,3},{5,6},{6,5},{7,8},{8,7},{9,10},{10,... | collective-permute-start | bytes 196616 | tf_op jit(solution)/shard_map/ppermute | solution.py:232
  35.8 2.2 %collective-permute-start.8 = (bf16[32,1024]{1,0:T(8,128)(2,1)S(1)}, bf16[32,1024]{1,0:T(8,128)(2,1)S(1)}, u32[]{:S(2)}, u32[]{:S(2)}) collective-permute-start(bf16[32,1024]{1,0:T(8,128)(2,1)S(1)} %get-tuple-element.70), channel_id=1, source_target_pairs={{0,1},{1,0},{2,3},{3,2},{4,5},{5,4},{6,7},{7,6},{8,9},{9,8},{10,11... | collective-permute-start | bytes 196616 | tf_op jit(solution)/shard_map/ppermute | solution.py:232
  38.0 1.0 %project.5 = (bf16[128,1024]{1,0:T(8,128)(2,1)S(1)}, bf16[128,1024]{1,0:T(8,128)(2,1)S(1)}, bf16[128,1024]{1,0:T(8,128)(2,1)S(1)}) custom-call(bf16[128,1024]{1,0:T(8,128)(2,1)S(1)} %get-tuple-element.65.normed, bf16[1024,1024]{1,0:T(8,128)(2,1)S(1)} %get-tuple-element.50.wq, bf16[1024,1024]{1,0:T(8,128)(2,1)S(1)} %get-tuple-element.46.wk, ...), custom_call_target="tpu_custom_call" | custom-call | flops 1000000000 | bytes 1000 | tf_op jit(solution)/shard_map/project/pallas_call | solution.py:25
  39.0 0.4 collective-permute-done.7.cross
  39.4 0.0 collective-permute-done.8.inner
  39.4 1.9 %last_0.1.attended = bf16[128,1024]{1,0:T(8,128)(2,1)S(1)} custom-call(bf16[128,1024]{1,0:T(8,128)(2,1)S(1)} %get-tuple-element.66.q, bf16[128,1024]{1,0:T(8,128)(2,1)S(1)} %get-tuple-element.67.k, bf16[128,1024]{1,0:T(8,128)(2,1)S(1)} %get-tuple-element.68.v, bf16[32,1024]{1,0:T(8,128)(2,1)S(1)} %collective-permute-done.7.cross, ...), custom_call_target="tpu_custom_call" | custom-call | flops 1000000000 | bytes 1000 | tf_op jit(solution)/shard_map/last_0/pallas_call | solution.py:25
  41.3 3.9 %collective-permute-done.9.arrived = bf16[128,1024]{1,0:T(8,128)(2,1)S(1)} collective-permute-done((bf16[128,1024]{1,0:T(8,128)(2,1)S(1)}, bf16[128,1024]{1,0:T(8,128)(2,1)S(1)}, u32[]{:S(2)}, u32[]{:S(2)}) %collective-permute-start.9) | collective-permute-done | bytes 262176 | tf_op jit(solution)/shard_map/ppermute | solution.py:276
  45.2 1.2 %finish.1 = bf16[1,2,128,1024]{3,2,1,0:T(8,128)(2,1)} custom-call(bf16[128,1024]{1,0:T(8,128)(2,1)S(1)} %get-tuple-element.64.state, bf16[128,1024]{1,0:T(8,128)(2,1)S(1)} %last_0.1.attended, bf16[1024,1024]{1,0:T(8,128)(2,1)S(1)} %get-tuple-element.48.wo, bf16[128,1024]{1,0:T(8,128)(2,1)S(1)} %collective-permute-done.9.arrived), custom_call_target="tpu_custom_call" | custom-call | flops 1000000000 | bytes 1000 | tf_op jit(solution)/shard_map/finish/pallas_call | solution.py:25
  (4 shorter events, 0.0 us)
Async XLA Ops:
  1.0 21.6 %collective-permute-start = (bf16[128,1024]{1,0:T(8,128)(2,1)S(1)}, bf16[128,1024]{1,0:T(8,128)(2,1)S(1)}, u32[]{:S(2)}, u32[]{:S(2)}) collective-permute-start(bf16[128,1024]{1,0:T(8,128)(2,1)S(1)} %fetch.1.token), channel_id=1, source_target_pairs={{0,32},{16,48},{32,64},{48,80},{64,96},{80,112},{96,128},{112,144}... | collective-permute-start | bytes 786440 | tf_op jit(solution)/shard_map/ppermute | solution.py:247
  5.5 9.1 %collective-permute-start.1 = (bf16[32,1024]{1,0:T(8,128)(2,1)S(1)}, bf16[32,1024]{1,0:T(8,128)(2,1)S(1)}, u32[]{:S(2)}, u32[]{:S(2)}) collective-permute-start(bf16[32,1024]{1,0:T(8,128)(2,1)S(1)} %get-tuple-element.43), channel_id=1, source_target_pairs={{0,15},{1,2},{2,1},{3,4},{4,3},{5,6},{6,5},{7,8},{8,7},{9,10},{10,... | collective-permute-start | bytes 196616 | tf_op jit(solution)/shard_map/ppermute | solution.py:232
  9.4 5.3 %collective-permute-start.2 = (bf16[32,1024]{1,0:T(8,128)(2,1)S(1)}, bf16[32,1024]{1,0:T(8,128)(2,1)S(1)}, u32[]{:S(2)}, u32[]{:S(2)}) collective-permute-start(bf16[32,1024]{1,0:T(8,128)(2,1)S(1)} %get-tuple-element.44), channel_id=1, source_target_pairs={{0,1},{1,0},{2,3},{3,2},{4,5},{5,4},{6,7},{7,6},{8,9},{9,8},{10,11... | collective-permute-start | bytes 196616 | tf_op jit(solution)/shard_map/ppermute | solution.py:232
  11.1 3.6 %copy-start = (f32[1024]{0:T(1024)S(1)}, f32[1024]{0:T(1024)}, u32[]{:S(2)}) copy-start(f32[1024]{0:T(1024)} %param.11) | copy-start | bytes 12292
  11.1 3.6 %copy-start.1 = (s32[1,2,32]{2,1,0:T(2,128)S(1)}, s32[1,2,32]{2,1,0:T(2,128)}, u32[]{:S(2)}) copy-start(s32[1,2,32]{2,1,0:T(2,128)} %param.17) | copy-start | bytes 772
  17.4 8.5 %collective-permute-start.5 = (bf16[32,1024]{1,0:T(8,128)(2,1)S(1)}, bf16[32,1024]{1,0:T(8,128)(2,1)S(1)}, u32[]{:S(2)}, u32[]{:S(2)}) collective-permute-start(bf16[32,1024]{1,0:T(8,128)(2,1)S(1)} %get-tuple-element.62), channel_id=1, source_target_pairs={{0,15},{1,2},{2,1},{3,4},{4,3},{5,6},{6,5},{7,8},{8,7},{9,10},{10,... | collective-permute-start | bytes 196616 | tf_op jit(solution)/shard_map/ppermute | solution.py:232
  17.5 8.4 %collective-permute-start.6 = (bf16[32,1024]{1,0:T(8,128)(2,1)S(1)}, bf16[32,1024]{1,0:T(8,128)(2,1)S(1)}, u32[]{:S(2)}, u32[]{:S(2)}) collective-permute-start(bf16[32,1024]{1,0:T(8,128)(2,1)S(1)} %get-tuple-element.63), channel_id=1, source_target_pairs={{0,1},{1,0},{2,3},{3,2},{4,5},{5,4},{6,7},{7,6},{8,9},{9,8},{10,11... | collective-permute-start | bytes 196616 | tf_op jit(solution)/shard_map/ppermute | solution.py:232
  24.0 7.2 %collective-permute-start.3 = (bf16[32,1024]{1,0:T(8,128)(2,1)S(1)}, bf16[32,1024]{1,0:T(8,128)(2,1)S(1)}, u32[]{:S(2)}, u32[]{:S(2)}) collective-permute-start(bf16[32,1024]{1,0:T(8,128)(2,1)S(1)} %get-tuple-element.57.token), channel_id=1, source_target_pairs={{0,15},{1,2},{2,1},{3,4},{4,3},{5,6},{6,5},{7,8},{8,7},{9,10},{10,... | collective-permute-start | bytes 196616 | tf_op jit(solution)/shard_map/ppermute | solution.py:232
  24.1 7.1 %collective-permute-start.4 = (bf16[32,1024]{1,0:T(8,128)(2,1)S(1)}, bf16[32,1024]{1,0:T(8,128)(2,1)S(1)}, u32[]{:S(2)}, u32[]{:S(2)}) collective-permute-start(bf16[32,1024]{1,0:T(8,128)(2,1)S(1)} %get-tuple-element.58), channel_id=1, source_target_pairs={{0,1},{1,0},{2,3},{3,2},{4,5},{5,4},{6,7},{7,6},{8,9},{9,8},{10,11... | collective-permute-start | bytes 196616 | tf_op jit(solution)/shard_map/ppermute | solution.py:232
  28.0 17.1 %collective-permute-start.9 = (bf16[128,1024]{1,0:T(8,128)(2,1)S(1)}, bf16[128,1024]{1,0:T(8,128)(2,1)S(1)}, u32[]{:S(2)}, u32[]{:S(2)}) collective-permute-start(bf16[128,1024]{1,0:T(8,128)(2,1)S(1)} %last_1.1.token), channel_id=1, source_target_pairs={{0,32},{16,48},{32,64},{48,80},{64,96},{80,112},{96,128},{112,144}... | collective-permute-start | bytes 786440 | tf_op jit(solution)/shard_map/ppermute | solution.py:276
  33.8 5.6 %collective-permute-start.7 = (bf16[32,1024]{1,0:T(8,128)(2,1)S(1)}, bf16[32,1024]{1,0:T(8,128)(2,1)S(1)}, u32[]{:S(2)}, u32[]{:S(2)}) collective-permute-start(bf16[32,1024]{1,0:T(8,128)(2,1)S(1)} %get-tuple-element.69), channel_id=1, source_target_pairs={{0,15},{1,2},{2,1},{3,4},{4,3},{5,6},{6,5},{7,8},{8,7},{9,10},{10,... | collective-permute-start | bytes 196616 | tf_op jit(solution)/shard_map/ppermute | solution.py:232
  35.8 3.6 %collective-permute-start.8 = (bf16[32,1024]{1,0:T(8,128)(2,1)S(1)}, bf16[32,1024]{1,0:T(8,128)(2,1)S(1)}, u32[]{:S(2)}, u32[]{:S(2)}) collective-permute-start(bf16[32,1024]{1,0:T(8,128)(2,1)S(1)} %get-tuple-element.70), channel_id=1, source_target_pairs={{0,1},{1,0},{2,3},{3,2},{4,5},{5,4},{6,7},{7,6},{8,9},{9,8},{10,11... | collective-permute-start | bytes 196616 | tf_op jit(solution)/shard_map/ppermute | solution.py:232

commit v4 on v2

v4 whole, which is shorter than its diff:
```python
import functools

import jax
import jax.numpy as jnp
from jax import lax
from jax.experimental import pallas as pl
from jax.experimental.pallas import tpu as pltpu

HEAD_DIM = 64
LANES = 128
NEVER = -1e30
BF = jnp.bfloat16
F32 = jnp.float32
CHUNKS = 4
VMEM_BYTES = 16 * 1024 * 1024
VMEM = pl.BlockSpec(memory_space=pltpu.VMEM)
HBM = pl.BlockSpec(memory_space=pltpu.HBM)
ANY = pl.BlockSpec(memory_space=pl.ANY)


def shape(*dims, dtype=BF):
    return jax.ShapeDtypeStruct(dims, dtype)


def call(body, name, ins, specs, outs, out_specs, scratch=(), micros=1.0, **more):
    return pl.pallas_call(
        body,
        out_shape=outs,
        in_specs=specs,
        out_specs=out_specs,
        scratch_shapes=list(scratch),
        compiler_params=pltpu.CompilerParams(vmem_limit_bytes=VMEM_BYTES),
        cost_estimate=pl.CostEstimate(flops=int(micros * 1e9), bytes_accessed=1000, transcendentals=0),
        name=name,
        **more,
    )(*ins)


def normalised(x, gain):
    values = x.astype(F32)
    centred = values - jnp.mean(values, axis=-1, keepdims=True)
    spread = jnp.mean(centred * centred, axis=-1, keepdims=True)
    return (centred * lax.rsqrt(spread + 1e-05) * gain).astype(BF)


def rows_of(table, indices):
    spots = lax.broadcasted_iota(jnp.int32, (table.shape[0], indices.shape[1]), 0)
    picks = jnp.where(spots == indices, 1.0, 0.0)
    return jnp.dot(picks.T.astype(BF), table, preferred_element_type=F32).astype(BF)


def begin(chosen, gain, halo, odd, state, normed, cross, inner):
    if state is not None:
        state[...] = chosen
    rows = normalised(chosen, gain[...])
    normed[...] = rows
    low, high = halo[0:1], halo[1:2]
    first, second = jnp.where(odd == 1, high, low), jnp.where(odd == 1, low, high)
    picked = rows_of(rows, jnp.concatenate([first, second], axis=1))
    cross[...] = picked[:halo.shape[1]]
    inner[...] = picked[halo.shape[1]:]


def bias_table(senders, odd, table):
    nodes = table.shape[0]
    count = jnp.zeros((table.shape[1], nodes), F32)
    spots = lax.broadcasted_iota(jnp.int32, count.shape, 0)
    half = (table.shape[1] - nodes) // 2
    spots = jnp.where((spots >= nodes) & (odd == 1), jnp.where(spots >= nodes + half, spots - half, spots + half), spots)
    for j in range(senders.shape[0]):
        count += jnp.where(spots == senders[j:j + 1], 1.0, 0.0)
    table[...] = jnp.where(count > 0, jnp.log(count), NEVER).T


def place_of(index):
    return lax.axis_index("lead") == index, lax.rem(lax.axis_index("mesh"), 2)


def fetch_body(index, states, entering, all_gain, all_halo, all_senders, far, own, gain, halo, senders, sems):
    special, _ = place_of(index)
    pairs = ((states.at[0, 0], far), (all_gain, gain), (all_halo, halo), (all_senders, senders), (states.at[0, 1], own))
    copies = [pltpu.make_async_copy(source, target, sems.at[i]) for i, (source, target) in enumerate(pairs)]
    for copy in copies[:-1]:
        copy.start()

    @pl.when(special)
    def _():
        pltpu.make_async_copy(entering.at[0, 1], own, sems.at[4]).start()

    @pl.when(jnp.logical_not(special))
    def _():
        copies[4].start()

    for copy in copies:
        copy.wait()


def near_first_body(own, gain, halo, senders, normed, cross, inner, table):
    odd = place_of(0)[1]
    bias_table(senders, odd, table)
    begin(own[...], gain, halo, odd, None, normed, cross, inner)


def far_first_body(index, moved, entering, gain, halo, token, state, normed, cross, inner, own, sem):
    special, odd = place_of(index)
    copy = pltpu.make_async_copy(entering.at[0, 0], own, sem)

    @pl.when(special)
    def _():
        copy.start()
        copy.wait()

    begin(jnp.where(special, own[...], moved[...]), gain, halo, odd, state, normed, cross, inner)


def queries_of(rows, weight):
    return jnp.dot(rows, weight, preferred_element_type=F32).astype(BF) * BF(HEAD_DIM ** -0.5)


def stream_body(normed, wq, wk, wv, wo, q, vq, vk, vv, vo, sems):
    copies = []
    for i, (source, target) in enumerate(((wq, vq), (wk, vk), (wv, vv), (wo, vo))):
        depth = source.shape[0] // CHUNKS
        for j in range(CHUNKS):
            at = pl.ds(j * depth, depth)
            copies.append(pltpu.make_async_copy(source.at[at], target.at[at], sems.at[i, j]))
            copies[-1].start()
    for copy in copies[:CHUNKS]:
        copy.wait()
    q[...] = queries_of(normed[...], vq[...])
    for copy in copies[CHUNKS:]:
        copy.wait()


def project_body(normed, wq, q):
    q[...] = queries_of(normed[...], wq[...])


def attention(q, normed, cross, inner, table, wk, wv, attended):
    rows = jnp.concatenate([normed[...], cross[...], inner[...]], axis=0)
    k = jnp.dot(rows, wk[...], preferred_element_type=F32).astype(BF)
    v = jnp.dot(rows, wv[...], preferred_element_type=F32).astype(BF)
    bias = table[...]
    nodes, width = q.shape
    bias = jnp.concatenate([bias, bias], axis=0)
    first = lax.broadcasted_iota(jnp.int32, (nodes, LANES), 1) < HEAD_DIM
    ones = jnp.ones((table.shape[1], LANES), BF)
    for i in range(width // LANES):
        at = slice(i * LANES, (i + 1) * LANES)
        pair = q[:, at]
        zero = jnp.zeros_like(pair)
        both = jnp.concatenate([jnp.where(first, pair, zero), jnp.where(first, zero, pair)], axis=0)
        keys, values = k[:, at], v[:, at]
        scores = lax.dot_general(both, keys, (((1,), (1,)), ((), ())), preferred_element_type=F32) + bias
        expo = jnp.exp(scores - jnp.max(scores, axis=1, keepdims=True)).astype(BF)
        sums = jnp.dot(expo, jnp.concatenate([values, ones], axis=1), preferred_element_type=F32)
        top = sums[:nodes, :LANES] / sums[:nodes, LANES:]
        low = sums[nodes:, :LANES] / sums[nodes:, LANES:]
        attended[:, at] = jnp.where(first, top, low).astype(BF)


def updated(state, attended, wo):
    update = jnp.dot(attended[...], wo[...], preferred_element_type=F32)
    return (state[...].astype(F32) + update).astype(BF)


def attend(state, q, normed, cross, inner, table, wk, wv, wo, attended):
    attention(q, normed, cross, inner, table, wk, wv, attended)
    return updated(state, attended, wo)


def middle_of(member, index):
    def body(state, q, normed, cross, inner, table, wk, wv, wo, entering, gain, halo, token,
             new_state, new_normed, new_cross, new_inner, attended, moved, sem):
        special, odd = place_of(index)

        @pl.when(special)
        def _():
            copy = pltpu.make_async_copy(entering.at[1, member], moved, sem)
            copy.start()
            copy.wait()

        @pl.when(jnp.logical_not(special))
        def _():
            moved[...] = attend(state, q, normed, cross, inner, table, wk, wv, wo, attended)

        begin(moved[...], gain, halo, odd, new_state, new_normed, new_cross, new_inner)

    return body


def last_body(state, q, normed, cross, inner, table, wk, wv, wo, token, out, attended):
    out[...] = attend(state, q, normed, cross, inner, table, wk, wv, wo, attended)


def finish_body(here, there, out, sems):
    copies = [pltpu.make_async_copy(x, out.at[0, i], sems.at[i]) for i, x in enumerate((here, there))]
    for copy in copies:
        copy.start()
    for copy in copies:
        copy.wait()


def per_device(states, entering, norm_gain, wq, wk, wv, wo, senders, halo_rows):
    leads, places = lax.axis_size("lead"), lax.axis_size("mesh")
    members, nodes, width = states.shape[1:]
    edge = halo_rows.shape[2]
    gain, halo, senders = norm_gain[None], halo_rows[0], senders.T
    states, entering = (pltpu.with_memory_space_constraint(x, pltpu.HBM) for x in (states, entering))
    vq, vk, vv, vo = wq, wk, wv, wo
    inner_route = [(i, i ^ 1) for i in range(places)]
    cross_route = [
        (a * places + i, ((a + leads // 2) % leads) * places + i if i in (0, places - 1) else a * places + ((i - 1) ^ 1) + 1)
        for a in range(leads)
        for i in range(places)
    ]
    route = [(i, (i + 2) % leads) for i in range(leads)]
    block, rim = shape(nodes, width), shape(edge, width)
    weight = shape(width, width)
    begun, begun_specs = [block, block, rim, rim], [VMEM] * 4
    dma = pltpu.SemaphoreType.DMA

    def exchanged(cross, inner):
        return lax.ppermute(cross, ("lead", "mesh"), cross_route), lax.ppermute(inner, "mesh", inner_route)

    def project(normed):
        return call(project_body, "project", [normed, vq], [VMEM] * 2, block, VMEM)

    def last(state, q, normed, cross, inner, token, name):
        return call(
            last_body, name, [state, q, normed, cross, inner, table, vk, vv, vo, token],
            [VMEM] * 9 + [ANY], block, VMEM, [pltpu.VMEM((nodes, width), BF)],
        )

    def middle(member, index, state, q, normed, cross, inner, token):
        return call(
            middle_of(member, index), f"middle_{member}",
            [state, q, normed, cross, inner, table, vk, vv, vo, entering, gain, halo, token],
            [VMEM] * 9 + [HBM, VMEM, VMEM, ANY], begun, begun_specs,
            [pltpu.VMEM((nodes, width), BF), pltpu.VMEM((nodes, width), BF), dma],
        )

    far, state1, gain, halo, senders = call(
        functools.partial(fetch_body, leads - 1), "fetch",
        [states, entering] + [pltpu.with_memory_space_constraint(x, pltpu.HBM) for x in (gain, halo, senders)],
        [HBM] * 5,
        [block, block] + [shape(*x.shape, dtype=x.dtype) for x in (gain, halo, senders)],
        [VMEM] * 5, [dma((5,))],
    )
    far = lax.ppermute(far, "lead", route)
    normed1, cross1, inner1, table = call(
        near_first_body, "near_first", [state1, gain, halo, senders], [VMEM] * 4,
        [block, rim, rim, shape(nodes, nodes + 2 * edge, dtype=F32)], [VMEM] * 4,
    )
    cross1, inner1 = exchanged(cross1, inner1)
    q1 = project(normed1)
    state1, normed1, cross1, inner1 = middle(1, leads - 2, state1, q1, normed1, cross1, inner1, q1)
    cross1, inner1 = exchanged(cross1, inner1)
    q1 = project(normed1)
    state0, normed0, cross0, inner0 = call(
        functools.partial(far_first_body, 1), "far_first",
        [far, entering, gain, halo, q1],
        [VMEM, HBM, VMEM, VMEM, ANY], begun, begun_specs,
        [pltpu.VMEM((nodes, width), BF), dma],
    )
    token = cross0
    cross0, inner0 = exchanged(cross0, inner0)
    near = last(state1, q1, normed1, cross1, inner1, token, "last_1")
    arrived = lax.ppermute(near, "lead", route)
    q0 = project(normed0)
    state0, normed0, cross0, inner0 = middle(0, 0, state0, q0, normed0, cross0, inner0, near)
    cross0, inner0 = exchanged(cross0, inner0)
    q0 = project(normed0)
    here = last(state0, q0, normed0, cross0, inner0, normed0, "last_0")
    return call(
        finish_body, "finish", [here, arrived], [VMEM] * 2,
        shape(1, members, nodes, width), HBM, [dma((2,))],
    )


def solution(mesh):
    P = jax.sharding.PartitionSpec
    in_specs = (
        P("lead", None, "mesh", None),
        P(None, None, "mesh", None),
        P(),
        P(),
        P(),
        P(),
        P(),
        P("mesh", None),
        P("mesh", None, None),
    )
    return jax.shard_map(
        per_device, mesh=mesh, in_specs=in_specs, out_specs=P("lead", None, "mesh", None), check_vma=False
    )
```

time: 52.3 us -> 44 us (0.84)
  starting transfers between devices: 26.8 us -> 14.3 us
  waiting for transfers between devices: 4.42 us -> 16.3 us
  Pallas kernels: 20.4 us -> 12.9 us
    ppermute x4, starting transfers between devices: 19.7 us -> 9.25 us  [exchanged(): lax.ppermute(cross, ('lead', 'mesh'), cross_route)]
    ppermute x4, waiting for transfers between devices: 4.22 us -> 12.1 us  [exchanged(): lax.ppermute(cross, ('lead', 'mesh'), cross_route)]
    pallas_call x11 -> x12, Pallas kernels: 20.4 us -> 12.9 us  [call(): pl.pallas_call(body, out_shape=outs, in_specs=specs, out_specs=out_specs,...]
    ppermute x1, waiting for transfers between devices: 0.01 us -> 4.18 us  [per_device(): arrived = lax.ppermute(near, 'lead', route)]
    ppermute x1, starting transfers between devices: 3.75 us -> 0.24 us  [per_device(): arrived = lax.ppermute(near, 'lead', route)]
    ppermute x1, starting transfers between devices: 3.07 us -> 3.9 us  [per_device(): far = lax.ppermute(far, 'lead', route)]
    ppermute x4, starting transfers between devices: 0.37 us -> 0.97 us  [exchanged(): lax.ppermute(inner, 'mesh', inner_route)]
  transfers between devices with their start and end apart: 10 -> 10, of which waited for: 2 -> 5; matrix products, arithmetic and copies ran while one was open for 0% -> 0% of each run, Pallas kernels for 35% -> 25%
where the time goes in v4:
time: 44 us; the launch traced here: 43.8 us
  waiting for transfers between devices  16.3 us (37%)
  starting transfers between devices  14.3 us (32%)
  Pallas kernels  12.9 us (29%)
    pallas_call x12, Pallas kernels, call(): pl.pallas_call(body, out_shape=outs, in_specs=specs, out_specs=out_specs,...  12.9 us
    ppermute x4, waiting for transfers between devices, exchanged(): lax.ppermute(cross, ('lead', 'mesh'), cross_route)  12.1 us
    ppermute x4, starting transfers between devices, exchanged(): lax.ppermute(cross, ('lead', 'mesh'), cross_route)  9.25 us
    ppermute x1, waiting for transfers between devices, per_device(): arrived = lax.ppermute(near, 'lead', route)  4.18 us
    ppermute x1, starting transfers between devices, per_device(): far = lax.ppermute(far, 'lead', route)  3.9 us
    ppermute x4, starting transfers between devices, exchanged(): lax.ppermute(inner, 'mesh', inner_route)  0.97 us
  transfers between devices with their start and end apart: 10, of which 5 were waited for; matrix products, arithmetic and copies ran while one was open for 0% of the time, Pallas kernels for 25%

profile of v4, /device:TPU:1, one launch (start us, length us, event | category | flops | bytes accessed | tf_op | source)
XLA Modules:
  0.0 43.8 jit_solution(3582823995894155634)
XLA Ops:
  0.0 1.3 %fetch.1 = (bf16[128,1024]{1,0:T(8,128)(2,1)S(1)}, bf16[128,1024]{1,0:T(8,128)(2,1)S(1)}, f32[1,1024]{1,0:T(1,128)S(1)}, s32[2,32]{1,0:T(2,128)S(1)}, s32[8,128]{1,0:T(8,128)S(1)}) custom-call(bf16[1,2,128,1024]{3,2,1,0:T(8,128)(2,1)} %states.1, bf16[2,2,128,1024]{3,2,1,0:T(8,128)(2,1)} %entering.7, f32[1,1024]{1,0:T(1,128)} %bitcast.3, s32[2,32]{1,0:T(2,128)} %bitcast.5, ...), custom_call_target="tpu_custom_call" | custom-call | flops 1000000000 | bytes 1000 | tf_op jit(solution)/shard_map/fetch/pallas_call | solution.py:26
  1.3 3.9 %collective-permute-start = (bf16[128,1024]{1,0:T(8,128)(2,1)S(1)}, bf16[128,1024]{1,0:T(8,128)(2,1)S(1)}, u32[]{:S(2)}, u32[]{:S(2)}) collective-permute-start(bf16[128,1024]{1,0:T(8,128)(2,1)S(1)} %get-tuple-element.26), channel_id=1, source_target_pairs={{0,32},{16,48},{32,64},{48,80},{64,96},{80,112},{96,128},{112,144}... | collective-permute-start | bytes 786440 | tf_op jit(solution)/shard_map/ppermute | solution.py:250
  5.2 0.5 %near_first.1 = (bf16[128,1024]{1,0:T(8,128)(2,1)S(1)}, bf16[32,1024]{1,0:T(8,128)(2,1)S(1)}, bf16[32,1024]{1,0:T(8,128)(2,1)S(1)}, f32[128,192]{1,0:T(8,128)S(1)}) custom-call(bf16[128,1024]{1,0:T(8,128)(2,1)S(1)} %get-tuple-element.29.own.state, f32[1,1024]{1,0:T(1,128)S(1)} %get-tuple-element.27.gain, s32[2,32]{1,0:T(2,128)S(1)} %get-tuple-element.28.halo, ...), custom_call_target="tpu_custom_call" | custom-call | flops 1000000000 | bytes 1000 | tf_op jit(solution)/shard_map/near_first/pallas_call | solution.py:26
  5.7 0.0 copy-start
  5.7 3.8 %collective-permute-start.1 = (bf16[32,1024]{1,0:T(8,128)(2,1)S(1)}, bf16[32,1024]{1,0:T(8,128)(2,1)S(1)}, u32[]{:S(2)}, u32[]{:S(2)}) collective-permute-start(bf16[32,1024]{1,0:T(8,128)(2,1)S(1)} %get-tuple-element.32), channel_id=1, source_target_pairs={{0,128},{1,2},{2,1},{3,4},{4,3},{5,6},{6,5},{7,8},{8,7},{9,10},{10... | collective-permute-start | bytes 196616 | tf_op jit(solution)/shard_map/ppermute | solution.py:224
  9.5 0.5 %project.4.q.token = bf16[128,1024]{1,0:T(8,128)(2,1)S(1)} custom-call(bf16[128,1024]{1,0:T(8,128)(2,1)S(1)} %get-tuple-element.31.normed, bf16[1024,1024]{1,0:T(8,128)(2,1)S(1)} %copy-done.3), custom_call_target="tpu_custom_call" | custom-call | flops 1000000000 | bytes 1000 | tf_op jit(solution)/shard_map/project/pallas_call | solution.py:26
  10.0 6.3 %collective-permute-done.1.cross = bf16[32,1024]{1,0:T(8,128)(2,1)S(1)} collective-permute-done((bf16[32,1024]{1,0:T(8,128)(2,1)S(1)}, bf16[32,1024]{1,0:T(8,128)(2,1)S(1)}, u32[]{:S(2)}, u32[]{:S(2)}) %collective-permute-start.1) | collective-permute-done | bytes 65568 | tf_op jit(solution)/shard_map/ppermute | solution.py:224
  16.3 0.0 collective-permute-done.2.inner
  16.3 2.5 %middle_1.1 = (bf16[128,1024]{1,0:T(8,128)(2,1)S(1)}, bf16[128,1024]{1,0:T(8,128)(2,1)S(1)}, bf16[32,1024]{1,0:T(8,128)(2,1)S(1)}, bf16[32,1024]{1,0:T(8,128)(2,1)S(1)}) custom-call(bf16[128,1024]{1,0:T(8,128)(2,1)S(1)} %get-tuple-element.29.own.state, bf16[128,1024]{1,0:T(8,128)(2,1)S(1)} %project.4.q.token, ...), custom_call_target="tpu_custom_call" | custom-call | flops 1000000000 | bytes 1000 | tf_op jit(solution)/shard_map/middle_1/pallas_call | solution.py:26
  18.9 4.0 %collective-permute-start.5 = (bf16[32,1024]{1,0:T(8,128)(2,1)S(1)}, bf16[32,1024]{1,0:T(8,128)(2,1)S(1)}, u32[]{:S(2)}, u32[]{:S(2)}) collective-permute-start(bf16[32,1024]{1,0:T(8,128)(2,1)S(1)} %get-tuple-element.41), channel_id=1, source_target_pairs={{0,128},{1,2},{2,1},{3,4},{4,3},{5,6},{6,5},{7,8},{8,7},{9,10},{10... | collective-permute-start | bytes 196616 | tf_op jit(solution)/shard_map/ppermute | solution.py:224
  22.9 0.0 collective-permute-start.6
  22.9 0.5 %project.5.token.q = bf16[128,1024]{1,0:T(8,128)(2,1)S(1)} custom-call(bf16[128,1024]{1,0:T(8,128)(2,1)S(1)} %get-tuple-element.35.normed, bf16[1024,1024]{1,0:T(8,128)(2,1)S(1)} %copy-done.3), custom_call_target="tpu_custom_call" | custom-call | flops 1000000000 | bytes 1000 | tf_op jit(solution)/shard_map/project/pallas_call | solution.py:26
  23.4 0.0 collective-permute-done.moved
  23.4 0.4 %far_first.1 = (bf16[128,1024]{1,0:T(8,128)(2,1)S(1)}, bf16[128,1024]{1,0:T(8,128)(2,1)S(1)}, bf16[32,1024]{1,0:T(8,128)(2,1)S(1)}, bf16[32,1024]{1,0:T(8,128)(2,1)S(1)}) custom-call(bf16[128,1024]{1,0:T(8,128)(2,1)S(1)} %collective-permute-done.moved, bf16[2,2,128,1024]{3,2,1,0:T(8,128)(2,1)} %entering.7, f32[1,1024]{1,0:T(1,128)S(1)} %get-tuple-element.27.gain, ...), custom_call_target="tpu_custom_call" | custom-call | flops 1000000000 | bytes 1000 | tf_op jit(solution)/shard_map/far_first/pallas_call | solution.py:26
  23.8 0.6 %collective-permute-start.4 = (bf16[32,1024]{1,0:T(8,128)(2,1)S(1)}, bf16[32,1024]{1,0:T(8,128)(2,1)S(1)}, u32[]{:S(2)}, u32[]{:S(2)}) collective-permute-start(bf16[32,1024]{1,0:T(8,128)(2,1)S(1)} %get-tuple-element.39), channel_id=1, source_target_pairs={{0,1},{1,0},{2,3},{3,2},{4,5},{5,4},{6,7},{7,6},{8,9},{9,8},{10,11... | collective-permute-start | bytes 196616 | tf_op jit(solution)/shard_map/ppermute | solution.py:224
  24.4 0.1 collective-permute-start.3
  24.5 0.3 collective-permute-done.5.cross
  24.9 0.0 collective-permute-done.6.inner
  24.9 2.1 %last_1.1.token = bf16[128,1024]{1,0:T(8,128)(2,1)S(1)} custom-call(bf16[128,1024]{1,0:T(8,128)(2,1)S(1)} %get-tuple-element.40.state, bf16[128,1024]{1,0:T(8,128)(2,1)S(1)} %project.5.token.q, bf16[128,1024]{1,0:T(8,128)(2,1)S(1)} %get-tuple-element.35.normed, bf16[32,1024]{1,0:T(8,128)(2,1)S(1)} %collective-permute-done.5.cross, ...), custom_call_target="tpu_custom_call" | custom-call | flops 1000000000 | bytes 1000 | tf_op jit(solution)/shard_map/last_1/pallas_call | solution.py:26
  27.0 0.2 collective-permute-start.9
  27.2 0.4 %project.6.q = bf16[128,1024]{1,0:T(8,128)(2,1)S(1)} custom-call(bf16[128,1024]{1,0:T(8,128)(2,1)S(1)} %get-tuple-element.37.normed, bf16[1024,1024]{1,0:T(8,128)(2,1)S(1)} %copy-done.3), custom_call_target="tpu_custom_call" | custom-call | flops 1000000000 | bytes 1000 | tf_op jit(solution)/shard_map/project/pallas_call | solution.py:26
  27.7 0.0 collective-permute-done.4.inner
  27.7 2.0 %collective-permute-done.3.cross = bf16[32,1024]{1,0:T(8,128)(2,1)S(1)} collective-permute-done((bf16[32,1024]{1,0:T(8,128)(2,1)S(1)}, bf16[32,1024]{1,0:T(8,128)(2,1)S(1)}, u32[]{:S(2)}, u32[]{:S(2)}) %collective-permute-start.3) | collective-permute-done | bytes 65568 | tf_op jit(solution)/shard_map/ppermute | solution.py:224
  29.6 1.4 %middle_0.1 = (bf16[128,1024]{1,0:T(8,128)(2,1)S(1)}, bf16[128,1024]{1,0:T(8,128)(2,1)S(1)}, bf16[32,1024]{1,0:T(8,128)(2,1)S(1)}, bf16[32,1024]{1,0:T(8,128)(2,1)S(1)}) custom-call(bf16[128,1024]{1,0:T(8,128)(2,1)S(1)} %get-tuple-element.36.state, bf16[128,1024]{1,0:T(8,128)(2,1)S(1)} %project.6.q, bf16[128,1024]{1,0:T(8,128)(2,1)S(1)} %get-tuple-element.37.normed, ...), custom_call_target="tpu_custom_call" | custom-call | flops 1000000000 | bytes 1000 | tf_op jit(solution)/shard_map/middle_0/pallas_call | solution.py:26
  31.0 1.3 %collective-permute-start.7 = (bf16[32,1024]{1,0:T(8,128)(2,1)S(1)}, bf16[32,1024]{1,0:T(8,128)(2,1)S(1)}, u32[]{:S(2)}, u32[]{:S(2)}) collective-permute-start(bf16[32,1024]{1,0:T(8,128)(2,1)S(1)} %get-tuple-element.45), channel_id=1, source_target_pairs={{0,128},{1,2},{2,1},{3,4},{4,3},{5,6},{6,5},{7,8},{8,7},{9,10},{10... | collective-permute-start | bytes 196616 | tf_op jit(solution)/shard_map/ppermute | solution.py:224
  32.3 0.4 collective-permute-start.8
  32.6 0.5 %project.7.q = bf16[128,1024]{1,0:T(8,128)(2,1)S(1)} custom-call(bf16[128,1024]{1,0:T(8,128)(2,1)S(1)} %get-tuple-element.44.normed.token, bf16[1024,1024]{1,0:T(8,128)(2,1)S(1)} %copy-done.3), custom_call_target="tpu_custom_call" | custom-call | flops 1000000000 | bytes 1000 | tf_op jit(solution)/shard_map/project/pallas_call | solution.py:26
  33.1 3.5 %collective-permute-done.7.cross = bf16[32,1024]{1,0:T(8,128)(2,1)S(1)} collective-permute-done((bf16[32,1024]{1,0:T(8,128)(2,1)S(1)}, bf16[32,1024]{1,0:T(8,128)(2,1)S(1)}, u32[]{:S(2)}, u32[]{:S(2)}) %collective-permute-start.7) | collective-permute-done | bytes 65568 | tf_op jit(solution)/shard_map/ppermute | solution.py:224
  36.6 0.0 collective-permute-done.8.inner
  36.6 2.1 %last_0.1.here = bf16[128,1024]{1,0:T(8,128)(2,1)S(1)} custom-call(bf16[128,1024]{1,0:T(8,128)(2,1)S(1)} %get-tuple-element.43.state, bf16[128,1024]{1,0:T(8,128)(2,1)S(1)} %project.7.q, bf16[128,1024]{1,0:T(8,128)(2,1)S(1)} %get-tuple-element.44.normed.token, bf16[32,1024]{1,0:T(8,128)(2,1)S(1)} %collective-permute-done.7.cross, ...), custom_call_target="tpu_custom_call" | custom-call | flops 1000000000 | bytes 1000 | tf_op jit(solution)/shard_map/last_0/pallas_call | solution.py:26
  38.7 4.2 %collective-permute-done.9.there = bf16[128,1024]{1,0:T(8,128)(2,1)S(1)} collective-permute-done((bf16[128,1024]{1,0:T(8,128)(2,1)S(1)}, bf16[128,1024]{1,0:T(8,128)(2,1)S(1)}, u32[]{:S(2)}, u32[]{:S(2)}) %collective-permute-start.9) | collective-permute-done | bytes 262176 | tf_op jit(solution)/shard_map/ppermute | solution.py:269
  42.9 0.8 %finish.1 = bf16[1,2,128,1024]{3,2,1,0:T(8,128)(2,1)} custom-call(bf16[128,1024]{1,0:T(8,128)(2,1)S(1)} %last_0.1.here, bf16[128,1024]{1,0:T(8,128)(2,1)S(1)} %collective-permute-done.9.there), custom_call_target="tpu_custom_call" | custom-call | flops 1000000000 | bytes 1000 | tf_op jit(solution)/shard_map/finish/pallas_call | solution.py:26
  (8 shorter events, 0.0 us)
Async XLA Ops:
  0.0 9.5 %copy-start.3 = (bf16[1024,1024]{1,0:T(8,128)(2,1)S(1)}, bf16[1024,1024]{1,0:T(8,128)(2,1)}, u32[]{:S(2)}) copy-start(bf16[1024,1024]{1,0:T(8,128)(2,1)} %wq.7) | copy-start | bytes 6291460
  1.3 22.1 %collective-permute-start = (bf16[128,1024]{1,0:T(8,128)(2,1)S(1)}, bf16[128,1024]{1,0:T(8,128)(2,1)S(1)}, u32[]{:S(2)}, u32[]{:S(2)}) collective-permute-start(bf16[128,1024]{1,0:T(8,128)(2,1)S(1)} %get-tuple-element.26), channel_id=1, source_target_pairs={{0,32},{16,48},{32,64},{48,80},{64,96},{80,112},{96,128},{112,144}... | collective-permute-start | bytes 786440 | tf_op jit(solution)/shard_map/ppermute | solution.py:250
  5.2 11.1 %copy-start.1 = (bf16[1024,1024]{1,0:T(8,128)(2,1)S(1)}, bf16[1024,1024]{1,0:T(8,128)(2,1)}, u32[]{:S(2)}) copy-start(bf16[1024,1024]{1,0:T(8,128)(2,1)} %wv.7) | copy-start | bytes 6291460
  5.2 11.1 %copy-start.2 = (bf16[1024,1024]{1,0:T(8,128)(2,1)S(1)}, bf16[1024,1024]{1,0:T(8,128)(2,1)}, u32[]{:S(2)}) copy-start(bf16[1024,1024]{1,0:T(8,128)(2,1)} %wo.7) | copy-start | bytes 6291460
  5.7 10.6 %copy-start = (bf16[1024,1024]{1,0:T(8,128)(2,1)S(1)}, bf16[1024,1024]{1,0:T(8,128)(2,1)}, u32[]{:S(2)}) copy-start(bf16[1024,1024]{1,0:T(8,128)(2,1)} %wk.7) | copy-start | bytes 6291460
  5.7 10.6 %collective-permute-start.1 = (bf16[32,1024]{1,0:T(8,128)(2,1)S(1)}, bf16[32,1024]{1,0:T(8,128)(2,1)S(1)}, u32[]{:S(2)}, u32[]{:S(2)}) collective-permute-start(bf16[32,1024]{1,0:T(8,128)(2,1)S(1)} %get-tuple-element.32), channel_id=1, source_target_pairs={{0,128},{1,2},{2,1},{3,4},{4,3},{5,6},{6,5},{7,8},{8,7},{9,10},{10... | collective-permute-start | bytes 196616 | tf_op jit(solution)/shard_map/ppermute | solution.py:224
  9.5 6.8 %collective-permute-start.2 = (bf16[32,1024]{1,0:T(8,128)(2,1)S(1)}, bf16[32,1024]{1,0:T(8,128)(2,1)S(1)}, u32[]{:S(2)}, u32[]{:S(2)}) collective-permute-start(bf16[32,1024]{1,0:T(8,128)(2,1)S(1)} %get-tuple-element.33), channel_id=1, source_target_pairs={{0,1},{1,0},{2,3},{3,2},{4,5},{5,4},{6,7},{7,6},{8,9},{9,8},{10,11... | collective-permute-start | bytes 196616 | tf_op jit(solution)/shard_map/ppermute | solution.py:224
  18.9 6.0 %collective-permute-start.5 = (bf16[32,1024]{1,0:T(8,128)(2,1)S(1)}, bf16[32,1024]{1,0:T(8,128)(2,1)S(1)}, u32[]{:S(2)}, u32[]{:S(2)}) collective-permute-start(bf16[32,1024]{1,0:T(8,128)(2,1)S(1)} %get-tuple-element.41), channel_id=1, source_target_pairs={{0,128},{1,2},{2,1},{3,4},{4,3},{5,6},{6,5},{7,8},{8,7},{9,10},{10... | collective-permute-start | bytes 196616 | tf_op jit(solution)/shard_map/ppermute | solution.py:224
  22.9 2.0 %collective-permute-start.6 = (bf16[32,1024]{1,0:T(8,128)(2,1)S(1)}, bf16[32,1024]{1,0:T(8,128)(2,1)S(1)}, u32[]{:S(2)}, u32[]{:S(2)}) collective-permute-start(bf16[32,1024]{1,0:T(8,128)(2,1)S(1)} %get-tuple-element.42), channel_id=1, source_target_pairs={{0,1},{1,0},{2,3},{3,2},{4,5},{5,4},{6,7},{7,6},{8,9},{9,8},{10,11... | collective-permute-start | bytes 196616 | tf_op jit(solution)/shard_map/ppermute | solution.py:224
  23.8 3.8 %collective-permute-start.4 = (bf16[32,1024]{1,0:T(8,128)(2,1)S(1)}, bf16[32,1024]{1,0:T(8,128)(2,1)S(1)}, u32[]{:S(2)}, u32[]{:S(2)}) collective-permute-start(bf16[32,1024]{1,0:T(8,128)(2,1)S(1)} %get-tuple-element.39), channel_id=1, source_target_pairs={{0,1},{1,0},{2,3},{3,2},{4,5},{5,4},{6,7},{7,6},{8,9},{9,8},{10,11... | collective-permute-start | bytes 196616 | tf_op jit(solution)/shard_map/ppermute | solution.py:224
  24.4 5.2 %collective-permute-start.3 = (bf16[32,1024]{1,0:T(8,128)(2,1)S(1)}, bf16[32,1024]{1,0:T(8,128)(2,1)S(1)}, u32[]{:S(2)}, u32[]{:S(2)}) collective-permute-start(bf16[32,1024]{1,0:T(8,128)(2,1)S(1)} %get-tuple-element.38.token), channel_id=1, source_target_pairs={{0,128},{1,2},{2,1},{3,4},{4,3},{5,6},{6,5},{7,8},{8,7},{9,10},{10... | collective-permute-start | bytes 196616 | tf_op jit(solution)/shard_map/ppermute | solution.py:224
  27.0 15.9 %collective-permute-start.9 = (bf16[128,1024]{1,0:T(8,128)(2,1)S(1)}, bf16[128,1024]{1,0:T(8,128)(2,1)S(1)}, u32[]{:S(2)}, u32[]{:S(2)}) collective-permute-start(bf16[128,1024]{1,0:T(8,128)(2,1)S(1)} %last_1.1.token), channel_id=1, source_target_pairs={{0,32},{16,48},{32,64},{48,80},{64,96},{80,112},{96,128},{112,144}... | collective-permute-start | bytes 786440 | tf_op jit(solution)/shard_map/ppermute | solution.py:269
  31.0 5.6 %collective-permute-start.7 = (bf16[32,1024]{1,0:T(8,128)(2,1)S(1)}, bf16[32,1024]{1,0:T(8,128)(2,1)S(1)}, u32[]{:S(2)}, u32[]{:S(2)}) collective-permute-start(bf16[32,1024]{1,0:T(8,128)(2,1)S(1)} %get-tuple-element.45), channel_id=1, source_target_pairs={{0,128},{1,2},{2,1},{3,4},{4,3},{5,6},{6,5},{7,8},{8,7},{9,10},{10... | collective-permute-start | bytes 196616 | tf_op jit(solution)/shard_map/ppermute | solution.py:224
  32.3 4.3 %collective-permute-start.8 = (bf16[32,1024]{1,0:T(8,128)(2,1)S(1)}, bf16[32,1024]{1,0:T(8,128)(2,1)S(1)}, u32[]{:S(2)}, u32[]{:S(2)}) collective-permute-start(bf16[32,1024]{1,0:T(8,128)(2,1)S(1)} %get-tuple-element.46), channel_id=1, source_target_pairs={{0,1},{1,0},{2,3},{3,2},{4,5},{5,4},{6,7},{7,6},{8,9},{9,8},{10,11... | collective-permute-start | bytes 196616 | tf_op jit(solution)/shard_map/ppermute | solution.py:224

commit v5 on v4

v5 whole, which is shorter than its diff:
```python
import functools

import jax
import jax.numpy as jnp
from jax import lax
from jax.experimental import pallas as pl
from jax.experimental.pallas import tpu as pltpu

HEAD_DIM = 64
LANES = 128
NEVER = -1e30
BF = jnp.bfloat16
F32 = jnp.float32
CHUNKS = 4
MP = 1.0
ML = 1.0
VMEM_BYTES = 16 * 1024 * 1024
VMEM = pl.BlockSpec(memory_space=pltpu.VMEM)
HBM = pl.BlockSpec(memory_space=pltpu.HBM)
ANY = pl.BlockSpec(memory_space=pl.ANY)


def shape(*dims, dtype=BF):
    return jax.ShapeDtypeStruct(dims, dtype)


def call(body, name, ins, specs, outs, out_specs, scratch=(), micros=1.0, **more):
    return pl.pallas_call(
        body,
        out_shape=outs,
        in_specs=specs,
        out_specs=out_specs,
        scratch_shapes=list(scratch),
        compiler_params=pltpu.CompilerParams(vmem_limit_bytes=VMEM_BYTES),
        cost_estimate=pl.CostEstimate(flops=int(micros * 1e9), bytes_accessed=1000, transcendentals=0),
        name=name,
        **more,
    )(*ins)


def normalised(x, gain):
    values = x.astype(F32)
    centred = values - jnp.mean(values, axis=-1, keepdims=True)
    spread = jnp.mean(centred * centred, axis=-1, keepdims=True)
    return (centred * lax.rsqrt(spread + 1e-05) * gain).astype(BF)


def rows_of(table, indices):
    spots = lax.broadcasted_iota(jnp.int32, (table.shape[0], indices.shape[1]), 0)
    picks = jnp.where(spots == indices, 1.0, 0.0)
    return jnp.dot(picks.T.astype(BF), table, preferred_element_type=F32).astype(BF)


def picked_rows(rows, halo, odd):
    low, high = halo[0:1], halo[1:2]
    first, second = jnp.where(odd == 1, high, low), jnp.where(odd == 1, low, high)
    return rows_of(rows, jnp.concatenate([first, second], axis=1))


def bias_table(senders, odd, table):
    nodes = table.shape[0]
    count = jnp.zeros((table.shape[1], nodes), F32)
    spots = lax.broadcasted_iota(jnp.int32, count.shape, 0)
    half = (table.shape[1] - nodes) // 2
    spots = jnp.where((spots >= nodes) & (odd == 1), jnp.where(spots >= nodes + half, spots - half, spots + half), spots)
    for j in range(senders.shape[0]):
        count += jnp.where(spots == senders[j:j + 1], 1.0, 0.0)
    table[...] = jnp.where(count > 0, jnp.log(count), NEVER).T


def parity():
    return lax.rem(lax.axis_index("mesh"), 2)


def start_body(once, twice, states, entering, all_gain, all_halo,
               far, own, gain, halo, normed, cross, inner, sems):
    lead = lax.axis_index("lead")
    small = ((all_gain, gain), (all_halo, halo))
    copies = [pltpu.make_async_copy(source, target, sems.at[i]) for i, (source, target) in enumerate(small)]
    for copy in copies:
        copy.start()
    choices = (
        (lead == once, entering, 1),
        (lead == twice, entering, 0),
        ((lead != once) & (lead != twice), states, 0),
    )
    for chosen, source, step in choices:

        @pl.when(chosen)
        def _(source=source, step=step):
            pltpu.make_async_copy(source.at[step, 1], own, sems.at[3]).start()
            pltpu.make_async_copy(source.at[step, 0], far, sems.at[4]).start()

    for copy in copies:
        copy.wait()
    odd = parity()
    edge = halo.shape[1]
    pltpu.make_async_copy(states.at[0, 1], own, sems.at[3]).wait()
    rows = normalised(own[...], gain[...])
    normed[...] = rows
    picked = picked_rows(rows, halo, odd)
    cross[:edge], inner[...] = picked[:edge], picked[edge:]
    pltpu.make_async_copy(states.at[0, 0], far, sems.at[4]).wait()
    low, high = halo[0:1], halo[1:2]
    cross[edge:] = rows_of(normalised(far[...], gain[...]), jnp.where(odd == 1, high, low))


def queries_of(rows, weight):
    return jnp.dot(rows, weight, preferred_element_type=F32).astype(BF) * BF(HEAD_DIM ** -0.5)


def stream_body(normed, wq, wk, wv, wo, q, vq, vk, vv, vo, sems):
    copies = []
    for i, (source, target) in enumerate(((wq, vq), (wk, vk), (wv, vv), (wo, vo))):
        depth = source.shape[0] // CHUNKS
        for j in range(CHUNKS):
            at = pl.ds(j * depth, depth)
            copies.append(pltpu.make_async_copy(source.at[at], target.at[at], sems.at[i, j]))
            copies[-1].start()
    for copy in copies[:CHUNKS]:
        copy.wait()
    q[...] = queries_of(normed[...], vq[...])
    for copy in copies[CHUNKS:]:
        copy.wait()


def project_first_body(normed, wq, senders, q, vq, table, sems):
    depth = wq.shape[0] // CHUNKS
    copies = []
    for i in range(CHUNKS):
        at = pl.ds(i * depth, depth)
        copies.append(pltpu.make_async_copy(wq.at[at], vq.at[at], sems.at[i]))
        copies[-1].start()
    bias_table(senders, parity(), table)
    for copy in copies:
        copy.wait()
    q[...] = queries_of(normed[...], vq[...])


def project_body(normed, wq, q):
    q[...] = queries_of(normed[...], wq[...])


def far_first_body(far, gain, halo, token, normed, inner):
    rows = normalised(far[...], gain[...])
    normed[...] = rows
    low, high = halo[0:1], halo[1:2]
    inner[...] = rows_of(rows, jnp.where(parity() == 1, low, high))


def attention(q, normed, cross, inner, table, wk, wv, attended):
    rows = jnp.concatenate([normed[...], cross, inner], axis=0)
    k = jnp.dot(rows, wk[...], preferred_element_type=F32).astype(BF)
    v = jnp.dot(rows, wv[...], preferred_element_type=F32).astype(BF)
    bias = table[...]
    nodes, width = q.shape
    bias = jnp.concatenate([bias, bias], axis=0)
    first = lax.broadcasted_iota(jnp.int32, (nodes, LANES), 1) < HEAD_DIM
    ones = jnp.ones((table.shape[1], LANES), BF)
    for i in range(width // LANES):
        at = slice(i * LANES, (i + 1) * LANES)
        pair = q[:, at]
        zero = jnp.zeros_like(pair)
        both = jnp.concatenate([jnp.where(first, pair, zero), jnp.where(first, zero, pair)], axis=0)
        scores = lax.dot_general(both, k[:, at], (((1,), (1,)), ((), ())), preferred_element_type=F32) + bias
        expo = jnp.exp(scores - jnp.max(scores, axis=1, keepdims=True)).astype(BF)
        sums = jnp.dot(expo, jnp.concatenate([v[:, at], ones], axis=1), preferred_element_type=F32)
        top = sums[:nodes, :LANES] / sums[:nodes, LANES:]
        low = sums[nodes:, :LANES] / sums[nodes:, LANES:]
        attended[:, at] = jnp.where(first, top, low).astype(BF)


def attend(state, q, normed, cross, inner, table, wk, wv, wo, attended):
    attention(q, normed, cross, inner, table, wk, wv, attended)
    update = jnp.dot(attended[...], wo[...], preferred_element_type=F32)
    return (state[...].astype(F32) + update).astype(BF)


def middle_body(splits, state, q, normed, cross, inner, table, wk, wv, wo, gain, halo,
                new_state, new_normed, new_cross, new_inner, *rest):
    edge = halo.shape[1]
    if splits:
        later, attended = rest
        later[...] = cross[edge:]
    else:
        attended, = rest
    moved = attend(state, q, normed, cross[:edge], inner[...], table, wk, wv, wo, attended)
    new_state[...] = moved
    rows = normalised(moved, gain[...])
    new_normed[...] = rows
    picked = picked_rows(rows, halo, parity())
    new_cross[...] = picked[:edge]
    new_inner[...] = picked[edge:]


def last_body(index, state, q, normed, cross, inner, table, wk, wv, wo, out, attended):
    special = lax.axis_index("lead") == index

    @pl.when(special)
    def _():
        out[...] = state[...]

    @pl.when(jnp.logical_not(special))
    def _():
        out[...] = attend(state, q, normed, cross[...], inner[...], table, wk, wv, wo, attended)


def finish_body(here, there, out, sems):
    copies = [pltpu.make_async_copy(x, out.at[0, i], sems.at[i]) for i, x in enumerate((here, there))]
    for copy in copies:
        copy.start()
    for copy in copies:
        copy.wait()


def per_device(states, entering, norm_gain, wq, wk, wv, wo, senders, halo_rows):
    leads, places = lax.axis_size("lead"), lax.axis_size("mesh")
    members, nodes, width = states.shape[1:]
    edge = halo_rows.shape[2]
    gain, halo, senders = norm_gain[None], halo_rows[0], senders.T
    states, entering = (pltpu.with_memory_space_constraint(x, pltpu.HBM) for x in (states, entering))
    vk, vv, vo = wk, wv, wo
    inner_route = [(i, i ^ 1) for i in range(places)]
    cross_route = [
        (a * places + i, ((a + leads // 2) % leads) * places + i if i in (0, places - 1) else a * places + ((i - 1) ^ 1) + 1)
        for a in range(leads)
        for i in range(places)
    ]
    route = [(i, (i + 2) % leads) for i in range(leads)]
    block, rim, rims = shape(nodes, width), shape(edge, width), shape(2 * edge, width)
    dma = pltpu.SemaphoreType.DMA

    def crossed(cross):
        return lax.ppermute(cross, ("lead", "mesh"), cross_route)

    def swapped(inner):
        return lax.ppermute(inner, "mesh", inner_route)

    def project(normed):
        return call(project_body, "project", [normed, vq], [VMEM] * 2, block, VMEM, micros=MP)

    def middle(name, splits, state, q, normed, cross, inner):
        return call(
            functools.partial(middle_body, splits), name,
            [state, q, normed, cross, inner, table, vk, vv, vo, gain, halo], [VMEM] * 11,
            [block, block, rim, rim] + [rim] * splits, [VMEM] * (4 + splits), [pltpu.VMEM((nodes, width), BF)],
        )

    def last(name, index, state, q, normed, cross, inner):
        return call(
            functools.partial(last_body, index), name,
            [state, q, normed, cross, inner, table, vk, vv, vo], [VMEM] * 9,
            block, VMEM, [pltpu.VMEM((nodes, width), BF)], micros=ML,
        )

    far, state1, gain, halo, normed1, cross, inner = call(
        functools.partial(start_body, leads - 2, leads - 1), "start",
        [states, entering] + [pltpu.with_memory_space_constraint(x, pltpu.HBM) for x in (gain, halo)],
        [HBM] * 4,
        [block, block] + [shape(*x.shape, dtype=x.dtype) for x in (gain, halo)] + [block, rims, rim],
        [VMEM] * 7, [dma((5,))],
    )
    cross = crossed(cross)
    inner = swapped(inner)
    q1, vq, table = call(
        project_first_body, "project_first",
        [normed1, pltpu.with_memory_space_constraint(wq, pltpu.HBM), senders], [VMEM, HBM, VMEM],
        [block, shape(width, width), shape(nodes, nodes + 2 * edge, dtype=F32)], [VMEM] * 3, [dma((CHUNKS,))],
        micros=MP,
    )
    far = lax.ppermute(far, "lead", route)
    state1, normed1, cross1, inner1, halo0 = middle("middle_1", True, state1, q1, normed1, cross, inner)
    cross1 = crossed(cross1)
    inner1 = swapped(inner1)
    q1 = project(normed1)
    halo0 = lax.ppermute(halo0, "lead", route)
    near = last("last_1", leads - 2, state1, q1, normed1, cross1, inner1)
    arrived = lax.ppermute(near, "lead", route)
    normed0, inner0 = call(
        far_first_body, "far_first", [far, gain, halo, near], [VMEM] * 3 + [ANY], [block, rim], [VMEM] * 2,
    )
    inner0 = swapped(inner0)
    q0 = project(normed0)
    state0, normed0, cross0, inner0 = middle("middle_0", False, far, q0, normed0, halo0, inner0)
    cross0 = crossed(cross0)
    inner0 = swapped(inner0)
    q0 = project(normed0)
    here = last("last_0", 0, state0, q0, normed0, cross0, inner0)
    return call(
        finish_body, "finish", [here, arrived], [VMEM] * 2,
        shape(1, members, nodes, width), HBM, [dma((2,))],
    )


def solution(mesh):
    P = jax.sharding.PartitionSpec
    in_specs = (
        P("lead", None, "mesh", None),
        P(None, None, "mesh", None),
        P(),
        P(),
        P(),
        P(),
        P(),
        P("mesh", None),
        P("mesh", None, None),
    )
    return jax.shard_map(
        per_device, mesh=mesh, in_specs=in_specs, out_specs=P("lead", None, "mesh", None), check_vma=False
    )
```

time: 44 us -> 43.2 us (0.982)
  the two profiles are of different devices: /device:TPU:1 before, /device:TPU:45 now
where the time goes in v5:
time: 43.2 us; the launch traced here: 43.1 us
  starting transfers between devices  16.9 us (39%)
  Pallas kernels  15.9 us (37%)
  waiting for transfers between devices  9.97 us (23%)
    pallas_call x11, Pallas kernels, call(): pl.pallas_call(body, out_shape=outs, in_specs=specs, out_specs=out_specs,...  15.9 us
    ppermute x3, waiting for transfers between devices, crossed(): return lax.ppermute(cross, ('lead', 'mesh'), cross_route)  9.54 us
    ppermute x3, starting transfers between devices, crossed(): return lax.ppermute(cross, ('lead', 'mesh'), cross_route)  6.17 us
    ppermute x1, starting transfers between devices, per_device(): halo0 = lax.ppermute(halo0, 'lead', route)  3.31 us
    ppermute x1, starting transfers between devices, per_device(): far = lax.ppermute(far, 'lead', route)  2.99 us
    ppermute x1, starting transfers between devices, per_device(): arrived = lax.ppermute(near, 'lead', route)  2.31 us
    ppermute x4, starting transfers between devices, swapped(): return lax.ppermute(inner, 'mesh', inner_route)  2.15 us
  transfers between devices with their start and end apart: 10, of which 3 were waited for; matrix products, arithmetic and copies ran while one was open for 0% of the time, Pallas kernels for 30%

profile of v5, /device:TPU:45, one launch (start us, length us, event | category | flops | bytes accessed | tf_op | source)
XLA Modules:
  0.0 43.1 jit_solution(2116511008602014294)
XLA Ops:
  0.0 2.0 %start.1 = (bf16[128,1024]{1,0:T(8,128)(2,1)S(1)}, bf16[128,1024]{1,0:T(8,128)(2,1)S(1)}, f32[1,1024]{1,0:T(1,128)S(1)}, s32[2,32]{1,0:T(2,128)S(1)}, bf16[128,1...) custom-call(bf16[1,2,128,1024]{3,2,1,0:T(8,128)(2,1)} %states.1, ...), custom_call_target="tpu_custom_call" | custom-call | flops 1000000000 | bytes 1000 | tf_op jit(solution)/shard_map/start/pallas_call | solution.py:28
  2.0 0.0 copy-start
  2.0 2.7 %collective-permute-start.1 = (bf16[64,1024]{1,0:T(8,128)(2,1)S(1)}, bf16[64,1024]{1,0:T(8,128)(2,1)S(1)}, u32[]{:S(2)}, u32[]{:S(2)}) collective-permute-start(bf16[64,1024]{1,0:T(8,128)(2,1)S(1)} %get-tuple-element.32), channel_id=1, source_target_pairs={{0,128},{1,2},{2,1},{3,4},{4,3},{5,6},{6,5},{7,8},{8,7},{9,10},{10... | collective-permute-start | bytes 393224 | tf_op jit(solution)/shard_map/ppermute | solution.py:234
  4.7 0.0 collective-permute-start.2
  4.7 3.0 %collective-permute-start = (bf16[128,1024]{1,0:T(8,128)(2,1)S(1)}, bf16[128,1024]{1,0:T(8,128)(2,1)S(1)}, u32[]{:S(2)}, u32[]{:S(2)}) collective-permute-start(bf16[128,1024]{1,0:T(8,128)(2,1)S(1)} %get-tuple-element.26), channel_id=1, source_target_pairs={{0,32},{16,48},{32,64},{48,80},{64,96},{80,112},{96,128},{112,144}... | collective-permute-start | bytes 786440 | tf_op jit(solution)/shard_map/ppermute | solution.py:271
  7.7 2.0 %project_first.1 = (bf16[128,1024]{1,0:T(8,128)(2,1)S(1)}, bf16[1024,1024]{1,0:T(8,128)(2,1)S(1)}, f32[128,192]{1,0:T(8,128)S(1)}) custom-call(bf16[128,1024]{1,0:T(8,128)(2,1)S(1)} %get-tuple-element.30.normed, bf16[1024,1024]{1,0:T(8,128)(2,1)} %wq.1, s32[8,128]{1,0:T(8,128)S(1)} %bitcast.3), custom_call_target="tpu_custom_call" | custom-call | flops 1000000000 | bytes 1000 | tf_op jit(solution)/shard_map/project_first/pallas_call | solution.py:28
  9.7 0.0 collective-permute-done.2.inner
  9.7 0.0 collective-permute-done.1.cross
  9.8 2.5 %middle_1.1 = (bf16[128,1024]{1,0:T(8,128)(2,1)S(1)}, bf16[128,1024]{1,0:T(8,128)(2,1)S(1)}, bf16[32,1024]{1,0:T(8,128)(2,1)S(1)}, bf16[32,1024]{1,0:T(8,128)(2,1)S(1)}, bf16[32,1024]{1,0:T(8,128)(2,1)S(1)}) custom-call(bf16[128,1024]{1,0:T(8,128)(2,1)S(1)} %get-tuple-element.29.state, bf16[128,1024]{1,0:T(8,128)(2,1)S(1)} %get-tuple-element.31.q, ...), custom_call_target="tpu_custom_call" | custom-call | flops 1000000000 | bytes 1000 | tf_op jit(solution)/shard_map/middle_1/pallas_call | solution.py:28
  12.3 2.4 %collective-permute-start.3 = (bf16[32,1024]{1,0:T(8,128)(2,1)S(1)}, bf16[32,1024]{1,0:T(8,128)(2,1)S(1)}, u32[]{:S(2)}, u32[]{:S(2)}) collective-permute-start(bf16[32,1024]{1,0:T(8,128)(2,1)S(1)} %get-tuple-element.38), channel_id=1, source_target_pairs={{0,128},{1,2},{2,1},{3,4},{4,3},{5,6},{6,5},{7,8},{8,7},{9,10},{10... | collective-permute-start | bytes 196616 | tf_op jit(solution)/shard_map/ppermute | solution.py:234
  14.6 0.0 collective-permute-start.4
  14.6 3.3 %collective-permute-start.5 = (bf16[32,1024]{1,0:T(8,128)(2,1)S(1)}, bf16[32,1024]{1,0:T(8,128)(2,1)S(1)}, u32[]{:S(2)}, u32[]{:S(2)}) collective-permute-start(bf16[32,1024]{1,0:T(8,128)(2,1)S(1)} %get-tuple-element.41), channel_id=1, source_target_pairs={{0,32},{16,48},{32,64},{48,80},{64,96},{80,112},{96,128},{112,144}... | collective-permute-start | bytes 196616 | tf_op jit(solution)/shard_map/ppermute | solution.py:276
  17.9 0.5 %project.3.q = bf16[128,1024]{1,0:T(8,128)(2,1)S(1)} custom-call(bf16[128,1024]{1,0:T(8,128)(2,1)S(1)} %get-tuple-element.36.normed, bf16[1024,1024]{1,0:T(8,128)(2,1)S(1)} %get-tuple-element.37.wq), custom_call_target="tpu_custom_call" | custom-call | flops 1000000000 | bytes 1000 | tf_op jit(solution)/shard_map/project/pallas_call | solution.py:28
  18.4 0.8 %collective-permute-done.3.cross = bf16[32,1024]{1,0:T(8,128)(2,1)S(1)} collective-permute-done((bf16[32,1024]{1,0:T(8,128)(2,1)S(1)}, bf16[32,1024]{1,0:T(8,128)(2,1)S(1)}, u32[]{:S(2)}, u32[]{:S(2)}) %collective-permute-start.3) | collective-permute-done | bytes 65568 | tf_op jit(solution)/shard_map/ppermute | solution.py:234
  19.2 0.0 collective-permute-done.4.inner
  19.2 2.1 %last_1.1.token = bf16[128,1024]{1,0:T(8,128)(2,1)S(1)} custom-call(bf16[128,1024]{1,0:T(8,128)(2,1)S(1)} %get-tuple-element.35.state, bf16[128,1024]{1,0:T(8,128)(2,1)S(1)} %project.3.q, bf16[128,1024]{1,0:T(8,128)(2,1)S(1)} %get-tuple-element.36.normed, bf16[32,1024]{1,0:T(8,128)(2,1)S(1)} %collective-permute-done.3.cross, ...), custom_call_target="tpu_custom_call" | custom-call | flops 1000000000 | bytes 1000 | tf_op jit(solution)/shard_map/last_1/pallas_call | solution.py:28
  21.3 2.3 %collective-permute-start.9 = (bf16[128,1024]{1,0:T(8,128)(2,1)S(1)}, bf16[128,1024]{1,0:T(8,128)(2,1)S(1)}, u32[]{:S(2)}, u32[]{:S(2)}) collective-permute-start(bf16[128,1024]{1,0:T(8,128)(2,1)S(1)} %last_1.1.token), channel_id=1, source_target_pairs={{0,32},{16,48},{32,64},{48,80},{64,96},{80,112},{96,128},{112,144}... | collective-permute-start | bytes 786440 | tf_op jit(solution)/shard_map/ppermute | solution.py:278
  23.6 0.0 collective-permute-done.far.state
  23.6 0.4 far_first.1
  24.0 1.7 %collective-permute-start.6 = (bf16[32,1024]{1,0:T(8,128)(2,1)S(1)}, bf16[32,1024]{1,0:T(8,128)(2,1)S(1)}, u32[]{:S(2)}, u32[]{:S(2)}) collective-permute-start(bf16[32,1024]{1,0:T(8,128)(2,1)S(1)} %get-tuple-element.42), channel_id=1, source_target_pairs={{0,1},{1,0},{2,3},{3,2},{4,5},{5,4},{6,7},{7,6},{8,9},{9,8},{10,11... | collective-permute-start | bytes 196616 | tf_op jit(solution)/shard_map/ppermute | solution.py:237
  25.7 0.5 %project.4.q = bf16[128,1024]{1,0:T(8,128)(2,1)S(1)} custom-call(bf16[128,1024]{1,0:T(8,128)(2,1)S(1)} %get-tuple-element.40.normed, bf16[1024,1024]{1,0:T(8,128)(2,1)S(1)} %get-tuple-element.37.wq), custom_call_target="tpu_custom_call" | custom-call | flops 1000000000 | bytes 1000 | tf_op jit(solution)/shard_map/project/pallas_call | solution.py:28
  26.2 0.0 collective-permute-done.5.cross
  26.2 0.4 collective-permute-done.6.inner
  26.6 2.5 %middle_0.1 = (bf16[128,1024]{1,0:T(8,128)(2,1)S(1)}, bf16[128,1024]{1,0:T(8,128)(2,1)S(1)}, bf16[32,1024]{1,0:T(8,128)(2,1)S(1)}, bf16[32,1024]{1,0:T(8,128)(2,1)S(1)}) custom-call(bf16[128,1024]{1,0:T(8,128)(2,1)S(1)} %collective-permute-done.far.state, bf16[128,1024]{1,0:T(8,128)(2,1)S(1)} %project.4.q, bf16[128,1024]{1,0:T(8,128)(2,1)S(1)} %get-tuple-element.40.normed, ...), custom_call_target="tpu_custom_call" | custom-call | flops 1000000000 | bytes 1000 | tf_op jit(solution)/shard_map/middle_0/pallas_call | solution.py:28
  29.1 1.2 %collective-permute-start.7 = (bf16[32,1024]{1,0:T(8,128)(2,1)S(1)}, bf16[32,1024]{1,0:T(8,128)(2,1)S(1)}, u32[]{:S(2)}, u32[]{:S(2)}) collective-permute-start(bf16[32,1024]{1,0:T(8,128)(2,1)S(1)} %get-tuple-element.45), channel_id=1, source_target_pairs={{0,128},{1,2},{2,1},{3,4},{4,3},{5,6},{6,5},{7,8},{8,7},{9,10},{10... | collective-permute-start | bytes 196616 | tf_op jit(solution)/shard_map/ppermute | solution.py:234
  30.3 0.4 %collective-permute-start.8 = (bf16[32,1024]{1,0:T(8,128)(2,1)S(1)}, bf16[32,1024]{1,0:T(8,128)(2,1)S(1)}, u32[]{:S(2)}, u32[]{:S(2)}) collective-permute-start(bf16[32,1024]{1,0:T(8,128)(2,1)S(1)} %get-tuple-element.46), channel_id=1, source_target_pairs={{0,1},{1,0},{2,3},{3,2},{4,5},{5,4},{6,7},{7,6},{8,9},{9,8},{10,11... | collective-permute-start | bytes 196616 | tf_op jit(solution)/shard_map/ppermute | solution.py:237
  30.7 0.5 %project.5.q = bf16[128,1024]{1,0:T(8,128)(2,1)S(1)} custom-call(bf16[128,1024]{1,0:T(8,128)(2,1)S(1)} %get-tuple-element.44.normed, bf16[1024,1024]{1,0:T(8,128)(2,1)S(1)} %get-tuple-element.37.wq), custom_call_target="tpu_custom_call" | custom-call | flops 1000000000 | bytes 1000 | tf_op jit(solution)/shard_map/project/pallas_call | solution.py:28
  31.2 8.8 %collective-permute-done.7.cross = bf16[32,1024]{1,0:T(8,128)(2,1)S(1)} collective-permute-done((bf16[32,1024]{1,0:T(8,128)(2,1)S(1)}, bf16[32,1024]{1,0:T(8,128)(2,1)S(1)}, u32[]{:S(2)}, u32[]{:S(2)}) %collective-permute-start.7) | collective-permute-done | bytes 65568 | tf_op jit(solution)/shard_map/ppermute | solution.py:234
  40.0 0.0 collective-permute-done.8.inner
  40.0 2.1 %last_0.1.here = bf16[128,1024]{1,0:T(8,128)(2,1)S(1)} custom-call(bf16[128,1024]{1,0:T(8,128)(2,1)S(1)} %get-tuple-element.43.state, bf16[128,1024]{1,0:T(8,128)(2,1)S(1)} %project.5.q, bf16[128,1024]{1,0:T(8,128)(2,1)S(1)} %get-tuple-element.44.normed, bf16[32,1024]{1,0:T(8,128)(2,1)S(1)} %collective-permute-done.7.cross, ...), custom_call_target="tpu_custom_call" | custom-call | flops 1000000000 | bytes 1000 | tf_op jit(solution)/shard_map/last_0/pallas_call | solution.py:28
  42.1 0.0 collective-permute-done.9.there
  42.1 0.8 %finish.1 = bf16[1,2,128,1024]{3,2,1,0:T(8,128)(2,1)} custom-call(bf16[128,1024]{1,0:T(8,128)(2,1)S(1)} %last_0.1.here, bf16[128,1024]{1,0:T(8,128)(2,1)S(1)} %collective-permute-done.9.there), custom_call_target="tpu_custom_call" | custom-call | flops 1000000000 | bytes 1000 | tf_op jit(solution)/shard_map/finish/pallas_call | solution.py:28
  (7 shorter events, 0.0 us)
Async XLA Ops:
  0.0 7.7 %copy-start.3 = (s32[128,8]{0,1:T(8,128)S(1)}, s32[128,8]{0,1:T(8,128)}, u32[]{:S(2)}) copy-start(s32[128,8]{0,1:T(8,128)} %param.16) | copy-start | bytes 12292
  0.0 9.7 %copy-start.1 = (bf16[1024,1024]{1,0:T(8,128)(2,1)S(1)}, bf16[1024,1024]{1,0:T(8,128)(2,1)}, u32[]{:S(2)}) copy-start(bf16[1024,1024]{1,0:T(8,128)(2,1)} %wv.7) | copy-start | bytes 6291460
  0.0 9.7 %copy-start.2 = (bf16[1024,1024]{1,0:T(8,128)(2,1)S(1)}, bf16[1024,1024]{1,0:T(8,128)(2,1)}, u32[]{:S(2)}) copy-start(bf16[1024,1024]{1,0:T(8,128)(2,1)} %wo.7) | copy-start | bytes 6291460
  2.0 7.7 %copy-start = (bf16[1024,1024]{1,0:T(8,128)(2,1)S(1)}, bf16[1024,1024]{1,0:T(8,128)(2,1)}, u32[]{:S(2)}) copy-start(bf16[1024,1024]{1,0:T(8,128)(2,1)} %wk.7) | copy-start | bytes 6291460
  2.0 7.7 %collective-permute-start.1 = (bf16[64,1024]{1,0:T(8,128)(2,1)S(1)}, bf16[64,1024]{1,0:T(8,128)(2,1)S(1)}, u32[]{:S(2)}, u32[]{:S(2)}) collective-permute-start(bf16[64,1024]{1,0:T(8,128)(2,1)S(1)} %get-tuple-element.32), channel_id=1, source_target_pairs={{0,128},{1,2},{2,1},{3,4},{4,3},{5,6},{6,5},{7,8},{8,7},{9,10},{10... | collective-permute-start | bytes 393224 | tf_op jit(solution)/shard_map/ppermute | solution.py:234
  4.7 5.0 %collective-permute-start.2 = (bf16[32,1024]{1,0:T(8,128)(2,1)S(1)}, bf16[32,1024]{1,0:T(8,128)(2,1)S(1)}, u32[]{:S(2)}, u32[]{:S(2)}) collective-permute-start(bf16[32,1024]{1,0:T(8,128)(2,1)S(1)} %get-tuple-element.33), channel_id=1, source_target_pairs={{0,1},{1,0},{2,3},{3,2},{4,5},{5,4},{6,7},{7,6},{8,9},{9,8},{10,11... | collective-permute-start | bytes 196616 | tf_op jit(solution)/shard_map/ppermute | solution.py:237
  4.7 18.9 %collective-permute-start = (bf16[128,1024]{1,0:T(8,128)(2,1)S(1)}, bf16[128,1024]{1,0:T(8,128)(2,1)S(1)}, u32[]{:S(2)}, u32[]{:S(2)}) collective-permute-start(bf16[128,1024]{1,0:T(8,128)(2,1)S(1)} %get-tuple-element.26), channel_id=1, source_target_pairs={{0,32},{16,48},{32,64},{48,80},{64,96},{80,112},{96,128},{112,144}... | collective-permute-start | bytes 786440 | tf_op jit(solution)/shard_map/ppermute | solution.py:271
  12.3 6.9 %collective-permute-start.3 = (bf16[32,1024]{1,0:T(8,128)(2,1)S(1)}, bf16[32,1024]{1,0:T(8,128)(2,1)S(1)}, u32[]{:S(2)}, u32[]{:S(2)}) collective-permute-start(bf16[32,1024]{1,0:T(8,128)(2,1)S(1)} %get-tuple-element.38), channel_id=1, source_target_pairs={{0,128},{1,2},{2,1},{3,4},{4,3},{5,6},{6,5},{7,8},{8,7},{9,10},{10... | collective-permute-start | bytes 196616 | tf_op jit(solution)/shard_map/ppermute | solution.py:234
  14.6 4.5 %collective-permute-start.4 = (bf16[32,1024]{1,0:T(8,128)(2,1)S(1)}, bf16[32,1024]{1,0:T(8,128)(2,1)S(1)}, u32[]{:S(2)}, u32[]{:S(2)}) collective-permute-start(bf16[32,1024]{1,0:T(8,128)(2,1)S(1)} %get-tuple-element.39), channel_id=1, source_target_pairs={{0,1},{1,0},{2,3},{3,2},{4,5},{5,4},{6,7},{7,6},{8,9},{9,8},{10,11... | collective-permute-start | bytes 196616 | tf_op jit(solution)/shard_map/ppermute | solution.py:237
  14.6 11.5 %collective-permute-start.5 = (bf16[32,1024]{1,0:T(8,128)(2,1)S(1)}, bf16[32,1024]{1,0:T(8,128)(2,1)S(1)}, u32[]{:S(2)}, u32[]{:S(2)}) collective-permute-start(bf16[32,1024]{1,0:T(8,128)(2,1)S(1)} %get-tuple-element.41), channel_id=1, source_target_pairs={{0,32},{16,48},{32,64},{48,80},{64,96},{80,112},{96,128},{112,144}... | collective-permute-start | bytes 196616 | tf_op jit(solution)/shard_map/ppermute | solution.py:276
  21.3 20.8 %collective-permute-start.9 = (bf16[128,1024]{1,0:T(8,128)(2,1)S(1)}, bf16[128,1024]{1,0:T(8,128)(2,1)S(1)}, u32[]{:S(2)}, u32[]{:S(2)}) collective-permute-start(bf16[128,1024]{1,0:T(8,128)(2,1)S(1)} %last_1.1.token), channel_id=1, source_target_pairs={{0,32},{16,48},{32,64},{48,80},{64,96},{80,112},{96,128},{112,144}... | collective-permute-start | bytes 786440 | tf_op jit(solution)/shard_map/ppermute | solution.py:278
  24.0 2.6 %collective-permute-start.6 = (bf16[32,1024]{1,0:T(8,128)(2,1)S(1)}, bf16[32,1024]{1,0:T(8,128)(2,1)S(1)}, u32[]{:S(2)}, u32[]{:S(2)}) collective-permute-start(bf16[32,1024]{1,0:T(8,128)(2,1)S(1)} %get-tuple-element.42), channel_id=1, source_target_pairs={{0,1},{1,0},{2,3},{3,2},{4,5},{5,4},{6,7},{7,6},{8,9},{9,8},{10,11... | collective-permute-start | bytes 196616 | tf_op jit(solution)/shard_map/ppermute | solution.py:237
  29.1 10.9 %collective-permute-start.7 = (bf16[32,1024]{1,0:T(8,128)(2,1)S(1)}, bf16[32,1024]{1,0:T(8,128)(2,1)S(1)}, u32[]{:S(2)}, u32[]{:S(2)}) collective-permute-start(bf16[32,1024]{1,0:T(8,128)(2,1)S(1)} %get-tuple-element.45), channel_id=1, source_target_pairs={{0,128},{1,2},{2,1},{3,4},{4,3},{5,6},{6,5},{7,8},{8,7},{9,10},{10... | collective-permute-start | bytes 196616 | tf_op jit(solution)/shard_map/ppermute | solution.py:234
  30.3 9.7 %collective-permute-start.8 = (bf16[32,1024]{1,0:T(8,128)(2,1)S(1)}, bf16[32,1024]{1,0:T(8,128)(2,1)S(1)}, u32[]{:S(2)}, u32[]{:S(2)}) collective-permute-start(bf16[32,1024]{1,0:T(8,128)(2,1)S(1)} %get-tuple-element.46), channel_id=1, source_target_pairs={{0,1},{1,0},{2,3},{3,2},{4,5},{5,4},{6,7},{7,6},{8,9},{9,8},{10,11... | collective-permute-start | bytes 196616 | tf_op jit(solution)/shard_map/ppermute | solution.py:237

commit v6 on v5

--- a/solution.py
+++ b/solution.py
@@ -11,7 +11,7 @@
 NEVER = -1e30
 BF = jnp.bfloat16
 F32 = jnp.float32
-CHUNKS = 4
+MS = 3.0
 MP = 1.0
 ML = 1.0
 VMEM_BYTES = 16 * 1024 * 1024
@@ -124,17 +124,9 @@
         copy.wait()
 
 
-def project_first_body(normed, wq, senders, q, vq, table, sems):
-    depth = wq.shape[0] // CHUNKS
-    copies = []
-    for i in range(CHUNKS):
-        at = pl.ds(i * depth, depth)
-        copies.append(pltpu.make_async_copy(wq.at[at], vq.at[at], sems.at[i]))
-        copies[-1].start()
+def project_first_body(normed, wq, senders, q, table):
     bias_table(senders, parity(), table)
-    for copy in copies:
-        copy.wait()
-    q[...] = queries_of(normed[...], vq[...])
+    q[...] = queries_of(normed[...], wq[...])
 
 
 def project_body(normed, wq, q):
@@ -219,7 +211,7 @@
     edge = halo_rows.shape[2]
     gain, halo, senders = norm_gain[None], halo_rows[0], senders.T
     states, entering = (pltpu.with_memory_space_constraint(x, pltpu.HBM) for x in (states, entering))
-    vk, vv, vo = wk, wv, wo
+    vq, vk, vv, vo = wq, wk, wv, wo
     inner_route = [(i, i ^ 1) for i in range(places)]
     cross_route = [
         (a * places + i, ((a + leads // 2) % leads) * places + i if i in (0, places - 1) else a * places + ((i - 1) ^ 1) + 1)
@@ -258,15 +250,13 @@
         [states, entering] + [pltpu.with_memory_space_constraint(x, pltpu.HBM) for x in (gain, halo)],
         [HBM] * 4,
         [block, block] + [shape(*x.shape, dtype=x.dtype) for x in (gain, halo)] + [block, rims, rim],
-        [VMEM] * 7, [dma((5,))],
+        [VMEM] * 7, [dma((5,))], micros=MS,
     )
     cross = crossed(cross)
     inner = swapped(inner)
-    q1, vq, table = call(
-        project_first_body, "project_first",
-        [normed1, pltpu.with_memory_space_constraint(wq, pltpu.HBM), senders], [VMEM, HBM, VMEM],
-        [block, shape(width, width), shape(nodes, nodes + 2 * edge, dtype=F32)], [VMEM] * 3, [dma((CHUNKS,))],
-        micros=MP,
+    q1, table = call(
+        project_first_body, "project_first", [normed1, vq, senders], [VMEM] * 3,
+        [block, shape(nodes, nodes + 2 * edge, dtype=F32)], [VMEM] * 2, micros=MP,
     )
     far = lax.ppermute(far, "lead", route)
     state1, normed1, cross1, inner1, halo0 = middle("middle_1", True, state1, q1, normed1, cross, inner)

time: 43.2 us -> 42.8 us (level)
  Pallas kernels: 15.9 us -> 14.3 us
  waiting for transfers between devices: 9.97 us -> 11.2 us
    pallas_call x11, Pallas kernels: 15.9 us -> 14.3 us  [call(): pl.pallas_call(body, out_shape=outs, in_specs=specs, out_specs=out_specs,...]
    ppermute x3, waiting for transfers between devices: 9.54 us -> 10.8 us  [crossed(): return lax.ppermute(cross, ('lead', 'mesh'), cross_route)]
    ppermute x3, starting transfers between devices: 6.17 us -> 7.05 us  [crossed(): return lax.ppermute(cross, ('lead', 'mesh'), cross_route)]
    ppermute x4, starting transfers between devices: 2.15 us -> 1.47 us  [swapped(): return lax.ppermute(inner, 'mesh', inner_route)]
  transfers between devices with their start and end apart: 10 -> 10, of which waited for: 3 -> 4; matrix products, arithmetic and copies ran while one was open for 0% -> 0% of each run, Pallas kernels for 30% -> 27%
where the time goes in v6:
time: 42.8 us
  starting transfers between devices  16.9 us (39%)
  Pallas kernels  14.3 us (33%)
  waiting for transfers between devices  11.2 us (26%)
    pallas_call x11, Pallas kernels, call(): pl.pallas_call(body, out_shape=outs, in_specs=specs, out_specs=out_specs,...  14.3 us
    ppermute x3, waiting for transfers between devices, crossed(): return lax.ppermute(cross, ('lead', 'mesh'), cross_route)  10.8 us
    ppermute x3, starting transfers between devices, crossed(): return lax.ppermute(cross, ('lead', 'mesh'), cross_route)  7.05 us
    ppermute x1, starting transfers between devices, per_device(): far = lax.ppermute(far, 'lead', route)  2.99 us
    ppermute x1, starting transfers between devices, per_device(): halo0 = lax.ppermute(halo0, 'lead', route)  2.99 us
    ppermute x1, starting transfers between devices, per_device(): arrived = lax.ppermute(near, 'lead', route)  2.41 us
    ppermute x4, starting transfers between devices, swapped(): return lax.ppermute(inner, 'mesh', inner_route)  1.47 us
  transfers between devices with their start and end apart: 10, of which 4 were waited for; matrix products, arithmetic and copies ran while one was open for 0% of the time, Pallas kernels for 27%

profile of v6, /device:TPU:45, one launch (start us, length us, event | category | flops | bytes accessed | tf_op | source)
XLA Modules:
  0.0 42.8 jit_solution(13967118801473968071)
XLA Ops:
  0.0 2.0 %start.1 = (bf16[128,1024]{1,0:T(8,128)(2,1)S(1)}, bf16[128,1024]{1,0:T(8,128)(2,1)S(1)}, f32[1,1024]{1,0:T(1,128)S(1)}, s32[2,32]{1,0:T(2,128)S(1)}, bf16[128,1...) custom-call(bf16[1,2,128,1024]{3,2,1,0:T(8,128)(2,1)} %states.1, ...), custom_call_target="tpu_custom_call" | custom-call | flops 3000000000 | bytes 1000 | tf_op jit(solution)/shard_map/start/pallas_call | solution.py:28
  2.0 0.0 copy-start
  2.0 2.7 %collective-permute-start.1 = (bf16[64,1024]{1,0:T(8,128)(2,1)S(1)}, bf16[64,1024]{1,0:T(8,128)(2,1)S(1)}, u32[]{:S(2)}, u32[]{:S(2)}) collective-permute-start(bf16[64,1024]{1,0:T(8,128)(2,1)S(1)} %get-tuple-element.31), channel_id=1, source_target_pairs={{0,128},{1,2},{2,1},{3,4},{4,3},{5,6},{6,5},{7,8},{8,7},{9,10},{10... | collective-permute-start | bytes 393224 | tf_op jit(solution)/shard_map/ppermute | solution.py:226
  4.7 0.0 collective-permute-start.2
  4.7 3.0 %collective-permute-start = (bf16[128,1024]{1,0:T(8,128)(2,1)S(1)}, bf16[128,1024]{1,0:T(8,128)(2,1)S(1)}, u32[]{:S(2)}, u32[]{:S(2)}) collective-permute-start(bf16[128,1024]{1,0:T(8,128)(2,1)S(1)} %get-tuple-element.25), channel_id=1, source_target_pairs={{0,32},{16,48},{32,64},{48,80},{64,96},{80,112},{96,128},{112,144}... | collective-permute-start | bytes 786440 | tf_op jit(solution)/shard_map/ppermute | solution.py:261
  7.7 0.5 %project_first.1 = (bf16[128,1024]{1,0:T(8,128)(2,1)S(1)}, f32[128,192]{1,0:T(8,128)S(1)}) custom-call(bf16[128,1024]{1,0:T(8,128)(2,1)S(1)} %get-tuple-element.29.normed, bf16[1024,1024]{1,0:T(8,128)(2,1)S(1)} %copy-done.3, s32[8,128]{1,0:T(8,128)S(1)} %bitcast.3), custom_call_target="tpu_custom_call" | custom-call | flops 1000000000 | bytes 1000 | tf_op jit(solution)/shard_map/project_first/pallas_call | solution.py:28
  8.2 0.0 collective-permute-done.2.inner
  8.2 1.2 %collective-permute-done.1.cross = bf16[64,1024]{1,0:T(8,128)(2,1)S(1)} collective-permute-done((bf16[64,1024]{1,0:T(8,128)(2,1)S(1)}, bf16[64,1024]{1,0:T(8,128)(2,1)S(1)}, u32[]{:S(2)}, u32[]{:S(2)}) %collective-permute-start.1) | collective-permute-done | bytes 131104 | tf_op jit(solution)/shard_map/ppermute | solution.py:226
  9.4 2.5 %middle_1.1 = (bf16[128,1024]{1,0:T(8,128)(2,1)S(1)}, bf16[128,1024]{1,0:T(8,128)(2,1)S(1)}, bf16[32,1024]{1,0:T(8,128)(2,1)S(1)}, bf16[32,1024]{1,0:T(8,128)(2,1)S(1)}, bf16[32,1024]{1,0:T(8,128)(2,1)S(1)}) custom-call(bf16[128,1024]{1,0:T(8,128)(2,1)S(1)} %get-tuple-element.28.state, bf16[128,1024]{1,0:T(8,128)(2,1)S(1)} %get-tuple-element.30.q, ...), custom_call_target="tpu_custom_call" | custom-call | flops 1000000000 | bytes 1000 | tf_op jit(solution)/shard_map/middle_1/pallas_call | solution.py:28
  12.0 2.7 %collective-permute-start.3 = (bf16[32,1024]{1,0:T(8,128)(2,1)S(1)}, bf16[32,1024]{1,0:T(8,128)(2,1)S(1)}, u32[]{:S(2)}, u32[]{:S(2)}) collective-permute-start(bf16[32,1024]{1,0:T(8,128)(2,1)S(1)} %get-tuple-element.36), channel_id=1, source_target_pairs={{0,128},{1,2},{2,1},{3,4},{4,3},{5,6},{6,5},{7,8},{8,7},{9,10},{10... | collective-permute-start | bytes 196616 | tf_op jit(solution)/shard_map/ppermute | solution.py:226
  14.6 0.0 collective-permute-start.4
  14.6 3.0 %collective-permute-start.5 = (bf16[32,1024]{1,0:T(8,128)(2,1)S(1)}, bf16[32,1024]{1,0:T(8,128)(2,1)S(1)}, u32[]{:S(2)}, u32[]{:S(2)}) collective-permute-start(bf16[32,1024]{1,0:T(8,128)(2,1)S(1)} %get-tuple-element.39), channel_id=1, source_target_pairs={{0,32},{16,48},{32,64},{48,80},{64,96},{80,112},{96,128},{112,144}... | collective-permute-start | bytes 196616 | tf_op jit(solution)/shard_map/ppermute | solution.py:266
  17.6 0.5 %project.3.q = bf16[128,1024]{1,0:T(8,128)(2,1)S(1)} custom-call(bf16[128,1024]{1,0:T(8,128)(2,1)S(1)} %get-tuple-element.35.normed, bf16[1024,1024]{1,0:T(8,128)(2,1)S(1)} %copy-done.3), custom_call_target="tpu_custom_call" | custom-call | flops 1000000000 | bytes 1000 | tf_op jit(solution)/shard_map/project/pallas_call | solution.py:28
  18.1 1.1 %collective-permute-done.3.cross = bf16[32,1024]{1,0:T(8,128)(2,1)S(1)} collective-permute-done((bf16[32,1024]{1,0:T(8,128)(2,1)S(1)}, bf16[32,1024]{1,0:T(8,128)(2,1)S(1)}, u32[]{:S(2)}, u32[]{:S(2)}) %collective-permute-start.3) | collective-permute-done | bytes 65568 | tf_op jit(solution)/shard_map/ppermute | solution.py:226
  19.2 0.0 collective-permute-done.4.inner
  19.2 2.1 %last_1.1.token = bf16[128,1024]{1,0:T(8,128)(2,1)S(1)} custom-call(bf16[128,1024]{1,0:T(8,128)(2,1)S(1)} %get-tuple-element.34.state, bf16[128,1024]{1,0:T(8,128)(2,1)S(1)} %project.3.q, bf16[128,1024]{1,0:T(8,128)(2,1)S(1)} %get-tuple-element.35.normed, bf16[32,1024]{1,0:T(8,128)(2,1)S(1)} %collective-permute-done.3.cross, ...), custom_call_target="tpu_custom_call" | custom-call | flops 1000000000 | bytes 1000 | tf_op jit(solution)/shard_map/last_1/pallas_call | solution.py:28
  21.3 2.4 %collective-permute-start.9 = (bf16[128,1024]{1,0:T(8,128)(2,1)S(1)}, bf16[128,1024]{1,0:T(8,128)(2,1)S(1)}, u32[]{:S(2)}, u32[]{:S(2)}) collective-permute-start(bf16[128,1024]{1,0:T(8,128)(2,1)S(1)} %last_1.1.token), channel_id=1, source_target_pairs={{0,32},{16,48},{32,64},{48,80},{64,96},{80,112},{96,128},{112,144}... | collective-permute-start | bytes 786440 | tf_op jit(solution)/shard_map/ppermute | solution.py:268
  23.7 0.0 collective-permute-done.far.state
  23.7 0.4 far_first.1
  24.1 1.2 %collective-permute-start.6 = (bf16[32,1024]{1,0:T(8,128)(2,1)S(1)}, bf16[32,1024]{1,0:T(8,128)(2,1)S(1)}, u32[]{:S(2)}, u32[]{:S(2)}) collective-permute-start(bf16[32,1024]{1,0:T(8,128)(2,1)S(1)} %get-tuple-element.40), channel_id=1, source_target_pairs={{0,1},{1,0},{2,3},{3,2},{4,5},{5,4},{6,7},{7,6},{8,9},{9,8},{10,11... | collective-permute-start | bytes 196616 | tf_op jit(solution)/shard_map/ppermute | solution.py:229
  25.4 0.5 %project.4.q = bf16[128,1024]{1,0:T(8,128)(2,1)S(1)} custom-call(bf16[128,1024]{1,0:T(8,128)(2,1)S(1)} %get-tuple-element.38.normed, bf16[1024,1024]{1,0:T(8,128)(2,1)S(1)} %copy-done.3), custom_call_target="tpu_custom_call" | custom-call | flops 1000000000 | bytes 1000 | tf_op jit(solution)/shard_map/project/pallas_call | solution.py:28
  25.8 0.0 collective-permute-done.5.cross
  25.8 0.4 collective-permute-done.6.inner
  26.3 2.5 %middle_0.1 = (bf16[128,1024]{1,0:T(8,128)(2,1)S(1)}, bf16[128,1024]{1,0:T(8,128)(2,1)S(1)}, bf16[32,1024]{1,0:T(8,128)(2,1)S(1)}, bf16[32,1024]{1,0:T(8,128)(2,1)S(1)}) custom-call(bf16[128,1024]{1,0:T(8,128)(2,1)S(1)} %collective-permute-done.far.state, bf16[128,1024]{1,0:T(8,128)(2,1)S(1)} %project.4.q, bf16[128,1024]{1,0:T(8,128)(2,1)S(1)} %get-tuple-element.38.normed, ...), custom_call_target="tpu_custom_call" | custom-call | flops 1000000000 | bytes 1000 | tf_op jit(solution)/shard_map/middle_0/pallas_call | solution.py:28
  28.8 1.7 %collective-permute-start.7 = (bf16[32,1024]{1,0:T(8,128)(2,1)S(1)}, bf16[32,1024]{1,0:T(8,128)(2,1)S(1)}, u32[]{:S(2)}, u32[]{:S(2)}) collective-permute-start(bf16[32,1024]{1,0:T(8,128)(2,1)S(1)} %get-tuple-element.43), channel_id=1, source_target_pairs={{0,128},{1,2},{2,1},{3,4},{4,3},{5,6},{6,5},{7,8},{8,7},{9,10},{10... | collective-permute-start | bytes 196616 | tf_op jit(solution)/shard_map/ppermute | solution.py:226
  30.5 0.2 collective-permute-start.8
  30.7 0.5 %project.5.q = bf16[128,1024]{1,0:T(8,128)(2,1)S(1)} custom-call(bf16[128,1024]{1,0:T(8,128)(2,1)S(1)} %get-tuple-element.42.normed, bf16[1024,1024]{1,0:T(8,128)(2,1)S(1)} %copy-done.3), custom_call_target="tpu_custom_call" | custom-call | flops 1000000000 | bytes 1000 | tf_op jit(solution)/shard_map/project/pallas_call | solution.py:28
  31.2 8.4 %collective-permute-done.7.cross = bf16[32,1024]{1,0:T(8,128)(2,1)S(1)} collective-permute-done((bf16[32,1024]{1,0:T(8,128)(2,1)S(1)}, bf16[32,1024]{1,0:T(8,128)(2,1)S(1)}, u32[]{:S(2)}, u32[]{:S(2)}) %collective-permute-start.7) | collective-permute-done | bytes 65568 | tf_op jit(solution)/shard_map/ppermute | solution.py:226
  39.6 0.0 collective-permute-done.8.inner
  39.6 2.1 %last_0.1.here = bf16[128,1024]{1,0:T(8,128)(2,1)S(1)} custom-call(bf16[128,1024]{1,0:T(8,128)(2,1)S(1)} %get-tuple-element.41.state, bf16[128,1024]{1,0:T(8,128)(2,1)S(1)} %project.5.q, bf16[128,1024]{1,0:T(8,128)(2,1)S(1)} %get-tuple-element.42.normed, bf16[32,1024]{1,0:T(8,128)(2,1)S(1)} %collective-permute-done.7.cross, ...), custom_call_target="tpu_custom_call" | custom-call | flops 1000000000 | bytes 1000 | tf_op jit(solution)/shard_map/last_0/pallas_call | solution.py:28
  41.8 0.0 collective-permute-done.9.there
  41.8 0.8 %finish.1 = bf16[1,2,128,1024]{3,2,1,0:T(8,128)(2,1)} custom-call(bf16[128,1024]{1,0:T(8,128)(2,1)S(1)} %last_0.1.here, bf16[128,1024]{1,0:T(8,128)(2,1)S(1)} %collective-permute-done.9.there), custom_call_target="tpu_custom_call" | custom-call | flops 1000000000 | bytes 1000 | tf_op jit(solution)/shard_map/finish/pallas_call | solution.py:28
  (9 shorter events, 0.0 us)
Async XLA Ops:
  0.0 7.7 %copy-start.3 = (bf16[1024,1024]{1,0:T(8,128)(2,1)S(1)}, bf16[1024,1024]{1,0:T(8,128)(2,1)}, u32[]{:S(2)}) copy-start(bf16[1024,1024]{1,0:T(8,128)(2,1)} %wq.7) | copy-start | bytes 6291460
  0.0 7.7 %copy-start.4 = (s32[128,8]{0,1:T(8,128)S(1)}, s32[128,8]{0,1:T(8,128)}, u32[]{:S(2)}) copy-start(s32[128,8]{0,1:T(8,128)} %param.16) | copy-start | bytes 12292
  0.0 9.4 %copy-start.1 = (bf16[1024,1024]{1,0:T(8,128)(2,1)S(1)}, bf16[1024,1024]{1,0:T(8,128)(2,1)}, u32[]{:S(2)}) copy-start(bf16[1024,1024]{1,0:T(8,128)(2,1)} %wv.7) | copy-start | bytes 6291460
  0.0 9.4 %copy-start.2 = (bf16[1024,1024]{1,0:T(8,128)(2,1)S(1)}, bf16[1024,1024]{1,0:T(8,128)(2,1)}, u32[]{:S(2)}) copy-start(bf16[1024,1024]{1,0:T(8,128)(2,1)} %wo.7) | copy-start | bytes 6291460
  2.0 7.4 %copy-start = (bf16[1024,1024]{1,0:T(8,128)(2,1)S(1)}, bf16[1024,1024]{1,0:T(8,128)(2,1)}, u32[]{:S(2)}) copy-start(bf16[1024,1024]{1,0:T(8,128)(2,1)} %wk.7) | copy-start | bytes 6291460
  2.0 7.4 %collective-permute-start.1 = (bf16[64,1024]{1,0:T(8,128)(2,1)S(1)}, bf16[64,1024]{1,0:T(8,128)(2,1)S(1)}, u32[]{:S(2)}, u32[]{:S(2)}) collective-permute-start(bf16[64,1024]{1,0:T(8,128)(2,1)S(1)} %get-tuple-element.31), channel_id=1, source_target_pairs={{0,128},{1,2},{2,1},{3,4},{4,3},{5,6},{6,5},{7,8},{8,7},{9,10},{10... | collective-permute-start | bytes 393224 | tf_op jit(solution)/shard_map/ppermute | solution.py:226
  4.7 3.5 %collective-permute-start.2 = (bf16[32,1024]{1,0:T(8,128)(2,1)S(1)}, bf16[32,1024]{1,0:T(8,128)(2,1)S(1)}, u32[]{:S(2)}, u32[]{:S(2)}) collective-permute-start(bf16[32,1024]{1,0:T(8,128)(2,1)S(1)} %get-tuple-element.32), channel_id=1, source_target_pairs={{0,1},{1,0},{2,3},{3,2},{4,5},{5,4},{6,7},{7,6},{8,9},{9,8},{10,11... | collective-permute-start | bytes 196616 | tf_op jit(solution)/shard_map/ppermute | solution.py:229
  4.7 19.0 %collective-permute-start = (bf16[128,1024]{1,0:T(8,128)(2,1)S(1)}, bf16[128,1024]{1,0:T(8,128)(2,1)S(1)}, u32[]{:S(2)}, u32[]{:S(2)}) collective-permute-start(bf16[128,1024]{1,0:T(8,128)(2,1)S(1)} %get-tuple-element.25), channel_id=1, source_target_pairs={{0,32},{16,48},{32,64},{48,80},{64,96},{80,112},{96,128},{112,144}... | collective-permute-start | bytes 786440 | tf_op jit(solution)/shard_map/ppermute | solution.py:261
  12.0 7.2 %collective-permute-start.3 = (bf16[32,1024]{1,0:T(8,128)(2,1)S(1)}, bf16[32,1024]{1,0:T(8,128)(2,1)S(1)}, u32[]{:S(2)}, u32[]{:S(2)}) collective-permute-start(bf16[32,1024]{1,0:T(8,128)(2,1)S(1)} %get-tuple-element.36), channel_id=1, source_target_pairs={{0,128},{1,2},{2,1},{3,4},{4,3},{5,6},{6,5},{7,8},{8,7},{9,10},{10... | collective-permute-start | bytes 196616 | tf_op jit(solution)/shard_map/ppermute | solution.py:226
  14.6 4.6 %collective-permute-start.4 = (bf16[32,1024]{1,0:T(8,128)(2,1)S(1)}, bf16[32,1024]{1,0:T(8,128)(2,1)S(1)}, u32[]{:S(2)}, u32[]{:S(2)}) collective-permute-start(bf16[32,1024]{1,0:T(8,128)(2,1)S(1)} %get-tuple-element.37), channel_id=1, source_target_pairs={{0,1},{1,0},{2,3},{3,2},{4,5},{5,4},{6,7},{7,6},{8,9},{9,8},{10,11... | collective-permute-start | bytes 196616 | tf_op jit(solution)/shard_map/ppermute | solution.py:229
  14.6 11.2 %collective-permute-start.5 = (bf16[32,1024]{1,0:T(8,128)(2,1)S(1)}, bf16[32,1024]{1,0:T(8,128)(2,1)S(1)}, u32[]{:S(2)}, u32[]{:S(2)}) collective-permute-start(bf16[32,1024]{1,0:T(8,128)(2,1)S(1)} %get-tuple-element.39), channel_id=1, source_target_pairs={{0,32},{16,48},{32,64},{48,80},{64,96},{80,112},{96,128},{112,144}... | collective-permute-start | bytes 196616 | tf_op jit(solution)/shard_map/ppermute | solution.py:266
  21.3 20.5 %collective-permute-start.9 = (bf16[128,1024]{1,0:T(8,128)(2,1)S(1)}, bf16[128,1024]{1,0:T(8,128)(2,1)S(1)}, u32[]{:S(2)}, u32[]{:S(2)}) collective-permute-start(bf16[128,1024]{1,0:T(8,128)(2,1)S(1)} %last_1.1.token), channel_id=1, source_target_pairs={{0,32},{16,48},{32,64},{48,80},{64,96},{80,112},{96,128},{112,144}... | collective-permute-start | bytes 786440 | tf_op jit(solution)/shard_map/ppermute | solution.py:268
  24.1 2.2 %collective-permute-start.6 = (bf16[32,1024]{1,0:T(8,128)(2,1)S(1)}, bf16[32,1024]{1,0:T(8,128)(2,1)S(1)}, u32[]{:S(2)}, u32[]{:S(2)}) collective-permute-start(bf16[32,1024]{1,0:T(8,128)(2,1)S(1)} %get-tuple-element.40), channel_id=1, source_target_pairs={{0,1},{1,0},{2,3},{3,2},{4,5},{5,4},{6,7},{7,6},{8,9},{9,8},{10,11... | collective-permute-start | bytes 196616 | tf_op jit(solution)/shard_map/ppermute | solution.py:229
  28.8 10.9 %collective-permute-start.7 = (bf16[32,1024]{1,0:T(8,128)(2,1)S(1)}, bf16[32,1024]{1,0:T(8,128)(2,1)S(1)}, u32[]{:S(2)}, u32[]{:S(2)}) collective-permute-start(bf16[32,1024]{1,0:T(8,128)(2,1)S(1)} %get-tuple-element.43), channel_id=1, source_target_pairs={{0,128},{1,2},{2,1},{3,4},{4,3},{5,6},{6,5},{7,8},{8,7},{9,10},{10... | collective-permute-start | bytes 196616 | tf_op jit(solution)/shard_map/ppermute | solution.py:226
  30.5 9.1 %collective-permute-start.8 = (bf16[32,1024]{1,0:T(8,128)(2,1)S(1)}, bf16[32,1024]{1,0:T(8,128)(2,1)S(1)}, u32[]{:S(2)}, u32[]{:S(2)}) collective-permute-start(bf16[32,1024]{1,0:T(8,128)(2,1)S(1)} %get-tuple-element.44), channel_id=1, source_target_pairs={{0,1},{1,0},{2,3},{3,2},{4,5},{5,4},{6,7},{7,6},{8,9},{9,8},{10,11... | collective-permute-start | bytes 196616 | tf_op jit(solution)/shard_map/ppermute | solution.py:229

commit v7 on v6

--- a/solution.py
+++ b/solution.py
@@ -126,6 +126,11 @@
 
 def project_first_body(normed, wq, senders, q, table):
     bias_table(senders, parity(), table)
+    q[...] = queries_of(normed[...], wq[...])
+
+
+def project_pass_body(normed, wq, inner, q, passed):
+    passed[...] = inner[...]
     q[...] = queries_of(normed[...], wq[...])
 
 
@@ -231,6 +236,11 @@
     def project(normed):
         return call(project_body, "project", [normed, vq], [VMEM] * 2, block, VMEM, micros=MP)
 
+    def project_pass(normed, inner):
+        return call(
+            project_pass_body, "project", [normed, vq, inner], [VMEM] * 3, [block, rim], [VMEM] * 2, micros=MP,
+        )
+
     def middle(name, splits, state, q, normed, cross, inner):
         return call(
             functools.partial(middle_body, splits), name,
@@ -262,7 +272,7 @@
     state1, normed1, cross1, inner1, halo0 = middle("middle_1", True, state1, q1, normed1, cross, inner)
     cross1 = crossed(cross1)
     inner1 = swapped(inner1)
-    q1 = project(normed1)
+    q1, halo0 = project_pass(normed1, halo0)
     halo0 = lax.ppermute(halo0, "lead", route)
     near = last("last_1", leads - 2, state1, q1, normed1, cross1, inner1)
     arrived = lax.ppermute(near, "lead", route)

time: 42.8 us -> 42.3 us (0.988)
  waiting for transfers between devices: 11.2 us -> 10.7 us
    ppermute x3, waiting for transfers between devices: 10.8 us -> 10.3 us  [crossed(): return lax.ppermute(cross, ('lead', 'mesh'), cross_route)]
where the time goes in v7:
time: 42.3 us; the launch traced here: 42.2 us
  starting transfers between devices  17 us (40%)
  Pallas kernels  14.2 us (34%)
  waiting for transfers between devices  10.7 us (25%)
    pallas_call x11, Pallas kernels, call(): pl.pallas_call(body, out_shape=outs, in_specs=specs, out_specs=out_specs,...  14.2 us
    ppermute x3, waiting for transfers between devices, crossed(): return lax.ppermute(cross, ('lead', 'mesh'), cross_route)  10.3 us
    ppermute x3, starting transfers between devices, crossed(): return lax.ppermute(cross, ('lead', 'mesh'), cross_route)  7.03 us
    ppermute x1, starting transfers between devices, per_device(): halo0 = lax.ppermute(halo0, 'lead', route)  3.07 us
    ppermute x1, starting transfers between devices, per_device(): far = lax.ppermute(far, 'lead', route)  2.99 us
    ppermute x1, starting transfers between devices, per_device(): arrived = lax.ppermute(near, 'lead', route)  2.4 us
    ppermute x4, starting transfers between devices, swapped(): return lax.ppermute(inner, 'mesh', inner_route)  1.51 us
  transfers between devices with their start and end apart: 10, of which 4 were waited for; matrix products, arithmetic and copies ran while one was open for 0% of the time, Pallas kernels for 27%

profile of v7, /device:TPU:45, one launch (start us, length us, event | category | flops | bytes accessed | tf_op | source)
XLA Modules:
  0.0 42.2 jit_solution(15915628985615368703)
XLA Ops:
  0.0 2.0 %start.1 = (bf16[128,1024]{1,0:T(8,128)(2,1)S(1)}, bf16[128,1024]{1,0:T(8,128)(2,1)S(1)}, f32[1,1024]{1,0:T(1,128)S(1)}, s32[2,32]{1,0:T(2,128)S(1)}, bf16[128,1...) custom-call(bf16[1,2,128,1024]{3,2,1,0:T(8,128)(2,1)} %states.1, ...), custom_call_target="tpu_custom_call" | custom-call | flops 3000000000 | bytes 1000 | tf_op jit(solution)/shard_map/start/pallas_call | solution.py:28
  2.0 0.0 copy-start
  2.0 2.7 %collective-permute-start.1 = (bf16[64,1024]{1,0:T(8,128)(2,1)S(1)}, bf16[64,1024]{1,0:T(8,128)(2,1)S(1)}, u32[]{:S(2)}, u32[]{:S(2)}) collective-permute-start(bf16[64,1024]{1,0:T(8,128)(2,1)S(1)} %get-tuple-element.33), channel_id=1, source_target_pairs={{0,128},{1,2},{2,1},{3,4},{4,3},{5,6},{6,5},{7,8},{8,7},{9,10},{10... | collective-permute-start | bytes 393224 | tf_op jit(solution)/shard_map/ppermute | solution.py:231
  4.7 0.0 collective-permute-start.2
  4.7 3.0 %collective-permute-start = (bf16[128,1024]{1,0:T(8,128)(2,1)S(1)}, bf16[128,1024]{1,0:T(8,128)(2,1)S(1)}, u32[]{:S(2)}, u32[]{:S(2)}) collective-permute-start(bf16[128,1024]{1,0:T(8,128)(2,1)S(1)} %get-tuple-element.27), channel_id=1, source_target_pairs={{0,32},{16,48},{32,64},{48,80},{64,96},{80,112},{96,128},{112,144}... | collective-permute-start | bytes 786440 | tf_op jit(solution)/shard_map/ppermute | solution.py:271
  7.7 0.5 %project_first.1 = (bf16[128,1024]{1,0:T(8,128)(2,1)S(1)}, f32[128,192]{1,0:T(8,128)S(1)}) custom-call(bf16[128,1024]{1,0:T(8,128)(2,1)S(1)} %get-tuple-element.31.normed, bf16[1024,1024]{1,0:T(8,128)(2,1)S(1)} %copy-done.3, s32[8,128]{1,0:T(8,128)S(1)} %bitcast.3), custom_call_target="tpu_custom_call" | custom-call | flops 1000000000 | bytes 1000 | tf_op jit(solution)/shard_map/project_first/pallas_call | solution.py:28
  8.2 0.0 collective-permute-done.2.inner
  8.2 1.2 %collective-permute-done.1.cross = bf16[64,1024]{1,0:T(8,128)(2,1)S(1)} collective-permute-done((bf16[64,1024]{1,0:T(8,128)(2,1)S(1)}, bf16[64,1024]{1,0:T(8,128)(2,1)S(1)}, u32[]{:S(2)}, u32[]{:S(2)}) %collective-permute-start.1) | collective-permute-done | bytes 131104 | tf_op jit(solution)/shard_map/ppermute | solution.py:231
  9.4 2.5 %middle_1.1 = (bf16[128,1024]{1,0:T(8,128)(2,1)S(1)}, bf16[128,1024]{1,0:T(8,128)(2,1)S(1)}, bf16[32,1024]{1,0:T(8,128)(2,1)S(1)}, bf16[32,1024]{1,0:T(8,128)(2,1)S(1)}, bf16[32,1024]{1,0:T(8,128)(2,1)S(1)}) custom-call(bf16[128,1024]{1,0:T(8,128)(2,1)S(1)} %get-tuple-element.30.state, bf16[128,1024]{1,0:T(8,128)(2,1)S(1)} %get-tuple-element.32.q, ...), custom_call_target="tpu_custom_call" | custom-call | flops 1000000000 | bytes 1000 | tf_op jit(solution)/shard_map/middle_1/pallas_call | solution.py:28
  11.9 2.7 %collective-permute-start.3 = (bf16[32,1024]{1,0:T(8,128)(2,1)S(1)}, bf16[32,1024]{1,0:T(8,128)(2,1)S(1)}, u32[]{:S(2)}, u32[]{:S(2)}) collective-permute-start(bf16[32,1024]{1,0:T(8,128)(2,1)S(1)} %get-tuple-element.40), channel_id=1, source_target_pairs={{0,128},{1,2},{2,1},{3,4},{4,3},{5,6},{6,5},{7,8},{8,7},{9,10},{10... | collective-permute-start | bytes 196616 | tf_op jit(solution)/shard_map/ppermute | solution.py:231
  14.6 0.0 collective-permute-start.4
  14.6 0.5 %project.3 = (bf16[128,1024]{1,0:T(8,128)(2,1)S(1)}, bf16[32,1024]{1,0:T(8,128)(2,1)S(1)}) custom-call(bf16[128,1024]{1,0:T(8,128)(2,1)S(1)} %get-tuple-element.37.normed, bf16[1024,1024]{1,0:T(8,128)(2,1)S(1)} %copy-done.3, bf16[32,1024]{1,0:T(8,128)(2,1)S(1)} %get-tuple-element.38.inner), custom_call_target="tpu_custom_call" | custom-call | flops 1000000000 | bytes 1000 | tf_op jit(solution)/shard_map/project/pallas_call | solution.py:28
  15.1 3.1 %collective-permute-start.5 = (bf16[32,1024]{1,0:T(8,128)(2,1)S(1)}, bf16[32,1024]{1,0:T(8,128)(2,1)S(1)}, u32[]{:S(2)}, u32[]{:S(2)}) collective-permute-start(bf16[32,1024]{1,0:T(8,128)(2,1)S(1)} %get-tuple-element.43), channel_id=1, source_target_pairs={{0,32},{16,48},{32,64},{48,80},{64,96},{80,112},{96,128},{112,144}... | collective-permute-start | bytes 196616 | tf_op jit(solution)/shard_map/ppermute | solution.py:276
  18.1 1.0 %collective-permute-done.3.cross = bf16[32,1024]{1,0:T(8,128)(2,1)S(1)} collective-permute-done((bf16[32,1024]{1,0:T(8,128)(2,1)S(1)}, bf16[32,1024]{1,0:T(8,128)(2,1)S(1)}, u32[]{:S(2)}, u32[]{:S(2)}) %collective-permute-start.3) | collective-permute-done | bytes 65568 | tf_op jit(solution)/shard_map/ppermute | solution.py:231
  19.2 0.0 collective-permute-done.4.inner
  19.2 2.1 %last_1.1.token = bf16[128,1024]{1,0:T(8,128)(2,1)S(1)} custom-call(bf16[128,1024]{1,0:T(8,128)(2,1)S(1)} %get-tuple-element.36.state, bf16[128,1024]{1,0:T(8,128)(2,1)S(1)} %get-tuple-element.39.q, bf16[128,1024]{1,0:T(8,128)(2,1)S(1)} %get-tuple-element.37.normed, bf16[32,1024]{1,0:T(8,128)(2,1)S(1)} %collective-permute-done.3.cross, ...), custom_call_target="tpu_custom_call" | custom-call | flops 1000000000 | bytes 1000 | tf_op jit(solution)/shard_map/last_1/pallas_call | solution.py:28
  21.3 2.4 %collective-permute-start.9 = (bf16[128,1024]{1,0:T(8,128)(2,1)S(1)}, bf16[128,1024]{1,0:T(8,128)(2,1)S(1)}, u32[]{:S(2)}, u32[]{:S(2)}) collective-permute-start(bf16[128,1024]{1,0:T(8,128)(2,1)S(1)} %last_1.1.token), channel_id=1, source_target_pairs={{0,32},{16,48},{32,64},{48,80},{64,96},{80,112},{96,128},{112,144}... | collective-permute-start | bytes 786440 | tf_op jit(solution)/shard_map/ppermute | solution.py:278
  23.7 0.0 collective-permute-done.far.state
  23.7 0.4 far_first.1
  24.1 1.3 %collective-permute-start.6 = (bf16[32,1024]{1,0:T(8,128)(2,1)S(1)}, bf16[32,1024]{1,0:T(8,128)(2,1)S(1)}, u32[]{:S(2)}, u32[]{:S(2)}) collective-permute-start(bf16[32,1024]{1,0:T(8,128)(2,1)S(1)} %get-tuple-element.44), channel_id=1, source_target_pairs={{0,1},{1,0},{2,3},{3,2},{4,5},{5,4},{6,7},{7,6},{8,9},{9,8},{10,11... | collective-permute-start | bytes 196616 | tf_op jit(solution)/shard_map/ppermute | solution.py:234
  25.3 0.4 %project.4.q = bf16[128,1024]{1,0:T(8,128)(2,1)S(1)} custom-call(bf16[128,1024]{1,0:T(8,128)(2,1)S(1)} %get-tuple-element.42.normed, bf16[1024,1024]{1,0:T(8,128)(2,1)S(1)} %copy-done.3), custom_call_target="tpu_custom_call" | custom-call | flops 1000000000 | bytes 1000 | tf_op jit(solution)/shard_map/project/pallas_call | solution.py:28
  25.8 0.0 collective-permute-done.5.cross
  25.8 0.4 %collective-permute-done.6.inner = bf16[32,1024]{1,0:T(8,128)(2,1)S(1)} collective-permute-done((bf16[32,1024]{1,0:T(8,128)(2,1)S(1)}, bf16[32,1024]{1,0:T(8,128)(2,1)S(1)}, u32[]{:S(2)}, u32[]{:S(2)}) %collective-permute-start.6) | collective-permute-done | bytes 65568 | tf_op jit(solution)/shard_map/ppermute | solution.py:234
  26.3 2.5 %middle_0.1 = (bf16[128,1024]{1,0:T(8,128)(2,1)S(1)}, bf16[128,1024]{1,0:T(8,128)(2,1)S(1)}, bf16[32,1024]{1,0:T(8,128)(2,1)S(1)}, bf16[32,1024]{1,0:T(8,128)(2,1)S(1)}) custom-call(bf16[128,1024]{1,0:T(8,128)(2,1)S(1)} %collective-permute-done.far.state, bf16[128,1024]{1,0:T(8,128)(2,1)S(1)} %project.4.q, bf16[128,1024]{1,0:T(8,128)(2,1)S(1)} %get-tuple-element.42.normed, ...), custom_call_target="tpu_custom_call" | custom-call | flops 1000000000 | bytes 1000 | tf_op jit(solution)/shard_map/middle_0/pallas_call | solution.py:28
  28.7 1.7 %collective-permute-start.7 = (bf16[32,1024]{1,0:T(8,128)(2,1)S(1)}, bf16[32,1024]{1,0:T(8,128)(2,1)S(1)}, u32[]{:S(2)}, u32[]{:S(2)}) collective-permute-start(bf16[32,1024]{1,0:T(8,128)(2,1)S(1)} %get-tuple-element.47), channel_id=1, source_target_pairs={{0,128},{1,2},{2,1},{3,4},{4,3},{5,6},{6,5},{7,8},{8,7},{9,10},{10... | collective-permute-start | bytes 196616 | tf_op jit(solution)/shard_map/ppermute | solution.py:231
  30.4 0.2 collective-permute-start.8
  30.7 0.5 %project.5.q = bf16[128,1024]{1,0:T(8,128)(2,1)S(1)} custom-call(bf16[128,1024]{1,0:T(8,128)(2,1)S(1)} %get-tuple-element.46.normed, bf16[1024,1024]{1,0:T(8,128)(2,1)S(1)} %copy-done.3), custom_call_target="tpu_custom_call" | custom-call | flops 1000000000 | bytes 1000 | tf_op jit(solution)/shard_map/project/pallas_call | solution.py:28
  31.1 8.0 %collective-permute-done.7.cross = bf16[32,1024]{1,0:T(8,128)(2,1)S(1)} collective-permute-done((bf16[32,1024]{1,0:T(8,128)(2,1)S(1)}, bf16[32,1024]{1,0:T(8,128)(2,1)S(1)}, u32[]{:S(2)}, u32[]{:S(2)}) %collective-permute-start.7) | collective-permute-done | bytes 65568 | tf_op jit(solution)/shard_map/ppermute | solution.py:231
  39.1 0.0 collective-permute-done.8.inner
  39.1 2.1 %last_0.1.here = bf16[128,1024]{1,0:T(8,128)(2,1)S(1)} custom-call(bf16[128,1024]{1,0:T(8,128)(2,1)S(1)} %get-tuple-element.45.state, bf16[128,1024]{1,0:T(8,128)(2,1)S(1)} %project.5.q, bf16[128,1024]{1,0:T(8,128)(2,1)S(1)} %get-tuple-element.46.normed, bf16[32,1024]{1,0:T(8,128)(2,1)S(1)} %collective-permute-done.7.cross, ...), custom_call_target="tpu_custom_call" | custom-call | flops 1000000000 | bytes 1000 | tf_op jit(solution)/shard_map/last_0/pallas_call | solution.py:28
  41.2 0.0 collective-permute-done.9.there
  41.2 0.8 %finish.1 = bf16[1,2,128,1024]{3,2,1,0:T(8,128)(2,1)} custom-call(bf16[128,1024]{1,0:T(8,128)(2,1)S(1)} %last_0.1.here, bf16[128,1024]{1,0:T(8,128)(2,1)S(1)} %collective-permute-done.9.there), custom_call_target="tpu_custom_call" | custom-call | flops 1000000000 | bytes 1000 | tf_op jit(solution)/shard_map/finish/pallas_call | solution.py:28
  (9 shorter events, 0.0 us)
Async XLA Ops:
  0.0 7.7 %copy-start.3 = (bf16[1024,1024]{1,0:T(8,128)(2,1)S(1)}, bf16[1024,1024]{1,0:T(8,128)(2,1)}, u32[]{:S(2)}) copy-start(bf16[1024,1024]{1,0:T(8,128)(2,1)} %wq.7) | copy-start | bytes 6291460
  0.0 7.7 %copy-start.4 = (s32[128,8]{0,1:T(8,128)S(1)}, s32[128,8]{0,1:T(8,128)}, u32[]{:S(2)}) copy-start(s32[128,8]{0,1:T(8,128)} %param.16) | copy-start | bytes 12292
  0.0 9.4 %copy-start.1 = (bf16[1024,1024]{1,0:T(8,128)(2,1)S(1)}, bf16[1024,1024]{1,0:T(8,128)(2,1)}, u32[]{:S(2)}) copy-start(bf16[1024,1024]{1,0:T(8,128)(2,1)} %wv.7) | copy-start | bytes 6291460
  0.0 9.4 %copy-start.2 = (bf16[1024,1024]{1,0:T(8,128)(2,1)S(1)}, bf16[1024,1024]{1,0:T(8,128)(2,1)}, u32[]{:S(2)}) copy-start(bf16[1024,1024]{1,0:T(8,128)(2,1)} %wo.7) | copy-start | bytes 6291460
  2.0 7.4 %copy-start = (bf16[1024,1024]{1,0:T(8,128)(2,1)S(1)}, bf16[1024,1024]{1,0:T(8,128)(2,1)}, u32[]{:S(2)}) copy-start(bf16[1024,1024]{1,0:T(8,128)(2,1)} %wk.7) | copy-start | bytes 6291460
  2.0 7.4 %collective-permute-start.1 = (bf16[64,1024]{1,0:T(8,128)(2,1)S(1)}, bf16[64,1024]{1,0:T(8,128)(2,1)S(1)}, u32[]{:S(2)}, u32[]{:S(2)}) collective-permute-start(bf16[64,1024]{1,0:T(8,128)(2,1)S(1)} %get-tuple-element.33), channel_id=1, source_target_pairs={{0,128},{1,2},{2,1},{3,4},{4,3},{5,6},{6,5},{7,8},{8,7},{9,10},{10... | collective-permute-start | bytes 393224 | tf_op jit(solution)/shard_map/ppermute | solution.py:231
  4.7 3.5 %collective-permute-start.2 = (bf16[32,1024]{1,0:T(8,128)(2,1)S(1)}, bf16[32,1024]{1,0:T(8,128)(2,1)S(1)}, u32[]{:S(2)}, u32[]{:S(2)}) collective-permute-start(bf16[32,1024]{1,0:T(8,128)(2,1)S(1)} %get-tuple-element.34), channel_id=1, source_target_pairs={{0,1},{1,0},{2,3},{3,2},{4,5},{5,4},{6,7},{7,6},{8,9},{9,8},{10,11... | collective-permute-start | bytes 196616 | tf_op jit(solution)/shard_map/ppermute | solution.py:234
  4.7 19.0 %collective-permute-start = (bf16[128,1024]{1,0:T(8,128)(2,1)S(1)}, bf16[128,1024]{1,0:T(8,128)(2,1)S(1)}, u32[]{:S(2)}, u32[]{:S(2)}) collective-permute-start(bf16[128,1024]{1,0:T(8,128)(2,1)S(1)} %get-tuple-element.27), channel_id=1, source_target_pairs={{0,32},{16,48},{32,64},{48,80},{64,96},{80,112},{96,128},{112,144}... | collective-permute-start | bytes 786440 | tf_op jit(solution)/shard_map/ppermute | solution.py:271
  11.9 7.2 %collective-permute-start.3 = (bf16[32,1024]{1,0:T(8,128)(2,1)S(1)}, bf16[32,1024]{1,0:T(8,128)(2,1)S(1)}, u32[]{:S(2)}, u32[]{:S(2)}) collective-permute-start(bf16[32,1024]{1,0:T(8,128)(2,1)S(1)} %get-tuple-element.40), channel_id=1, source_target_pairs={{0,128},{1,2},{2,1},{3,4},{4,3},{5,6},{6,5},{7,8},{8,7},{9,10},{10... | collective-permute-start | bytes 196616 | tf_op jit(solution)/shard_map/ppermute | solution.py:231
  14.6 4.6 %collective-permute-start.4 = (bf16[32,1024]{1,0:T(8,128)(2,1)S(1)}, bf16[32,1024]{1,0:T(8,128)(2,1)S(1)}, u32[]{:S(2)}, u32[]{:S(2)}) collective-permute-start(bf16[32,1024]{1,0:T(8,128)(2,1)S(1)} %get-tuple-element.41), channel_id=1, source_target_pairs={{0,1},{1,0},{2,3},{3,2},{4,5},{5,4},{6,7},{7,6},{8,9},{9,8},{10,11... | collective-permute-start | bytes 196616 | tf_op jit(solution)/shard_map/ppermute | solution.py:234
  15.1 10.7 %collective-permute-start.5 = (bf16[32,1024]{1,0:T(8,128)(2,1)S(1)}, bf16[32,1024]{1,0:T(8,128)(2,1)S(1)}, u32[]{:S(2)}, u32[]{:S(2)}) collective-permute-start(bf16[32,1024]{1,0:T(8,128)(2,1)S(1)} %get-tuple-element.43), channel_id=1, source_target_pairs={{0,32},{16,48},{32,64},{48,80},{64,96},{80,112},{96,128},{112,144}... | collective-permute-start | bytes 196616 | tf_op jit(solution)/shard_map/ppermute | solution.py:276
  21.3 19.9 %collective-permute-start.9 = (bf16[128,1024]{1,0:T(8,128)(2,1)S(1)}, bf16[128,1024]{1,0:T(8,128)(2,1)S(1)}, u32[]{:S(2)}, u32[]{:S(2)}) collective-permute-start(bf16[128,1024]{1,0:T(8,128)(2,1)S(1)} %last_1.1.token), channel_id=1, source_target_pairs={{0,32},{16,48},{32,64},{48,80},{64,96},{80,112},{96,128},{112,144}... | collective-permute-start | bytes 786440 | tf_op jit(solution)/shard_map/ppermute | solution.py:278
  24.1 2.2 %collective-permute-start.6 = (bf16[32,1024]{1,0:T(8,128)(2,1)S(1)}, bf16[32,1024]{1,0:T(8,128)(2,1)S(1)}, u32[]{:S(2)}, u32[]{:S(2)}) collective-permute-start(bf16[32,1024]{1,0:T(8,128)(2,1)S(1)} %get-tuple-element.44), channel_id=1, source_target_pairs={{0,1},{1,0},{2,3},{3,2},{4,5},{5,4},{6,7},{7,6},{8,9},{9,8},{10,11... | collective-permute-start | bytes 196616 | tf_op jit(solution)/shard_map/ppermute | solution.py:234
  28.7 10.4 %collective-permute-start.7 = (bf16[32,1024]{1,0:T(8,128)(2,1)S(1)}, bf16[32,1024]{1,0:T(8,128)(2,1)S(1)}, u32[]{:S(2)}, u32[]{:S(2)}) collective-permute-start(bf16[32,1024]{1,0:T(8,128)(2,1)S(1)} %get-tuple-element.47), channel_id=1, source_target_pairs={{0,128},{1,2},{2,1},{3,4},{4,3},{5,6},{6,5},{7,8},{8,7},{9,10},{10... | collective-permute-start | bytes 196616 | tf_op jit(solution)/shard_map/ppermute | solution.py:231
  30.4 8.7 %collective-permute-start.8 = (bf16[32,1024]{1,0:T(8,128)(2,1)S(1)}, bf16[32,1024]{1,0:T(8,128)(2,1)S(1)}, u32[]{:S(2)}, u32[]{:S(2)}) collective-permute-start(bf16[32,1024]{1,0:T(8,128)(2,1)S(1)} %get-tuple-element.48), channel_id=1, source_target_pairs={{0,1},{1,0},{2,3},{3,2},{4,5},{5,4},{6,7},{7,6},{8,9},{9,8},{10,11... | collective-permute-start | bytes 196616 | tf_op jit(solution)/shard_map/ppermute | solution.py:234

commit v8 on v7

--- a/solution.py
+++ b/solution.py
@@ -8,7 +8,6 @@
 
 HEAD_DIM = 64
 LANES = 128
-NEVER = -1e30
 BF = jnp.bfloat16
 F32 = jnp.float32
 MS = 3.0
@@ -57,7 +56,7 @@
     return rows_of(rows, jnp.concatenate([first, second], axis=1))
 
 
-def bias_table(senders, odd, table):
+def count_table(senders, odd, table):
     nodes = table.shape[0]
     count = jnp.zeros((table.shape[1], nodes), F32)
     spots = lax.broadcasted_iota(jnp.int32, count.shape, 0)
@@ -65,7 +64,7 @@
     spots = jnp.where((spots >= nodes) & (odd == 1), jnp.where(spots >= nodes + half, spots - half, spots + half), spots)
     for j in range(senders.shape[0]):
         count += jnp.where(spots == senders[j:j + 1], 1.0, 0.0)
-    table[...] = jnp.where(count > 0, jnp.log(count), NEVER).T
+    table[...] = count.T
 
 
 def parity():
@@ -125,7 +124,7 @@
 
 
 def project_first_body(normed, wq, senders, q, table):
-    bias_table(senders, parity(), table)
+    count_table(senders, parity(), table)
     q[...] = queries_of(normed[...], wq[...])
 
 
@@ -149,9 +148,10 @@
     rows = jnp.concatenate([normed[...], cross, inner], axis=0)
     k = jnp.dot(rows, wk[...], preferred_element_type=F32).astype(BF)
     v = jnp.dot(rows, wv[...], preferred_element_type=F32).astype(BF)
-    bias = table[...]
+    count = table[...]
     nodes, width = q.shape
-    bias = jnp.concatenate([bias, bias], axis=0)
+    count = jnp.concatenate([count, count], axis=0)
+    named = count > 0
     first = lax.broadcasted_iota(jnp.int32, (nodes, LANES), 1) < HEAD_DIM
     ones = jnp.ones((table.shape[1], LANES), BF)
     for i in range(width // LANES):
@@ -159,8 +159,9 @@
         pair = q[:, at]
         zero = jnp.zeros_like(pair)
         both = jnp.concatenate([jnp.where(first, pair, zero), jnp.where(first, zero, pair)], axis=0)
-        scores = lax.dot_general(both, k[:, at], (((1,), (1,)), ((), ())), preferred_element_type=F32) + bias
-        expo = jnp.exp(scores - jnp.max(scores, axis=1, keepdims=True)).astype(BF)
+        scores = lax.dot_general(both, k[:, at], (((1,), (1,)), ((), ())), preferred_element_type=F32)
+        scores = jnp.where(named, scores, -jnp.inf)
+        expo = (jnp.exp(scores - jnp.max(scores, axis=1, keepdims=True)) * count).astype(BF)
         sums = jnp.dot(expo, jnp.concatenate([v[:, at], ones], axis=1), preferred_element_type=F32)
         top = sums[:nodes, :LANES] / sums[:nodes, LANES:]
         low = sums[nodes:, :LANES] / sums[nodes:, LANES:]

time: 42.3 us -> 42.5 us (level)
  no operation moved by 1% of the time
where the time goes in v8:
time: 42.5 us; the launch traced here: 42.3 us
  starting transfers between devices  17 us (40%)
  Pallas kernels  14.4 us (34%)
  waiting for transfers between devices  10.5 us (25%)
    pallas_call x11, Pallas kernels, call(): pl.pallas_call(body, out_shape=outs, in_specs=specs, out_specs=out_specs,...  14.4 us
    ppermute x3, waiting for transfers between devices, crossed(): return lax.ppermute(cross, ('lead', 'mesh'), cross_route)  10.1 us
    ppermute x3, starting transfers between devices, crossed(): return lax.ppermute(cross, ('lead', 'mesh'), cross_route)  7.02 us
    ppermute x1, starting transfers between devices, per_device(): halo0 = lax.ppermute(halo0, 'lead', route)  3.07 us
    ppermute x1, starting transfers between devices, per_device(): far = lax.ppermute(far, 'lead', route)  2.99 us
    ppermute x1, starting transfers between devices, per_device(): arrived = lax.ppermute(near, 'lead', route)  2.45 us
    ppermute x4, starting transfers between devices, swapped(): return lax.ppermute(inner, 'mesh', inner_route)  1.51 us
  transfers between devices with their start and end apart: 10, of which 4 were waited for; matrix products, arithmetic and copies ran while one was open for 0% of the time, Pallas kernels for 27%

profile of v8, /device:TPU:45, one launch (start us, length us, event | category | flops | bytes accessed | tf_op | source)
XLA Modules:
  0.0 42.3 jit_solution(12475817998602279257)
XLA Ops:
  0.0 2.0 %start.1 = (bf16[128,1024]{1,0:T(8,128)(2,1)S(1)}, bf16[128,1024]{1,0:T(8,128)(2,1)S(1)}, f32[1,1024]{1,0:T(1,128)S(1)}, s32[2,32]{1,0:T(2,128)S(1)}, bf16[128,1...) custom-call(bf16[1,2,128,1024]{3,2,1,0:T(8,128)(2,1)} %states.1, ...), custom_call_target="tpu_custom_call" | custom-call | flops 3000000000 | bytes 1000 | tf_op jit(solution)/shard_map/start/pallas_call | solution.py:27
  2.0 0.0 copy-start
  2.0 2.7 %collective-permute-start.1 = (bf16[64,1024]{1,0:T(8,128)(2,1)S(1)}, bf16[64,1024]{1,0:T(8,128)(2,1)S(1)}, u32[]{:S(2)}, u32[]{:S(2)}) collective-permute-start(bf16[64,1024]{1,0:T(8,128)(2,1)S(1)} %get-tuple-element.33), channel_id=1, source_target_pairs={{0,128},{1,2},{2,1},{3,4},{4,3},{5,6},{6,5},{7,8},{8,7},{9,10},{10... | collective-permute-start | bytes 393224 | tf_op jit(solution)/shard_map/ppermute | solution.py:232
  4.7 0.0 collective-permute-start.2
  4.7 3.0 %collective-permute-start = (bf16[128,1024]{1,0:T(8,128)(2,1)S(1)}, bf16[128,1024]{1,0:T(8,128)(2,1)S(1)}, u32[]{:S(2)}, u32[]{:S(2)}) collective-permute-start(bf16[128,1024]{1,0:T(8,128)(2,1)S(1)} %get-tuple-element.27), channel_id=1, source_target_pairs={{0,32},{16,48},{32,64},{48,80},{64,96},{80,112},{96,128},{112,144}... | collective-permute-start | bytes 786440 | tf_op jit(solution)/shard_map/ppermute | solution.py:272
  7.7 0.5 %project_first.1 = (bf16[128,1024]{1,0:T(8,128)(2,1)S(1)}, f32[128,192]{1,0:T(8,128)S(1)}) custom-call(bf16[128,1024]{1,0:T(8,128)(2,1)S(1)} %get-tuple-element.31.normed, bf16[1024,1024]{1,0:T(8,128)(2,1)S(1)} %copy-done.3, s32[8,128]{1,0:T(8,128)S(1)} %bitcast.3), custom_call_target="tpu_custom_call" | custom-call | flops 1000000000 | bytes 1000 | tf_op jit(solution)/shard_map/project_first/pallas_call | solution.py:27
  8.2 0.0 collective-permute-done.2.inner
  8.2 1.2 %collective-permute-done.1.cross = bf16[64,1024]{1,0:T(8,128)(2,1)S(1)} collective-permute-done((bf16[64,1024]{1,0:T(8,128)(2,1)S(1)}, bf16[64,1024]{1,0:T(8,128)(2,1)S(1)}, u32[]{:S(2)}, u32[]{:S(2)}) %collective-permute-start.1) | collective-permute-done | bytes 131104 | tf_op jit(solution)/shard_map/ppermute | solution.py:232
  9.4 2.5 %middle_1.1 = (bf16[128,1024]{1,0:T(8,128)(2,1)S(1)}, bf16[128,1024]{1,0:T(8,128)(2,1)S(1)}, bf16[32,1024]{1,0:T(8,128)(2,1)S(1)}, bf16[32,1024]{1,0:T(8,128)(2,1)S(1)}, bf16[32,1024]{1,0:T(8,128)(2,1)S(1)}) custom-call(bf16[128,1024]{1,0:T(8,128)(2,1)S(1)} %get-tuple-element.30.state, bf16[128,1024]{1,0:T(8,128)(2,1)S(1)} %get-tuple-element.32.q, ...), custom_call_target="tpu_custom_call" | custom-call | flops 1000000000 | bytes 1000 | tf_op jit(solution)/shard_map/middle_1/pallas_call | solution.py:27
  12.0 2.7 %collective-permute-start.3 = (bf16[32,1024]{1,0:T(8,128)(2,1)S(1)}, bf16[32,1024]{1,0:T(8,128)(2,1)S(1)}, u32[]{:S(2)}, u32[]{:S(2)}) collective-permute-start(bf16[32,1024]{1,0:T(8,128)(2,1)S(1)} %get-tuple-element.40), channel_id=1, source_target_pairs={{0,128},{1,2},{2,1},{3,4},{4,3},{5,6},{6,5},{7,8},{8,7},{9,10},{10... | collective-permute-start | bytes 196616 | tf_op jit(solution)/shard_map/ppermute | solution.py:232
  14.7 0.0 collective-permute-start.4
  14.7 0.5 %project.3 = (bf16[128,1024]{1,0:T(8,128)(2,1)S(1)}, bf16[32,1024]{1,0:T(8,128)(2,1)S(1)}) custom-call(bf16[128,1024]{1,0:T(8,128)(2,1)S(1)} %get-tuple-element.37.normed, bf16[1024,1024]{1,0:T(8,128)(2,1)S(1)} %copy-done.3, bf16[32,1024]{1,0:T(8,128)(2,1)S(1)} %get-tuple-element.38.inner), custom_call_target="tpu_custom_call" | custom-call | flops 1000000000 | bytes 1000 | tf_op jit(solution)/shard_map/project/pallas_call | solution.py:27
  15.1 3.1 %collective-permute-start.5 = (bf16[32,1024]{1,0:T(8,128)(2,1)S(1)}, bf16[32,1024]{1,0:T(8,128)(2,1)S(1)}, u32[]{:S(2)}, u32[]{:S(2)}) collective-permute-start(bf16[32,1024]{1,0:T(8,128)(2,1)S(1)} %get-tuple-element.43), channel_id=1, source_target_pairs={{0,32},{16,48},{32,64},{48,80},{64,96},{80,112},{96,128},{112,144}... | collective-permute-start | bytes 196616 | tf_op jit(solution)/shard_map/ppermute | solution.py:277
  18.2 1.0 %collective-permute-done.3.cross = bf16[32,1024]{1,0:T(8,128)(2,1)S(1)} collective-permute-done((bf16[32,1024]{1,0:T(8,128)(2,1)S(1)}, bf16[32,1024]{1,0:T(8,128)(2,1)S(1)}, u32[]{:S(2)}, u32[]{:S(2)}) %collective-permute-start.3) | collective-permute-done | bytes 65568 | tf_op jit(solution)/shard_map/ppermute | solution.py:232
  19.2 0.0 collective-permute-done.4.inner
  19.2 2.2 %last_1.1.token = bf16[128,1024]{1,0:T(8,128)(2,1)S(1)} custom-call(bf16[128,1024]{1,0:T(8,128)(2,1)S(1)} %get-tuple-element.36.state, bf16[128,1024]{1,0:T(8,128)(2,1)S(1)} %get-tuple-element.39.q, bf16[128,1024]{1,0:T(8,128)(2,1)S(1)} %get-tuple-element.37.normed, bf16[32,1024]{1,0:T(8,128)(2,1)S(1)} %collective-permute-done.3.cross, ...), custom_call_target="tpu_custom_call" | custom-call | flops 1000000000 | bytes 1000 | tf_op jit(solution)/shard_map/last_1/pallas_call | solution.py:27
  21.4 2.4 %collective-permute-start.9 = (bf16[128,1024]{1,0:T(8,128)(2,1)S(1)}, bf16[128,1024]{1,0:T(8,128)(2,1)S(1)}, u32[]{:S(2)}, u32[]{:S(2)}) collective-permute-start(bf16[128,1024]{1,0:T(8,128)(2,1)S(1)} %last_1.1.token), channel_id=1, source_target_pairs={{0,32},{16,48},{32,64},{48,80},{64,96},{80,112},{96,128},{112,144}... | collective-permute-start | bytes 786440 | tf_op jit(solution)/shard_map/ppermute | solution.py:279
  23.8 0.0 collective-permute-done.far.state
  23.8 0.4 far_first.1
  24.2 1.3 %collective-permute-start.6 = (bf16[32,1024]{1,0:T(8,128)(2,1)S(1)}, bf16[32,1024]{1,0:T(8,128)(2,1)S(1)}, u32[]{:S(2)}, u32[]{:S(2)}) collective-permute-start(bf16[32,1024]{1,0:T(8,128)(2,1)S(1)} %get-tuple-element.44), channel_id=1, source_target_pairs={{0,1},{1,0},{2,3},{3,2},{4,5},{5,4},{6,7},{7,6},{8,9},{9,8},{10,11... | collective-permute-start | bytes 196616 | tf_op jit(solution)/shard_map/ppermute | solution.py:235
  25.5 0.5 %project.4.q = bf16[128,1024]{1,0:T(8,128)(2,1)S(1)} custom-call(bf16[128,1024]{1,0:T(8,128)(2,1)S(1)} %get-tuple-element.42.normed, bf16[1024,1024]{1,0:T(8,128)(2,1)S(1)} %copy-done.3), custom_call_target="tpu_custom_call" | custom-call | flops 1000000000 | bytes 1000 | tf_op jit(solution)/shard_map/project/pallas_call | solution.py:27
  25.9 0.0 collective-permute-done.5.cross
  25.9 0.4 %collective-permute-done.6.inner = bf16[32,1024]{1,0:T(8,128)(2,1)S(1)} collective-permute-done((bf16[32,1024]{1,0:T(8,128)(2,1)S(1)}, bf16[32,1024]{1,0:T(8,128)(2,1)S(1)}, u32[]{:S(2)}, u32[]{:S(2)}) %collective-permute-start.6) | collective-permute-done | bytes 65568 | tf_op jit(solution)/shard_map/ppermute | solution.py:235
  26.4 2.5 %middle_0.1 = (bf16[128,1024]{1,0:T(8,128)(2,1)S(1)}, bf16[128,1024]{1,0:T(8,128)(2,1)S(1)}, bf16[32,1024]{1,0:T(8,128)(2,1)S(1)}, bf16[32,1024]{1,0:T(8,128)(2,1)S(1)}) custom-call(bf16[128,1024]{1,0:T(8,128)(2,1)S(1)} %collective-permute-done.far.state, bf16[128,1024]{1,0:T(8,128)(2,1)S(1)} %project.4.q, bf16[128,1024]{1,0:T(8,128)(2,1)S(1)} %get-tuple-element.42.normed, ...), custom_call_target="tpu_custom_call" | custom-call | flops 1000000000 | bytes 1000 | tf_op jit(solution)/shard_map/middle_0/pallas_call | solution.py:27
  28.9 1.7 %collective-permute-start.7 = (bf16[32,1024]{1,0:T(8,128)(2,1)S(1)}, bf16[32,1024]{1,0:T(8,128)(2,1)S(1)}, u32[]{:S(2)}, u32[]{:S(2)}) collective-permute-start(bf16[32,1024]{1,0:T(8,128)(2,1)S(1)} %get-tuple-element.47), channel_id=1, source_target_pairs={{0,128},{1,2},{2,1},{3,4},{4,3},{5,6},{6,5},{7,8},{8,7},{9,10},{10... | collective-permute-start | bytes 196616 | tf_op jit(solution)/shard_map/ppermute | solution.py:232
  30.6 0.2 collective-permute-start.8
  30.9 0.4 %project.5.q = bf16[128,1024]{1,0:T(8,128)(2,1)S(1)} custom-call(bf16[128,1024]{1,0:T(8,128)(2,1)S(1)} %get-tuple-element.46.normed, bf16[1024,1024]{1,0:T(8,128)(2,1)S(1)} %copy-done.3), custom_call_target="tpu_custom_call" | custom-call | flops 1000000000 | bytes 1000 | tf_op jit(solution)/shard_map/project/pallas_call | solution.py:27
  31.3 7.9 %collective-permute-done.7.cross = bf16[32,1024]{1,0:T(8,128)(2,1)S(1)} collective-permute-done((bf16[32,1024]{1,0:T(8,128)(2,1)S(1)}, bf16[32,1024]{1,0:T(8,128)(2,1)S(1)}, u32[]{:S(2)}, u32[]{:S(2)}) %collective-permute-start.7) | collective-permute-done | bytes 65568 | tf_op jit(solution)/shard_map/ppermute | solution.py:232
  39.2 0.0 collective-permute-done.8.inner
  39.2 2.2 %last_0.1.here = bf16[128,1024]{1,0:T(8,128)(2,1)S(1)} custom-call(bf16[128,1024]{1,0:T(8,128)(2,1)S(1)} %get-tuple-element.45.state, bf16[128,1024]{1,0:T(8,128)(2,1)S(1)} %project.5.q, bf16[128,1024]{1,0:T(8,128)(2,1)S(1)} %get-tuple-element.46.normed, bf16[32,1024]{1,0:T(8,128)(2,1)S(1)} %collective-permute-done.7.cross, ...), custom_call_target="tpu_custom_call" | custom-call | flops 1000000000 | bytes 1000 | tf_op jit(solution)/shard_map/last_0/pallas_call | solution.py:27
  41.3 0.0 collective-permute-done.9.there
  41.4 0.8 %finish.1 = bf16[1,2,128,1024]{3,2,1,0:T(8,128)(2,1)} custom-call(bf16[128,1024]{1,0:T(8,128)(2,1)S(1)} %last_0.1.here, bf16[128,1024]{1,0:T(8,128)(2,1)S(1)} %collective-permute-done.9.there), custom_call_target="tpu_custom_call" | custom-call | flops 1000000000 | bytes 1000 | tf_op jit(solution)/shard_map/finish/pallas_call | solution.py:27
  (9 shorter events, 0.0 us)
Async XLA Ops:
  0.0 7.7 %copy-start.3 = (bf16[1024,1024]{1,0:T(8,128)(2,1)S(1)}, bf16[1024,1024]{1,0:T(8,128)(2,1)}, u32[]{:S(2)}) copy-start(bf16[1024,1024]{1,0:T(8,128)(2,1)} %wq.7) | copy-start | bytes 6291460
  0.0 7.7 %copy-start.4 = (s32[128,8]{0,1:T(8,128)S(1)}, s32[128,8]{0,1:T(8,128)}, u32[]{:S(2)}) copy-start(s32[128,8]{0,1:T(8,128)} %param.16) | copy-start | bytes 12292
  0.0 9.4 %copy-start.1 = (bf16[1024,1024]{1,0:T(8,128)(2,1)S(1)}, bf16[1024,1024]{1,0:T(8,128)(2,1)}, u32[]{:S(2)}) copy-start(bf16[1024,1024]{1,0:T(8,128)(2,1)} %wv.7) | copy-start | bytes 6291460
  0.0 9.4 %copy-start.2 = (bf16[1024,1024]{1,0:T(8,128)(2,1)S(1)}, bf16[1024,1024]{1,0:T(8,128)(2,1)}, u32[]{:S(2)}) copy-start(bf16[1024,1024]{1,0:T(8,128)(2,1)} %wo.7) | copy-start | bytes 6291460
  2.0 7.4 %copy-start = (bf16[1024,1024]{1,0:T(8,128)(2,1)S(1)}, bf16[1024,1024]{1,0:T(8,128)(2,1)}, u32[]{:S(2)}) copy-start(bf16[1024,1024]{1,0:T(8,128)(2,1)} %wk.7) | copy-start | bytes 6291460
  2.0 7.4 %collective-permute-start.1 = (bf16[64,1024]{1,0:T(8,128)(2,1)S(1)}, bf16[64,1024]{1,0:T(8,128)(2,1)S(1)}, u32[]{:S(2)}, u32[]{:S(2)}) collective-permute-start(bf16[64,1024]{1,0:T(8,128)(2,1)S(1)} %get-tuple-element.33), channel_id=1, source_target_pairs={{0,128},{1,2},{2,1},{3,4},{4,3},{5,6},{6,5},{7,8},{8,7},{9,10},{10... | collective-permute-start | bytes 393224 | tf_op jit(solution)/shard_map/ppermute | solution.py:232
  4.7 3.5 %collective-permute-start.2 = (bf16[32,1024]{1,0:T(8,128)(2,1)S(1)}, bf16[32,1024]{1,0:T(8,128)(2,1)S(1)}, u32[]{:S(2)}, u32[]{:S(2)}) collective-permute-start(bf16[32,1024]{1,0:T(8,128)(2,1)S(1)} %get-tuple-element.34), channel_id=1, source_target_pairs={{0,1},{1,0},{2,3},{3,2},{4,5},{5,4},{6,7},{7,6},{8,9},{9,8},{10,11... | collective-permute-start | bytes 196616 | tf_op jit(solution)/shard_map/ppermute | solution.py:235
  4.7 19.1 %collective-permute-start = (bf16[128,1024]{1,0:T(8,128)(2,1)S(1)}, bf16[128,1024]{1,0:T(8,128)(2,1)S(1)}, u32[]{:S(2)}, u32[]{:S(2)}) collective-permute-start(bf16[128,1024]{1,0:T(8,128)(2,1)S(1)} %get-tuple-element.27), channel_id=1, source_target_pairs={{0,32},{16,48},{32,64},{48,80},{64,96},{80,112},{96,128},{112,144}... | collective-permute-start | bytes 786440 | tf_op jit(solution)/shard_map/ppermute | solution.py:272
  12.0 7.2 %collective-permute-start.3 = (bf16[32,1024]{1,0:T(8,128)(2,1)S(1)}, bf16[32,1024]{1,0:T(8,128)(2,1)S(1)}, u32[]{:S(2)}, u32[]{:S(2)}) collective-permute-start(bf16[32,1024]{1,0:T(8,128)(2,1)S(1)} %get-tuple-element.40), channel_id=1, source_target_pairs={{0,128},{1,2},{2,1},{3,4},{4,3},{5,6},{6,5},{7,8},{8,7},{9,10},{10... | collective-permute-start | bytes 196616 | tf_op jit(solution)/shard_map/ppermute | solution.py:232
  14.7 4.5 %collective-permute-start.4 = (bf16[32,1024]{1,0:T(8,128)(2,1)S(1)}, bf16[32,1024]{1,0:T(8,128)(2,1)S(1)}, u32[]{:S(2)}, u32[]{:S(2)}) collective-permute-start(bf16[32,1024]{1,0:T(8,128)(2,1)S(1)} %get-tuple-element.41), channel_id=1, source_target_pairs={{0,1},{1,0},{2,3},{3,2},{4,5},{5,4},{6,7},{7,6},{8,9},{9,8},{10,11... | collective-permute-start | bytes 196616 | tf_op jit(solution)/shard_map/ppermute | solution.py:235
  15.1 10.8 %collective-permute-start.5 = (bf16[32,1024]{1,0:T(8,128)(2,1)S(1)}, bf16[32,1024]{1,0:T(8,128)(2,1)S(1)}, u32[]{:S(2)}, u32[]{:S(2)}) collective-permute-start(bf16[32,1024]{1,0:T(8,128)(2,1)S(1)} %get-tuple-element.43), channel_id=1, source_target_pairs={{0,32},{16,48},{32,64},{48,80},{64,96},{80,112},{96,128},{112,144}... | collective-permute-start | bytes 196616 | tf_op jit(solution)/shard_map/ppermute | solution.py:277
  21.4 20.0 %collective-permute-start.9 = (bf16[128,1024]{1,0:T(8,128)(2,1)S(1)}, bf16[128,1024]{1,0:T(8,128)(2,1)S(1)}, u32[]{:S(2)}, u32[]{:S(2)}) collective-permute-start(bf16[128,1024]{1,0:T(8,128)(2,1)S(1)} %last_1.1.token), channel_id=1, source_target_pairs={{0,32},{16,48},{32,64},{48,80},{64,96},{80,112},{96,128},{112,144}... | collective-permute-start | bytes 786440 | tf_op jit(solution)/shard_map/ppermute | solution.py:279
  24.2 2.2 %collective-permute-start.6 = (bf16[32,1024]{1,0:T(8,128)(2,1)S(1)}, bf16[32,1024]{1,0:T(8,128)(2,1)S(1)}, u32[]{:S(2)}, u32[]{:S(2)}) collective-permute-start(bf16[32,1024]{1,0:T(8,128)(2,1)S(1)} %get-tuple-element.44), channel_id=1, source_target_pairs={{0,1},{1,0},{2,3},{3,2},{4,5},{5,4},{6,7},{7,6},{8,9},{9,8},{10,11... | collective-permute-start | bytes 196616 | tf_op jit(solution)/shard_map/ppermute | solution.py:235
  28.9 10.2 %collective-permute-start.7 = (bf16[32,1024]{1,0:T(8,128)(2,1)S(1)}, bf16[32,1024]{1,0:T(8,128)(2,1)S(1)}, u32[]{:S(2)}, u32[]{:S(2)}) collective-permute-start(bf16[32,1024]{1,0:T(8,128)(2,1)S(1)} %get-tuple-element.47), channel_id=1, source_target_pairs={{0,128},{1,2},{2,1},{3,4},{4,3},{5,6},{6,5},{7,8},{8,7},{9,10},{10... | collective-permute-start | bytes 196616 | tf_op jit(solution)/shard_map/ppermute | solution.py:232
  30.6 8.5 %collective-permute-start.8 = (bf16[32,1024]{1,0:T(8,128)(2,1)S(1)}, bf16[32,1024]{1,0:T(8,128)(2,1)S(1)}, u32[]{:S(2)}, u32[]{:S(2)}) collective-permute-start(bf16[32,1024]{1,0:T(8,128)(2,1)S(1)} %get-tuple-element.48), channel_id=1, source_target_pairs={{0,1},{1,0},{2,3},{3,2},{4,5},{5,4},{6,7},{7,6},{8,9},{9,8},{10,11... | collective-permute-start | bytes 196616 | tf_op jit(solution)/shard_map/ppermute | solution.py:235

commit v9 on v7

--- a/solution.py
+++ b/solution.py
@@ -8,7 +8,7 @@
 
 HEAD_DIM = 64
 LANES = 128
-NEVER = -1e30
+NEVER = -jnp.inf
 BF = jnp.bfloat16
 F32 = jnp.float32
 MS = 3.0

time: 42.3 us -> 42.3 us (level)
  no operation moved by 1% of the time
where the time goes in v9:
time: 42.3 us; the launch traced here: 42.2 us
  starting transfers between devices  17 us (40%)
  Pallas kernels  14.2 us (34%)
  waiting for transfers between devices  10.7 us (25%)
    pallas_call x11, Pallas kernels, call(): pl.pallas_call(body, out_shape=outs, in_specs=specs, out_specs=out_specs,...  14.2 us
    ppermute x3, waiting for transfers between devices, crossed(): return lax.ppermute(cross, ('lead', 'mesh'), cross_route)  10.3 us
    ppermute x3, starting transfers between devices, crossed(): return lax.ppermute(cross, ('lead', 'mesh'), cross_route)  7.03 us
    ppermute x1, starting transfers between devices, per_device(): halo0 = lax.ppermute(halo0, 'lead', route)  3.07 us
    ppermute x1, starting transfers between devices, per_device(): far = lax.ppermute(far, 'lead', route)  2.99 us
    ppermute x1, starting transfers between devices, per_device(): arrived = lax.ppermute(near, 'lead', route)  2.4 us
    ppermute x4, starting transfers between devices, swapped(): return lax.ppermute(inner, 'mesh', inner_route)  1.51 us
  transfers between devices with their start and end apart: 10, of which 4 were waited for; matrix products, arithmetic and copies ran while one was open for 0% of the time, Pallas kernels for 27%

profile of v9, /device:TPU:45, one launch (start us, length us, event | category | flops | bytes accessed | tf_op | source)
XLA Modules:
  0.0 42.2 jit_solution(15199270319263900377)
XLA Ops:
  0.0 2.0 %start.1 = (bf16[128,1024]{1,0:T(8,128)(2,1)S(1)}, bf16[128,1024]{1,0:T(8,128)(2,1)S(1)}, f32[1,1024]{1,0:T(1,128)S(1)}, s32[2,32]{1,0:T(2,128)S(1)}, bf16[128,1...) custom-call(bf16[1,2,128,1024]{3,2,1,0:T(8,128)(2,1)} %states.1, ...), custom_call_target="tpu_custom_call" | custom-call | flops 3000000000 | bytes 1000 | tf_op jit(solution)/shard_map/start/pallas_call | solution.py:28
  2.0 0.0 copy-start
  2.0 2.7 %collective-permute-start.1 = (bf16[64,1024]{1,0:T(8,128)(2,1)S(1)}, bf16[64,1024]{1,0:T(8,128)(2,1)S(1)}, u32[]{:S(2)}, u32[]{:S(2)}) collective-permute-start(bf16[64,1024]{1,0:T(8,128)(2,1)S(1)} %get-tuple-element.33), channel_id=1, source_target_pairs={{0,128},{1,2},{2,1},{3,4},{4,3},{5,6},{6,5},{7,8},{8,7},{9,10},{10... | collective-permute-start | bytes 393224 | tf_op jit(solution)/shard_map/ppermute | solution.py:231
  4.7 0.0 collective-permute-start.2
  4.7 3.0 %collective-permute-start = (bf16[128,1024]{1,0:T(8,128)(2,1)S(1)}, bf16[128,1024]{1,0:T(8,128)(2,1)S(1)}, u32[]{:S(2)}, u32[]{:S(2)}) collective-permute-start(bf16[128,1024]{1,0:T(8,128)(2,1)S(1)} %get-tuple-element.27), channel_id=1, source_target_pairs={{0,32},{16,48},{32,64},{48,80},{64,96},{80,112},{96,128},{112,144}... | collective-permute-start | bytes 786440 | tf_op jit(solution)/shard_map/ppermute | solution.py:271
  7.7 0.5 %project_first.1 = (bf16[128,1024]{1,0:T(8,128)(2,1)S(1)}, f32[128,192]{1,0:T(8,128)S(1)}) custom-call(bf16[128,1024]{1,0:T(8,128)(2,1)S(1)} %get-tuple-element.31.normed, bf16[1024,1024]{1,0:T(8,128)(2,1)S(1)} %copy-done.3, s32[8,128]{1,0:T(8,128)S(1)} %bitcast.3), custom_call_target="tpu_custom_call" | custom-call | flops 1000000000 | bytes 1000 | tf_op jit(solution)/shard_map/project_first/pallas_call | solution.py:28
  8.2 0.0 collective-permute-done.2.inner
  8.2 1.2 %collective-permute-done.1.cross = bf16[64,1024]{1,0:T(8,128)(2,1)S(1)} collective-permute-done((bf16[64,1024]{1,0:T(8,128)(2,1)S(1)}, bf16[64,1024]{1,0:T(8,128)(2,1)S(1)}, u32[]{:S(2)}, u32[]{:S(2)}) %collective-permute-start.1) | collective-permute-done | bytes 131104 | tf_op jit(solution)/shard_map/ppermute | solution.py:231
  9.4 2.5 %middle_1.1 = (bf16[128,1024]{1,0:T(8,128)(2,1)S(1)}, bf16[128,1024]{1,0:T(8,128)(2,1)S(1)}, bf16[32,1024]{1,0:T(8,128)(2,1)S(1)}, bf16[32,1024]{1,0:T(8,128)(2,1)S(1)}, bf16[32,1024]{1,0:T(8,128)(2,1)S(1)}) custom-call(bf16[128,1024]{1,0:T(8,128)(2,1)S(1)} %get-tuple-element.30.state, bf16[128,1024]{1,0:T(8,128)(2,1)S(1)} %get-tuple-element.32.q, ...), custom_call_target="tpu_custom_call" | custom-call | flops 1000000000 | bytes 1000 | tf_op jit(solution)/shard_map/middle_1/pallas_call | solution.py:28
  11.9 2.7 %collective-permute-start.3 = (bf16[32,1024]{1,0:T(8,128)(2,1)S(1)}, bf16[32,1024]{1,0:T(8,128)(2,1)S(1)}, u32[]{:S(2)}, u32[]{:S(2)}) collective-permute-start(bf16[32,1024]{1,0:T(8,128)(2,1)S(1)} %get-tuple-element.40), channel_id=1, source_target_pairs={{0,128},{1,2},{2,1},{3,4},{4,3},{5,6},{6,5},{7,8},{8,7},{9,10},{10... | collective-permute-start | bytes 196616 | tf_op jit(solution)/shard_map/ppermute | solution.py:231
  14.6 0.0 collective-permute-start.4
  14.6 0.5 %project.3 = (bf16[128,1024]{1,0:T(8,128)(2,1)S(1)}, bf16[32,1024]{1,0:T(8,128)(2,1)S(1)}) custom-call(bf16[128,1024]{1,0:T(8,128)(2,1)S(1)} %get-tuple-element.37.normed, bf16[1024,1024]{1,0:T(8,128)(2,1)S(1)} %copy-done.3, bf16[32,1024]{1,0:T(8,128)(2,1)S(1)} %get-tuple-element.38.inner), custom_call_target="tpu_custom_call" | custom-call | flops 1000000000 | bytes 1000 | tf_op jit(solution)/shard_map/project/pallas_call | solution.py:28
  15.1 3.1 %collective-permute-start.5 = (bf16[32,1024]{1,0:T(8,128)(2,1)S(1)}, bf16[32,1024]{1,0:T(8,128)(2,1)S(1)}, u32[]{:S(2)}, u32[]{:S(2)}) collective-permute-start(bf16[32,1024]{1,0:T(8,128)(2,1)S(1)} %get-tuple-element.43), channel_id=1, source_target_pairs={{0,32},{16,48},{32,64},{48,80},{64,96},{80,112},{96,128},{112,144}... | collective-permute-start | bytes 196616 | tf_op jit(solution)/shard_map/ppermute | solution.py:276
  18.1 1.0 %collective-permute-done.3.cross = bf16[32,1024]{1,0:T(8,128)(2,1)S(1)} collective-permute-done((bf16[32,1024]{1,0:T(8,128)(2,1)S(1)}, bf16[32,1024]{1,0:T(8,128)(2,1)S(1)}, u32[]{:S(2)}, u32[]{:S(2)}) %collective-permute-start.3) | collective-permute-done | bytes 65568 | tf_op jit(solution)/shard_map/ppermute | solution.py:231
  19.2 0.0 collective-permute-done.4.inner
  19.2 2.1 %last_1.1.token = bf16[128,1024]{1,0:T(8,128)(2,1)S(1)} custom-call(bf16[128,1024]{1,0:T(8,128)(2,1)S(1)} %get-tuple-element.36.state, bf16[128,1024]{1,0:T(8,128)(2,1)S(1)} %get-tuple-element.39.q, bf16[128,1024]{1,0:T(8,128)(2,1)S(1)} %get-tuple-element.37.normed, bf16[32,1024]{1,0:T(8,128)(2,1)S(1)} %collective-permute-done.3.cross, ...), custom_call_target="tpu_custom_call" | custom-call | flops 1000000000 | bytes 1000 | tf_op jit(solution)/shard_map/last_1/pallas_call | solution.py:28
  21.3 2.4 %collective-permute-start.9 = (bf16[128,1024]{1,0:T(8,128)(2,1)S(1)}, bf16[128,1024]{1,0:T(8,128)(2,1)S(1)}, u32[]{:S(2)}, u32[]{:S(2)}) collective-permute-start(bf16[128,1024]{1,0:T(8,128)(2,1)S(1)} %last_1.1.token), channel_id=1, source_target_pairs={{0,32},{16,48},{32,64},{48,80},{64,96},{80,112},{96,128},{112,144}... | collective-permute-start | bytes 786440 | tf_op jit(solution)/shard_map/ppermute | solution.py:278
  23.7 0.0 collective-permute-done.far.state
  23.7 0.4 far_first.1
  24.1 1.3 %collective-permute-start.6 = (bf16[32,1024]{1,0:T(8,128)(2,1)S(1)}, bf16[32,1024]{1,0:T(8,128)(2,1)S(1)}, u32[]{:S(2)}, u32[]{:S(2)}) collective-permute-start(bf16[32,1024]{1,0:T(8,128)(2,1)S(1)} %get-tuple-element.44), channel_id=1, source_target_pairs={{0,1},{1,0},{2,3},{3,2},{4,5},{5,4},{6,7},{7,6},{8,9},{9,8},{10,11... | collective-permute-start | bytes 196616 | tf_op jit(solution)/shard_map/ppermute | solution.py:234
  25.3 0.4 %project.4.q = bf16[128,1024]{1,0:T(8,128)(2,1)S(1)} custom-call(bf16[128,1024]{1,0:T(8,128)(2,1)S(1)} %get-tuple-element.42.normed, bf16[1024,1024]{1,0:T(8,128)(2,1)S(1)} %copy-done.3), custom_call_target="tpu_custom_call" | custom-call | flops 1000000000 | bytes 1000 | tf_op jit(solution)/shard_map/project/pallas_call | solution.py:28
  25.8 0.0 collective-permute-done.5.cross
  25.8 0.4 %collective-permute-done.6.inner = bf16[32,1024]{1,0:T(8,128)(2,1)S(1)} collective-permute-done((bf16[32,1024]{1,0:T(8,128)(2,1)S(1)}, bf16[32,1024]{1,0:T(8,128)(2,1)S(1)}, u32[]{:S(2)}, u32[]{:S(2)}) %collective-permute-start.6) | collective-permute-done | bytes 65568 | tf_op jit(solution)/shard_map/ppermute | solution.py:234
  26.3 2.5 %middle_0.1 = (bf16[128,1024]{1,0:T(8,128)(2,1)S(1)}, bf16[128,1024]{1,0:T(8,128)(2,1)S(1)}, bf16[32,1024]{1,0:T(8,128)(2,1)S(1)}, bf16[32,1024]{1,0:T(8,128)(2,1)S(1)}) custom-call(bf16[128,1024]{1,0:T(8,128)(2,1)S(1)} %collective-permute-done.far.state, bf16[128,1024]{1,0:T(8,128)(2,1)S(1)} %project.4.q, bf16[128,1024]{1,0:T(8,128)(2,1)S(1)} %get-tuple-element.42.normed, ...), custom_call_target="tpu_custom_call" | custom-call | flops 1000000000 | bytes 1000 | tf_op jit(solution)/shard_map/middle_0/pallas_call | solution.py:28
  28.7 1.7 %collective-permute-start.7 = (bf16[32,1024]{1,0:T(8,128)(2,1)S(1)}, bf16[32,1024]{1,0:T(8,128)(2,1)S(1)}, u32[]{:S(2)}, u32[]{:S(2)}) collective-permute-start(bf16[32,1024]{1,0:T(8,128)(2,1)S(1)} %get-tuple-element.47), channel_id=1, source_target_pairs={{0,128},{1,2},{2,1},{3,4},{4,3},{5,6},{6,5},{7,8},{8,7},{9,10},{10... | collective-permute-start | bytes 196616 | tf_op jit(solution)/shard_map/ppermute | solution.py:231
  30.4 0.2 collective-permute-start.8
  30.7 0.5 %project.5.q = bf16[128,1024]{1,0:T(8,128)(2,1)S(1)} custom-call(bf16[128,1024]{1,0:T(8,128)(2,1)S(1)} %get-tuple-element.46.normed, bf16[1024,1024]{1,0:T(8,128)(2,1)S(1)} %copy-done.3), custom_call_target="tpu_custom_call" | custom-call | flops 1000000000 | bytes 1000 | tf_op jit(solution)/shard_map/project/pallas_call | solution.py:28
  31.1 8.0 %collective-permute-done.7.cross = bf16[32,1024]{1,0:T(8,128)(2,1)S(1)} collective-permute-done((bf16[32,1024]{1,0:T(8,128)(2,1)S(1)}, bf16[32,1024]{1,0:T(8,128)(2,1)S(1)}, u32[]{:S(2)}, u32[]{:S(2)}) %collective-permute-start.7) | collective-permute-done | bytes 65568 | tf_op jit(solution)/shard_map/ppermute | solution.py:231
  39.1 0.0 collective-permute-done.8.inner
  39.1 2.1 %last_0.1.here = bf16[128,1024]{1,0:T(8,128)(2,1)S(1)} custom-call(bf16[128,1024]{1,0:T(8,128)(2,1)S(1)} %get-tuple-element.45.state, bf16[128,1024]{1,0:T(8,128)(2,1)S(1)} %project.5.q, bf16[128,1024]{1,0:T(8,128)(2,1)S(1)} %get-tuple-element.46.normed, bf16[32,1024]{1,0:T(8,128)(2,1)S(1)} %collective-permute-done.7.cross, ...), custom_call_target="tpu_custom_call" | custom-call | flops 1000000000 | bytes 1000 | tf_op jit(solution)/shard_map/last_0/pallas_call | solution.py:28
  41.2 0.0 collective-permute-done.9.there
  41.2 0.8 %finish.1 = bf16[1,2,128,1024]{3,2,1,0:T(8,128)(2,1)} custom-call(bf16[128,1024]{1,0:T(8,128)(2,1)S(1)} %last_0.1.here, bf16[128,1024]{1,0:T(8,128)(2,1)S(1)} %collective-permute-done.9.there), custom_call_target="tpu_custom_call" | custom-call | flops 1000000000 | bytes 1000 | tf_op jit(solution)/shard_map/finish/pallas_call | solution.py:28
  (9 shorter events, 0.0 us)
Async XLA Ops:
  0.0 7.7 %copy-start.3 = (bf16[1024,1024]{1,0:T(8,128)(2,1)S(1)}, bf16[1024,1024]{1,0:T(8,128)(2,1)}, u32[]{:S(2)}) copy-start(bf16[1024,1024]{1,0:T(8,128)(2,1)} %wq.7) | copy-start | bytes 6291460
  0.0 7.7 %copy-start.4 = (s32[128,8]{0,1:T(8,128)S(1)}, s32[128,8]{0,1:T(8,128)}, u32[]{:S(2)}) copy-start(s32[128,8]{0,1:T(8,128)} %param.16) | copy-start | bytes 12292
  0.0 9.4 %copy-start.1 = (bf16[1024,1024]{1,0:T(8,128)(2,1)S(1)}, bf16[1024,1024]{1,0:T(8,128)(2,1)}, u32[]{:S(2)}) copy-start(bf16[1024,1024]{1,0:T(8,128)(2,1)} %wv.7) | copy-start | bytes 6291460
  0.0 9.4 %copy-start.2 = (bf16[1024,1024]{1,0:T(8,128)(2,1)S(1)}, bf16[1024,1024]{1,0:T(8,128)(2,1)}, u32[]{:S(2)}) copy-start(bf16[1024,1024]{1,0:T(8,128)(2,1)} %wo.7) | copy-start | bytes 6291460
  2.0 7.4 %copy-start = (bf16[1024,1024]{1,0:T(8,128)(2,1)S(1)}, bf16[1024,1024]{1,0:T(8,128)(2,1)}, u32[]{:S(2)}) copy-start(bf16[1024,1024]{1,0:T(8,128)(2,1)} %wk.7) | copy-start | bytes 6291460
  2.0 7.4 %collective-permute-start.1 = (bf16[64,1024]{1,0:T(8,128)(2,1)S(1)}, bf16[64,1024]{1,0:T(8,128)(2,1)S(1)}, u32[]{:S(2)}, u32[]{:S(2)}) collective-permute-start(bf16[64,1024]{1,0:T(8,128)(2,1)S(1)} %get-tuple-element.33), channel_id=1, source_target_pairs={{0,128},{1,2},{2,1},{3,4},{4,3},{5,6},{6,5},{7,8},{8,7},{9,10},{10... | collective-permute-start | bytes 393224 | tf_op jit(solution)/shard_map/ppermute | solution.py:231
  4.7 3.5 %collective-permute-start.2 = (bf16[32,1024]{1,0:T(8,128)(2,1)S(1)}, bf16[32,1024]{1,0:T(8,128)(2,1)S(1)}, u32[]{:S(2)}, u32[]{:S(2)}) collective-permute-start(bf16[32,1024]{1,0:T(8,128)(2,1)S(1)} %get-tuple-element.34), channel_id=1, source_target_pairs={{0,1},{1,0},{2,3},{3,2},{4,5},{5,4},{6,7},{7,6},{8,9},{9,8},{10,11... | collective-permute-start | bytes 196616 | tf_op jit(solution)/shard_map/ppermute | solution.py:234
  4.7 19.0 %collective-permute-start = (bf16[128,1024]{1,0:T(8,128)(2,1)S(1)}, bf16[128,1024]{1,0:T(8,128)(2,1)S(1)}, u32[]{:S(2)}, u32[]{:S(2)}) collective-permute-start(bf16[128,1024]{1,0:T(8,128)(2,1)S(1)} %get-tuple-element.27), channel_id=1, source_target_pairs={{0,32},{16,48},{32,64},{48,80},{64,96},{80,112},{96,128},{112,144}... | collective-permute-start | bytes 786440 | tf_op jit(solution)/shard_map/ppermute | solution.py:271
  11.9 7.2 %collective-permute-start.3 = (bf16[32,1024]{1,0:T(8,128)(2,1)S(1)}, bf16[32,1024]{1,0:T(8,128)(2,1)S(1)}, u32[]{:S(2)}, u32[]{:S(2)}) collective-permute-start(bf16[32,1024]{1,0:T(8,128)(2,1)S(1)} %get-tuple-element.40), channel_id=1, source_target_pairs={{0,128},{1,2},{2,1},{3,4},{4,3},{5,6},{6,5},{7,8},{8,7},{9,10},{10... | collective-permute-start | bytes 196616 | tf_op jit(solution)/shard_map/ppermute | solution.py:231
  14.6 4.6 %collective-permute-start.4 = (bf16[32,1024]{1,0:T(8,128)(2,1)S(1)}, bf16[32,1024]{1,0:T(8,128)(2,1)S(1)}, u32[]{:S(2)}, u32[]{:S(2)}) collective-permute-start(bf16[32,1024]{1,0:T(8,128)(2,1)S(1)} %get-tuple-element.41), channel_id=1, source_target_pairs={{0,1},{1,0},{2,3},{3,2},{4,5},{5,4},{6,7},{7,6},{8,9},{9,8},{10,11... | collective-permute-start | bytes 196616 | tf_op jit(solution)/shard_map/ppermute | solution.py:234
  15.1 10.7 %collective-permute-start.5 = (bf16[32,1024]{1,0:T(8,128)(2,1)S(1)}, bf16[32,1024]{1,0:T(8,128)(2,1)S(1)}, u32[]{:S(2)}, u32[]{:S(2)}) collective-permute-start(bf16[32,1024]{1,0:T(8,128)(2,1)S(1)} %get-tuple-element.43), channel_id=1, source_target_pairs={{0,32},{16,48},{32,64},{48,80},{64,96},{80,112},{96,128},{112,144}... | collective-permute-start | bytes 196616 | tf_op jit(solution)/shard_map/ppermute | solution.py:276
  21.3 19.9 %collective-permute-start.9 = (bf16[128,1024]{1,0:T(8,128)(2,1)S(1)}, bf16[128,1024]{1,0:T(8,128)(2,1)S(1)}, u32[]{:S(2)}, u32[]{:S(2)}) collective-permute-start(bf16[128,1024]{1,0:T(8,128)(2,1)S(1)} %last_1.1.token), channel_id=1, source_target_pairs={{0,32},{16,48},{32,64},{48,80},{64,96},{80,112},{96,128},{112,144}... | collective-permute-start | bytes 786440 | tf_op jit(solution)/shard_map/ppermute | solution.py:278
  24.1 2.2 %collective-permute-start.6 = (bf16[32,1024]{1,0:T(8,128)(2,1)S(1)}, bf16[32,1024]{1,0:T(8,128)(2,1)S(1)}, u32[]{:S(2)}, u32[]{:S(2)}) collective-permute-start(bf16[32,1024]{1,0:T(8,128)(2,1)S(1)} %get-tuple-element.44), channel_id=1, source_target_pairs={{0,1},{1,0},{2,3},{3,2},{4,5},{5,4},{6,7},{7,6},{8,9},{9,8},{10,11... | collective-permute-start | bytes 196616 | tf_op jit(solution)/shard_map/ppermute | solution.py:234
  28.7 10.4 %collective-permute-start.7 = (bf16[32,1024]{1,0:T(8,128)(2,1)S(1)}, bf16[32,1024]{1,0:T(8,128)(2,1)S(1)}, u32[]{:S(2)}, u32[]{:S(2)}) collective-permute-start(bf16[32,1024]{1,0:T(8,128)(2,1)S(1)} %get-tuple-element.47), channel_id=1, source_target_pairs={{0,128},{1,2},{2,1},{3,4},{4,3},{5,6},{6,5},{7,8},{8,7},{9,10},{10... | collective-permute-start | bytes 196616 | tf_op jit(solution)/shard_map/ppermute | solution.py:231
  30.4 8.7 %collective-permute-start.8 = (bf16[32,1024]{1,0:T(8,128)(2,1)S(1)}, bf16[32,1024]{1,0:T(8,128)(2,1)S(1)}, u32[]{:S(2)}, u32[]{:S(2)}) collective-permute-start(bf16[32,1024]{1,0:T(8,128)(2,1)S(1)} %get-tuple-element.48), channel_id=1, source_target_pairs={{0,1},{1,0},{2,3},{3,2},{4,5},{5,4},{6,7},{7,6},{8,9},{9,8},{10,11... | collective-permute-start | bytes 196616 | tf_op jit(solution)/shard_map/ppermute | solution.py:234

commit v10 on v9

--- a/solution.py
+++ b/solution.py
@@ -202,12 +202,23 @@
         out[...] = attend(state, q, normed, cross[...], inner[...], table, wk, wv, wo, attended)
 
 
-def finish_body(here, there, out, sems):
-    copies = [pltpu.make_async_copy(x, out.at[0, i], sems.at[i]) for i, x in enumerate((here, there))]
-    for copy in copies:
-        copy.start()
-    for copy in copies:
-        copy.wait()
+def finish_body(index, state, q, normed, cross, inner, table, wk, wv, wo, arrived, out, attended, result, sems):
+    there = pltpu.make_async_copy(arrived, out.at[0, 1], sems.at[0])
+    there.start()
+    special = lax.axis_index("lead") == index
+
+    @pl.when(special)
+    def _():
+        result[...] = state[...]
+
+    @pl.when(jnp.logical_not(special))
+    def _():
+        result[...] = attend(state, q, normed, cross[...], inner[...], table, wk, wv, wo, attended)
+
+    here = pltpu.make_async_copy(result, out.at[0, 0], sems.at[1])
+    here.start()
+    there.wait()
+    here.wait()
 
 
 def per_device(states, entering, norm_gain, wq, wk, wv, wo, senders, halo_rows):
@@ -285,10 +296,11 @@
     cross0 = crossed(cross0)
     inner0 = swapped(inner0)
     q0 = project(normed0)
-    here = last("last_0", 0, state0, q0, normed0, cross0, inner0)
     return call(
-        finish_body, "finish", [here, arrived], [VMEM] * 2,
-        shape(1, members, nodes, width), HBM, [dma((2,))],
+        functools.partial(finish_body, 0), "finish",
+        [state0, q0, normed0, cross0, inner0, table, vk, vv, vo, arrived], [VMEM] * 10,
+        shape(1, members, nodes, width), HBM,
+        [pltpu.VMEM((nodes, width), BF)] * 2 + [dma((2,))],
     )
 
 

time: 42.3 us -> 42.3 us (level)
    pallas_call x11 -> x10, Pallas kernels: 14.2 us -> 14.1 us  [call(): pl.pallas_call(body, out_shape=outs, in_specs=specs, out_specs=out_specs,...]
  transfers between devices with their start and end apart: 10 -> 10, of which waited for: 4 -> 4; matrix products, arithmetic and copies ran while one was open for 0% -> 0% of each run, Pallas kernels for 27% -> 22%
where the time goes in v10:
time: 42.3 us; the launch traced here: 42.1 us
  starting transfers between devices  17 us (40%)
  Pallas kernels  14.1 us (33%)
  waiting for transfers between devices  10.7 us (25%)
    pallas_call x10, Pallas kernels, call(): pl.pallas_call(body, out_shape=outs, in_specs=specs, out_specs=out_specs,...  14.1 us
    ppermute x3, waiting for transfers between devices, crossed(): return lax.ppermute(cross, ('lead', 'mesh'), cross_route)  10.2 us
    ppermute x3, starting transfers between devices, crossed(): return lax.ppermute(cross, ('lead', 'mesh'), cross_route)  7.03 us
    ppermute x1, starting transfers between devices, per_device(): halo0 = lax.ppermute(halo0, 'lead', route)  3.07 us
    ppermute x1, starting transfers between devices, per_device(): far = lax.ppermute(far, 'lead', route)  2.99 us
    ppermute x1, starting transfers between devices, per_device(): arrived = lax.ppermute(near, 'lead', route)  2.4 us
    ppermute x4, starting transfers between devices, swapped(): return lax.ppermute(inner, 'mesh', inner_route)  1.51 us
  transfers between devices with their start and end apart: 10, of which 4 were waited for; matrix products, arithmetic and copies ran while one was open for 0% of the time, Pallas kernels for 22%

profile of v10, /device:TPU:45, one launch (start us, length us, event | category | flops | bytes accessed | tf_op | source)
XLA Modules:
  0.0 42.1 jit_solution(7801984958685281739)
XLA Ops:
  0.0 0.0 copy-start.2
  0.0 2.0 %start.1 = (bf16[128,1024]{1,0:T(8,128)(2,1)S(1)}, bf16[128,1024]{1,0:T(8,128)(2,1)S(1)}, f32[1,1024]{1,0:T(1,128)S(1)}, s32[2,32]{1,0:T(2,128)S(1)}, bf16[128,1...) custom-call(bf16[1,2,128,1024]{3,2,1,0:T(8,128)(2,1)} %states.1, ...), custom_call_target="tpu_custom_call" | custom-call | flops 3000000000 | bytes 1000 | tf_op jit(solution)/shard_map/start/pallas_call | solution.py:28
  2.0 0.0 copy-start
  2.0 2.7 %collective-permute-start.1 = (bf16[64,1024]{1,0:T(8,128)(2,1)S(1)}, bf16[64,1024]{1,0:T(8,128)(2,1)S(1)}, u32[]{:S(2)}, u32[]{:S(2)}) collective-permute-start(bf16[64,1024]{1,0:T(8,128)(2,1)S(1)} %get-tuple-element.33), channel_id=1, source_target_pairs={{0,128},{1,2},{2,1},{3,4},{4,3},{5,6},{6,5},{7,8},{8,7},{9,10},{10... | collective-permute-start | bytes 393224 | tf_op jit(solution)/shard_map/ppermute | solution.py:242
  4.7 0.0 collective-permute-start.2
  4.7 3.0 %collective-permute-start = (bf16[128,1024]{1,0:T(8,128)(2,1)S(1)}, bf16[128,1024]{1,0:T(8,128)(2,1)S(1)}, u32[]{:S(2)}, u32[]{:S(2)}) collective-permute-start(bf16[128,1024]{1,0:T(8,128)(2,1)S(1)} %get-tuple-element.27), channel_id=1, source_target_pairs={{0,32},{16,48},{32,64},{48,80},{64,96},{80,112},{96,128},{112,144}... | collective-permute-start | bytes 786440 | tf_op jit(solution)/shard_map/ppermute | solution.py:282
  7.7 0.5 %project_first.1 = (bf16[128,1024]{1,0:T(8,128)(2,1)S(1)}, f32[128,192]{1,0:T(8,128)S(1)}) custom-call(bf16[128,1024]{1,0:T(8,128)(2,1)S(1)} %get-tuple-element.31.normed, bf16[1024,1024]{1,0:T(8,128)(2,1)S(1)} %copy-done.3, s32[8,128]{1,0:T(8,128)S(1)} %bitcast.3), custom_call_target="tpu_custom_call" | custom-call | flops 1000000000 | bytes 1000 | tf_op jit(solution)/shard_map/project_first/pallas_call | solution.py:28
  8.2 0.0 collective-permute-done.2.inner
  8.2 1.2 %collective-permute-done.1.cross = bf16[64,1024]{1,0:T(8,128)(2,1)S(1)} collective-permute-done((bf16[64,1024]{1,0:T(8,128)(2,1)S(1)}, bf16[64,1024]{1,0:T(8,128)(2,1)S(1)}, u32[]{:S(2)}, u32[]{:S(2)}) %collective-permute-start.1) | collective-permute-done | bytes 131104 | tf_op jit(solution)/shard_map/ppermute | solution.py:242
  9.4 2.5 %middle_1.1 = (bf16[128,1024]{1,0:T(8,128)(2,1)S(1)}, bf16[128,1024]{1,0:T(8,128)(2,1)S(1)}, bf16[32,1024]{1,0:T(8,128)(2,1)S(1)}, bf16[32,1024]{1,0:T(8,128)(2,1)S(1)}, bf16[32,1024]{1,0:T(8,128)(2,1)S(1)}) custom-call(bf16[128,1024]{1,0:T(8,128)(2,1)S(1)} %get-tuple-element.30.state, bf16[128,1024]{1,0:T(8,128)(2,1)S(1)} %get-tuple-element.32.q, ...), custom_call_target="tpu_custom_call" | custom-call | flops 1000000000 | bytes 1000 | tf_op jit(solution)/shard_map/middle_1/pallas_call | solution.py:28
  11.9 2.7 %collective-permute-start.3 = (bf16[32,1024]{1,0:T(8,128)(2,1)S(1)}, bf16[32,1024]{1,0:T(8,128)(2,1)S(1)}, u32[]{:S(2)}, u32[]{:S(2)}) collective-permute-start(bf16[32,1024]{1,0:T(8,128)(2,1)S(1)} %get-tuple-element.40), channel_id=1, source_target_pairs={{0,128},{1,2},{2,1},{3,4},{4,3},{5,6},{6,5},{7,8},{8,7},{9,10},{10... | collective-permute-start | bytes 196616 | tf_op jit(solution)/shard_map/ppermute | solution.py:242
  14.6 0.0 collective-permute-start.4
  14.6 0.5 %project.3 = (bf16[128,1024]{1,0:T(8,128)(2,1)S(1)}, bf16[32,1024]{1,0:T(8,128)(2,1)S(1)}) custom-call(bf16[128,1024]{1,0:T(8,128)(2,1)S(1)} %get-tuple-element.37.normed, bf16[1024,1024]{1,0:T(8,128)(2,1)S(1)} %copy-done.3, bf16[32,1024]{1,0:T(8,128)(2,1)S(1)} %get-tuple-element.38.inner), custom_call_target="tpu_custom_call" | custom-call | flops 1000000000 | bytes 1000 | tf_op jit(solution)/shard_map/project/pallas_call | solution.py:28
  15.1 3.1 %collective-permute-start.5 = (bf16[32,1024]{1,0:T(8,128)(2,1)S(1)}, bf16[32,1024]{1,0:T(8,128)(2,1)S(1)}, u32[]{:S(2)}, u32[]{:S(2)}) collective-permute-start(bf16[32,1024]{1,0:T(8,128)(2,1)S(1)} %get-tuple-element.43), channel_id=1, source_target_pairs={{0,32},{16,48},{32,64},{48,80},{64,96},{80,112},{96,128},{112,144}... | collective-permute-start | bytes 196616 | tf_op jit(solution)/shard_map/ppermute | solution.py:287
  18.1 1.0 %collective-permute-done.3.cross = bf16[32,1024]{1,0:T(8,128)(2,1)S(1)} collective-permute-done((bf16[32,1024]{1,0:T(8,128)(2,1)S(1)}, bf16[32,1024]{1,0:T(8,128)(2,1)S(1)}, u32[]{:S(2)}, u32[]{:S(2)}) %collective-permute-start.3) | collective-permute-done | bytes 65568 | tf_op jit(solution)/shard_map/ppermute | solution.py:242
  19.2 0.0 collective-permute-done.4.inner
  19.2 2.1 %last_1.1.token = bf16[128,1024]{1,0:T(8,128)(2,1)S(1)} custom-call(bf16[128,1024]{1,0:T(8,128)(2,1)S(1)} %get-tuple-element.36.state, bf16[128,1024]{1,0:T(8,128)(2,1)S(1)} %get-tuple-element.39.q, bf16[128,1024]{1,0:T(8,128)(2,1)S(1)} %get-tuple-element.37.normed, bf16[32,1024]{1,0:T(8,128)(2,1)S(1)} %collective-permute-done.3.cross, ...), custom_call_target="tpu_custom_call" | custom-call | flops 1000000000 | bytes 1000 | tf_op jit(solution)/shard_map/last_1/pallas_call | solution.py:28
  21.3 2.4 %collective-permute-start.9 = (bf16[128,1024]{1,0:T(8,128)(2,1)S(1)}, bf16[128,1024]{1,0:T(8,128)(2,1)S(1)}, u32[]{:S(2)}, u32[]{:S(2)}) collective-permute-start(bf16[128,1024]{1,0:T(8,128)(2,1)S(1)} %last_1.1.token), channel_id=1, source_target_pairs={{0,32},{16,48},{32,64},{48,80},{64,96},{80,112},{96,128},{112,144}... | collective-permute-start | bytes 786440 | tf_op jit(solution)/shard_map/ppermute | solution.py:289
  23.7 0.0 collective-permute-done.far.state
  23.7 0.4 far_first.1
  24.1 1.3 %collective-permute-start.6 = (bf16[32,1024]{1,0:T(8,128)(2,1)S(1)}, bf16[32,1024]{1,0:T(8,128)(2,1)S(1)}, u32[]{:S(2)}, u32[]{:S(2)}) collective-permute-start(bf16[32,1024]{1,0:T(8,128)(2,1)S(1)} %get-tuple-element.44), channel_id=1, source_target_pairs={{0,1},{1,0},{2,3},{3,2},{4,5},{5,4},{6,7},{7,6},{8,9},{9,8},{10,11... | collective-permute-start | bytes 196616 | tf_op jit(solution)/shard_map/ppermute | solution.py:245
  25.3 0.5 %project.4.q = bf16[128,1024]{1,0:T(8,128)(2,1)S(1)} custom-call(bf16[128,1024]{1,0:T(8,128)(2,1)S(1)} %get-tuple-element.42.normed, bf16[1024,1024]{1,0:T(8,128)(2,1)S(1)} %copy-done.3), custom_call_target="tpu_custom_call" | custom-call | flops 1000000000 | bytes 1000 | tf_op jit(solution)/shard_map/project/pallas_call | solution.py:28
  25.8 0.0 collective-permute-done.5.cross
  25.8 0.4 %collective-permute-done.6.inner = bf16[32,1024]{1,0:T(8,128)(2,1)S(1)} collective-permute-done((bf16[32,1024]{1,0:T(8,128)(2,1)S(1)}, bf16[32,1024]{1,0:T(8,128)(2,1)S(1)}, u32[]{:S(2)}, u32[]{:S(2)}) %collective-permute-start.6) | collective-permute-done | bytes 65568 | tf_op jit(solution)/shard_map/ppermute | solution.py:245
  26.3 2.5 %middle_0.1 = (bf16[128,1024]{1,0:T(8,128)(2,1)S(1)}, bf16[128,1024]{1,0:T(8,128)(2,1)S(1)}, bf16[32,1024]{1,0:T(8,128)(2,1)S(1)}, bf16[32,1024]{1,0:T(8,128)(2,1)S(1)}) custom-call(bf16[128,1024]{1,0:T(8,128)(2,1)S(1)} %collective-permute-done.far.state, bf16[128,1024]{1,0:T(8,128)(2,1)S(1)} %project.4.q, bf16[128,1024]{1,0:T(8,128)(2,1)S(1)} %get-tuple-element.42.normed, ...), custom_call_target="tpu_custom_call" | custom-call | flops 1000000000 | bytes 1000 | tf_op jit(solution)/shard_map/middle_0/pallas_call | solution.py:28
  28.7 1.7 %collective-permute-start.7 = (bf16[32,1024]{1,0:T(8,128)(2,1)S(1)}, bf16[32,1024]{1,0:T(8,128)(2,1)S(1)}, u32[]{:S(2)}, u32[]{:S(2)}) collective-permute-start(bf16[32,1024]{1,0:T(8,128)(2,1)S(1)} %get-tuple-element.47), channel_id=1, source_target_pairs={{0,128},{1,2},{2,1},{3,4},{4,3},{5,6},{6,5},{7,8},{8,7},{9,10},{10... | collective-permute-start | bytes 196616 | tf_op jit(solution)/shard_map/ppermute | solution.py:242
  30.4 0.2 collective-permute-start.8
  30.7 0.5 %project.5.q = bf16[128,1024]{1,0:T(8,128)(2,1)S(1)} custom-call(bf16[128,1024]{1,0:T(8,128)(2,1)S(1)} %get-tuple-element.46.normed, bf16[1024,1024]{1,0:T(8,128)(2,1)S(1)} %copy-done.3), custom_call_target="tpu_custom_call" | custom-call | flops 1000000000 | bytes 1000 | tf_op jit(solution)/shard_map/project/pallas_call | solution.py:28
  31.1 8.0 %collective-permute-done.7.cross = bf16[32,1024]{1,0:T(8,128)(2,1)S(1)} collective-permute-done((bf16[32,1024]{1,0:T(8,128)(2,1)S(1)}, bf16[32,1024]{1,0:T(8,128)(2,1)S(1)}, u32[]{:S(2)}, u32[]{:S(2)}) %collective-permute-start.7) | collective-permute-done | bytes 65568 | tf_op jit(solution)/shard_map/ppermute | solution.py:242
  39.1 0.0 collective-permute-done.8.inner
  39.1 0.0 collective-permute-done.9.arrived
  39.1 2.8 %finish.1 = bf16[1,2,128,1024]{3,2,1,0:T(8,128)(2,1)} custom-call(bf16[128,1024]{1,0:T(8,128)(2,1)S(1)} %get-tuple-element.45.state, bf16[128,1024]{1,0:T(8,128)(2,1)S(1)} %project.5.q, bf16[128,1024]{1,0:T(8,128)(2,1)S(1)} %get-tuple-element.46.normed, bf16[32,1024]{1,0:T(8,128)(2,1)S(1)} %collective-permute-done.7.cross, ...), custom_call_target="tpu_custom_call" | custom-call | flops 1000000000 | bytes 1000 | tf_op jit(solution)/shard_map/finish/pallas_call | solution.py:28
  (8 shorter events, 0.0 us)
Async XLA Ops:
  0.0 7.7 %copy-start.3 = (bf16[1024,1024]{1,0:T(8,128)(2,1)S(1)}, bf16[1024,1024]{1,0:T(8,128)(2,1)}, u32[]{:S(2)}) copy-start(bf16[1024,1024]{1,0:T(8,128)(2,1)} %wq.7) | copy-start | bytes 6291460
  0.0 7.7 %copy-start.4 = (s32[128,8]{0,1:T(8,128)S(1)}, s32[128,8]{0,1:T(8,128)}, u32[]{:S(2)}) copy-start(s32[128,8]{0,1:T(8,128)} %param.16) | copy-start | bytes 12292
  0.0 9.4 %copy-start.1 = (bf16[1024,1024]{1,0:T(8,128)(2,1)S(1)}, bf16[1024,1024]{1,0:T(8,128)(2,1)}, u32[]{:S(2)}) copy-start(bf16[1024,1024]{1,0:T(8,128)(2,1)} %wv.7) | copy-start | bytes 6291460
  0.0 9.4 %copy-start.2 = (bf16[1024,1024]{1,0:T(8,128)(2,1)S(1)}, bf16[1024,1024]{1,0:T(8,128)(2,1)}, u32[]{:S(2)}) copy-start(bf16[1024,1024]{1,0:T(8,128)(2,1)} %wo.7) | copy-start | bytes 6291460
  2.0 7.4 %copy-start = (bf16[1024,1024]{1,0:T(8,128)(2,1)S(1)}, bf16[1024,1024]{1,0:T(8,128)(2,1)}, u32[]{:S(2)}) copy-start(bf16[1024,1024]{1,0:T(8,128)(2,1)} %wk.7) | copy-start | bytes 6291460
  2.0 7.4 %collective-permute-start.1 = (bf16[64,1024]{1,0:T(8,128)(2,1)S(1)}, bf16[64,1024]{1,0:T(8,128)(2,1)S(1)}, u32[]{:S(2)}, u32[]{:S(2)}) collective-permute-start(bf16[64,1024]{1,0:T(8,128)(2,1)S(1)} %get-tuple-element.33), channel_id=1, source_target_pairs={{0,128},{1,2},{2,1},{3,4},{4,3},{5,6},{6,5},{7,8},{8,7},{9,10},{10... | collective-permute-start | bytes 393224 | tf_op jit(solution)/shard_map/ppermute | solution.py:242
  4.7 3.5 %collective-permute-start.2 = (bf16[32,1024]{1,0:T(8,128)(2,1)S(1)}, bf16[32,1024]{1,0:T(8,128)(2,1)S(1)}, u32[]{:S(2)}, u32[]{:S(2)}) collective-permute-start(bf16[32,1024]{1,0:T(8,128)(2,1)S(1)} %get-tuple-element.34), channel_id=1, source_target_pairs={{0,1},{1,0},{2,3},{3,2},{4,5},{5,4},{6,7},{7,6},{8,9},{9,8},{10,11... | collective-permute-start | bytes 196616 | tf_op jit(solution)/shard_map/ppermute | solution.py:245
  4.7 19.0 %collective-permute-start = (bf16[128,1024]{1,0:T(8,128)(2,1)S(1)}, bf16[128,1024]{1,0:T(8,128)(2,1)S(1)}, u32[]{:S(2)}, u32[]{:S(2)}) collective-permute-start(bf16[128,1024]{1,0:T(8,128)(2,1)S(1)} %get-tuple-element.27), channel_id=1, source_target_pairs={{0,32},{16,48},{32,64},{48,80},{64,96},{80,112},{96,128},{112,144}... | collective-permute-start | bytes 786440 | tf_op jit(solution)/shard_map/ppermute | solution.py:282
  11.9 7.2 %collective-permute-start.3 = (bf16[32,1024]{1,0:T(8,128)(2,1)S(1)}, bf16[32,1024]{1,0:T(8,128)(2,1)S(1)}, u32[]{:S(2)}, u32[]{:S(2)}) collective-permute-start(bf16[32,1024]{1,0:T(8,128)(2,1)S(1)} %get-tuple-element.40), channel_id=1, source_target_pairs={{0,128},{1,2},{2,1},{3,4},{4,3},{5,6},{6,5},{7,8},{8,7},{9,10},{10... | collective-permute-start | bytes 196616 | tf_op jit(solution)/shard_map/ppermute | solution.py:242
  14.6 4.6 %collective-permute-start.4 = (bf16[32,1024]{1,0:T(8,128)(2,1)S(1)}, bf16[32,1024]{1,0:T(8,128)(2,1)S(1)}, u32[]{:S(2)}, u32[]{:S(2)}) collective-permute-start(bf16[32,1024]{1,0:T(8,128)(2,1)S(1)} %get-tuple-element.41), channel_id=1, source_target_pairs={{0,1},{1,0},{2,3},{3,2},{4,5},{5,4},{6,7},{7,6},{8,9},{9,8},{10,11... | collective-permute-start | bytes 196616 | tf_op jit(solution)/shard_map/ppermute | solution.py:245
  15.1 10.7 %collective-permute-start.5 = (bf16[32,1024]{1,0:T(8,128)(2,1)S(1)}, bf16[32,1024]{1,0:T(8,128)(2,1)S(1)}, u32[]{:S(2)}, u32[]{:S(2)}) collective-permute-start(bf16[32,1024]{1,0:T(8,128)(2,1)S(1)} %get-tuple-element.43), channel_id=1, source_target_pairs={{0,32},{16,48},{32,64},{48,80},{64,96},{80,112},{96,128},{112,144}... | collective-permute-start | bytes 196616 | tf_op jit(solution)/shard_map/ppermute | solution.py:287
  21.3 17.8 %collective-permute-start.9 = (bf16[128,1024]{1,0:T(8,128)(2,1)S(1)}, bf16[128,1024]{1,0:T(8,128)(2,1)S(1)}, u32[]{:S(2)}, u32[]{:S(2)}) collective-permute-start(bf16[128,1024]{1,0:T(8,128)(2,1)S(1)} %last_1.1.token), channel_id=1, source_target_pairs={{0,32},{16,48},{32,64},{48,80},{64,96},{80,112},{96,128},{112,144}... | collective-permute-start | bytes 786440 | tf_op jit(solution)/shard_map/ppermute | solution.py:289
  24.1 2.2 %collective-permute-start.6 = (bf16[32,1024]{1,0:T(8,128)(2,1)S(1)}, bf16[32,1024]{1,0:T(8,128)(2,1)S(1)}, u32[]{:S(2)}, u32[]{:S(2)}) collective-permute-start(bf16[32,1024]{1,0:T(8,128)(2,1)S(1)} %get-tuple-element.44), channel_id=1, source_target_pairs={{0,1},{1,0},{2,3},{3,2},{4,5},{5,4},{6,7},{7,6},{8,9},{9,8},{10,11... | collective-permute-start | bytes 196616 | tf_op jit(solution)/shard_map/ppermute | solution.py:245
  28.7 10.3 %collective-permute-start.7 = (bf16[32,1024]{1,0:T(8,128)(2,1)S(1)}, bf16[32,1024]{1,0:T(8,128)(2,1)S(1)}, u32[]{:S(2)}, u32[]{:S(2)}) collective-permute-start(bf16[32,1024]{1,0:T(8,128)(2,1)S(1)} %get-tuple-element.47), channel_id=1, source_target_pairs={{0,128},{1,2},{2,1},{3,4},{4,3},{5,6},{6,5},{7,8},{8,7},{9,10},{10... | collective-permute-start | bytes 196616 | tf_op jit(solution)/shard_map/ppermute | solution.py:242
  30.4 8.6 %collective-permute-start.8 = (bf16[32,1024]{1,0:T(8,128)(2,1)S(1)}, bf16[32,1024]{1,0:T(8,128)(2,1)S(1)}, u32[]{:S(2)}, u32[]{:S(2)}) collective-permute-start(bf16[32,1024]{1,0:T(8,128)(2,1)S(1)} %get-tuple-element.48), channel_id=1, source_target_pairs={{0,1},{1,0},{2,3},{3,2},{4,5},{5,4},{6,7},{7,6},{8,9},{9,8},{10,11... | collective-permute-start | bytes 196616 | tf_op jit(solution)/shard_map/ppermute | solution.py:245
